TPU v7x, 32 devices: a whole 2x2x4 slice. The times are simulated.
32 devices in a mesh: rep: 8 (over z, x), fsdp: 4 (over y, core).
Axes of the slice: x: 2, y: 2, z: 4, core: 2. Of those that a mesh axis runs over, the one named last changes fastest.
Arguments:
- block_input: bfloat16 [4096, 2048], P(('rep', 'fsdp')), may hold values from -6 to 6
- positions: int32 [4096], P(('rep', 'fsdp')), may hold values from 0 to 511, as said below
- cotangent: bfloat16 [4096, 2048], P(('rep', 'fsdp')), may hold values from -6 to 6
- norm_attn: bfloat16 [2048], P(('rep', 'fsdp')), may hold values from 0.5 to 1.5
- w_qkv: bfloat16 [2048, 4096], P(('rep', 'fsdp')), may hold values from -0.125 to 0.125
- w_out: bfloat16 [2048, 2048], P(('rep', 'fsdp')), may hold values from -2 to 2
- norm_ffn: bfloat16 [2048], P(('rep', 'fsdp')), may hold values from 0.5 to 1.5
- w_gate: bfloat16 [2048, 8192], P(('rep', 'fsdp')), may hold values from -0.125 to 0.125
- w_up: bfloat16 [2048, 8192], P(('rep', 'fsdp')), may hold values from -0.125 to 0.125
- w_down: bfloat16 [2048, 8192], P(('rep', 'fsdp')), may hold values from -0.0625 to 0.0625
Outputs:
- layer_output: bfloat16 [4096, 2048], P(('rep', 'fsdp'))
- input_gradient: float32 [4096, 2048], P(('rep', 'fsdp'))
- grad_norm_attn: float32 [2048], P(('rep', 'fsdp'))
- grad_qkv: float32 [2048, 4096], P(('rep', 'fsdp'))
- grad_out: float32 [2048, 2048], P(('rep', 'fsdp'))
- grad_norm_ffn: float32 [2048], P(('rep', 'fsdp'))
- grad_gate: float32 [2048, 8192], P(('rep', 'fsdp'))
- grad_up: float32 [2048, 8192], P(('rep', 'fsdp'))
- grad_down: float32 [2048, 8192], P(('rep', 'fsdp'))
Inputs may be any that keep to these rules, and one draw needn't show every extreme that they name: Each aligned group of 512 tokens holds up to three documents; positions start at 0 at each document's first token and rise by one; the group's first token starts a document; the middle document starts within the group's first 64 tokens and ends within its last 64.
All inputs are finite; a program needn't handle non-finite values.
Results may differ from a plain program's by a relative error of at most 0.02.
Values may be sent and summed in bfloat16 or wider, within the bound.
A program may use at most 576 MiB of HBM per device.

v0:
```python
import jax
import jax.numpy as jnp
from jax import lax
from jax.sharding import PartitionSpec as P

HEADS = 16
KV_HEADS = 8
HEAD_DIM = 128
BLOCK = 256


EPS = 1e-05
THETA = 1000000.0


def rope_tables(places, head_width):
    frequency = THETA ** (-(jnp.arange(0, head_width, 2, dtype=jnp.float32) / head_width))
    angles = places.astype(jnp.float32)[:, None] * frequency[None, :]
    angles = jnp.concatenate([angles, angles], axis=-1)
    return (jnp.cos(angles)[:, None, :], jnp.sin(angles)[:, None, :])


def rotate(vectors, cosine, sine_table):
    half_dim = vectors.shape[-1] // 2
    turned = jnp.concatenate([-vectors[..., half_dim:], vectors[..., :half_dim]], axis=-1)
    return vectors * cosine + turned * sine_table


def rotate_back(upstream, cosine, sine_table):
    half_dim = upstream.shape[-1] // 2
    scaled_rows = upstream * sine_table
    turned = jnp.concatenate([scaled_rows[..., half_dim:], -scaled_rows[..., :half_dim]], axis=-1)
    return upstream * cosine + turned


def times_transpose(left_side, right_side):
    return lax.dot_general(
        left_side, right_side, (((1,), (1,)), ((), ())), preferred_element_type=jnp.float32
    )


def norm_backward_step(normalized_gradient, unit_rows, inverse_rootmean, gain_vector_value):
    scaled_rows = normalized_gradient * gain_vector_value
    return inverse_rootmean * (
        scaled_rows - unit_rows * jnp.mean(scaled_rows * unit_rows, axis=-1, keepdims=True)
    )


def owner_sum(left_side, right_side):
    section = lax.psum_scatter(
        lax.dot_general(
            left_side, right_side, (((0,), (0,)), ((), ())), preferred_element_type=jnp.float32
        ).astype(jnp.bfloat16),
        "rep",
        scatter_dimension=0,
        tiled=True,
    )
    return lax.psum_scatter(section, "fsdp", scatter_dimension=0, tiled=True).astype(jnp.float32)


def shards(
    block_input, positions, cotangent, norm_attn, w_qkv, w_out, norm_ffn, w_gate, w_up, w_down
):
    token_count, model_width = block_input.shape
    group_size = HEADS // KV_HEADS
    q_cols = HEADS * HEAD_DIM
    kv_cols = KV_HEADS * HEAD_DIM
    score_scale = HEAD_DIM ** (-0.5)
    gain_a, attn_qkv, attn_proj = (
        lax.all_gather(norm_attn, ("rep", "fsdp"), axis=0, tiled=True),
        lax.all_gather(w_qkv, ("rep", "fsdp"), axis=0, tiled=True),
        lax.all_gather(w_out, ("rep", "fsdp"), axis=0, tiled=True),
    )
    gain_f, ffn_gate, ffn_up, ffn_down = (
        lax.all_gather(norm_ffn, ("rep", "fsdp"), axis=0, tiled=True),
        lax.all_gather(w_gate, ("rep", "fsdp"), axis=0, tiled=True),
        lax.all_gather(w_up, ("rep", "fsdp"), axis=0, tiled=True),
        lax.all_gather(w_down, ("rep", "fsdp"), axis=0, tiled=True),
    )
    attention_gain_value = gain_a.astype(jnp.float32)
    feedforward_gain_value = gain_f.astype(jnp.float32)
    residual_flow = block_input.astype(jnp.float32)
    attention_inverse_norm = lax.rsqrt(
        jnp.mean(residual_flow * residual_flow, axis=-1, keepdims=True) + EPS
    )
    attention_unit_rows = residual_flow * attention_inverse_norm
    attention_normalized = (attention_unit_rows * attention_gain_value).astype(jnp.bfloat16)
    qkv = jnp.dot(attention_normalized, attn_qkv, preferred_element_type=jnp.float32)
    cosine, sine_table = rope_tables(positions, HEAD_DIM)
    queries = rotate(
        qkv[:, :q_cols].reshape(token_count, HEADS, HEAD_DIM), cosine, sine_table
    ).astype(jnp.bfloat16)
    key_heads = rotate(
        qkv[:, q_cols : q_cols + kv_cols].reshape(token_count, KV_HEADS, HEAD_DIM),
        cosine,
        sine_table,
    ).astype(jnp.bfloat16)
    value_heads = (
        qkv[:, q_cols + kv_cols :].reshape(token_count, KV_HEADS, HEAD_DIM).astype(jnp.bfloat16)
    )
    key_all, value_all = (
        lax.all_gather(key_heads, "fsdp", axis=0, tiled=True),
        lax.all_gather(value_heads, "fsdp", axis=0, tiled=True),
    )
    key_places = lax.all_gather(positions, "fsdp", axis=0, tiled=True)
    key_count = key_places.shape[0]
    query_index = lax.axis_index("fsdp") * token_count + jnp.arange(token_count, dtype=jnp.int32)
    key_index = jnp.arange(key_count, dtype=jnp.int32)
    same_doc = (query_index - positions)[:, None] == (key_index - key_places)[None, :]
    earlier_block = (key_places // BLOCK)[None, :] <= (positions // BLOCK)[:, None]
    allowed = same_doc & earlier_block
    grouped_q = queries.reshape(token_count, KV_HEADS, group_size, HEAD_DIM)

    def score_all():
        raw = (
            jnp.einsum("tkgd,skd->kgts", grouped_q, key_all, preferred_element_type=jnp.float32)
            * score_scale
        )
        return jnp.where(allowed, raw, -1e30)

    scores = score_all()
    row_max = jnp.max(scores, axis=-1, keepdims=True)
    exponent = jnp.exp(scores - row_max)
    row_total = jnp.sum(exponent, axis=-1, keepdims=True)
    log_total = row_max + jnp.log(row_total)
    weights_low = (exponent / row_total).astype(jnp.bfloat16)
    mixed_heads = jnp.einsum(
        "kgts,skd->tkgd", weights_low, value_all, preferred_element_type=jnp.float32
    )
    attended = mixed_heads.reshape(token_count, q_cols).astype(jnp.bfloat16)
    middle_residual = residual_flow + jnp.dot(
        attended, attn_proj, preferred_element_type=jnp.float32
    )
    feedforward_inverse_norm = lax.rsqrt(
        jnp.mean(middle_residual * middle_residual, axis=-1, keepdims=True) + EPS
    )
    feedforward_unit_rows = middle_residual * feedforward_inverse_norm
    feedforward_normalized = (feedforward_unit_rows * feedforward_gain_value).astype(jnp.bfloat16)
    gate_pre = jnp.dot(feedforward_normalized, ffn_gate, preferred_element_type=jnp.float32)
    up_pre = jnp.dot(feedforward_normalized, ffn_up, preferred_element_type=jnp.float32)
    sigmoid_gate = jax.nn.sigmoid(gate_pre)
    activated = gate_pre * sigmoid_gate
    hidden = (activated * up_pre).astype(jnp.bfloat16)
    layer_output = (middle_residual + times_transpose(hidden, ffn_down)).astype(jnp.bfloat16)
    back_qkv, back_proj = (
        lax.all_gather(w_qkv, ("rep", "fsdp"), axis=0, tiled=True),
        lax.all_gather(w_out, ("rep", "fsdp"), axis=0, tiled=True),
    )
    back_gate, back_up, back_down = (
        lax.all_gather(w_gate, ("rep", "fsdp"), axis=0, tiled=True),
        lax.all_gather(w_up, ("rep", "fsdp"), axis=0, tiled=True),
        lax.all_gather(w_down, ("rep", "fsdp"), axis=0, tiled=True),
    )
    d_hidden = jnp.dot(cotangent, back_down, preferred_element_type=jnp.float32)
    d_gate = (d_hidden * up_pre * sigmoid_gate * (1.0 + gate_pre * (1.0 - sigmoid_gate))).astype(
        jnp.bfloat16
    )
    d_up = (d_hidden * activated).astype(jnp.bfloat16)
    feedforward_normalized_gradient = times_transpose(d_gate, back_gate) + times_transpose(
        d_up, back_up
    )
    feedforward_gain_piece = jnp.sum(
        feedforward_normalized_gradient * feedforward_unit_rows, axis=0
    )
    middle_gradient = cotangent.astype(jnp.float32) + norm_backward_step(
        feedforward_normalized_gradient,
        feedforward_unit_rows,
        feedforward_inverse_norm,
        feedforward_gain_value,
    )
    d_branch = middle_gradient.astype(jnp.bfloat16)
    d_attended = times_transpose(d_branch, back_proj).astype(jnp.bfloat16)
    d_grouped = d_attended.reshape(token_count, KV_HEADS, group_size, HEAD_DIM)
    weights = jnp.exp(score_all() - log_total)
    d_weights = jnp.einsum(
        "tkgd,skd->kgts", d_grouped, value_all, preferred_element_type=jnp.float32
    )
    d_scores = (
        weights * (d_weights - jnp.sum(weights * d_weights, axis=-1, keepdims=True))
    ).astype(jnp.bfloat16)
    d_queries = (
        jnp.einsum("kgts,skd->tkgd", d_scores, key_all, preferred_element_type=jnp.float32)
        * score_scale
    )
    d_key_all = (
        jnp.einsum("kgts,tkgd->skd", d_scores, grouped_q, preferred_element_type=jnp.float32)
        * score_scale
    )
    d_value_all = jnp.einsum(
        "kgts,tkgd->skd", weights_low, d_grouped, preferred_element_type=jnp.float32
    )
    d_keys, d_values = (
        lax.psum_scatter(
            d_key_all.astype(jnp.bfloat16), "fsdp", scatter_dimension=0, tiled=True
        ).astype(jnp.float32),
        lax.psum_scatter(
            d_value_all.astype(jnp.bfloat16), "fsdp", scatter_dimension=0, tiled=True
        ).astype(jnp.float32),
    )
    d_qkv = jnp.concatenate(
        [
            rotate_back(
                d_queries.reshape(token_count, HEADS, HEAD_DIM), cosine, sine_table
            ).reshape(token_count, q_cols),
            rotate_back(d_keys, cosine, sine_table).reshape(token_count, kv_cols),
            d_values.reshape(token_count, kv_cols),
        ],
        axis=1,
    ).astype(jnp.bfloat16)
    attention_normalized_gradient = times_transpose(d_qkv, back_qkv)
    attention_gain_piece = jnp.sum(attention_normalized_gradient * attention_unit_rows, axis=0)
    input_gradient = middle_gradient + norm_backward_step(
        attention_normalized_gradient,
        attention_unit_rows,
        attention_inverse_norm,
        attention_gain_value,
    )
    gains_term = jnp.stack([attention_gain_piece, feedforward_gain_piece], axis=1)
    gain_rows = lax.psum_scatter(gains_term, ("rep", "fsdp"), scatter_dimension=0, tiled=True)
    pairs = [
        (attention_normalized, d_qkv),
        (attended, d_branch),
        (feedforward_normalized, d_gate),
        (feedforward_normalized, d_up),
        (cotangent, hidden),
    ]
    owned = []
    for left_side, right_side in pairs:
        owned.append(owner_sum(left_side, right_side))
    return (
        layer_output,
        input_gradient,
        gain_rows[:, 0],
        owned[0],
        owned[1],
        gain_rows[:, 1],
        owned[2],
        owned[3],
        owned[4],
    )


def solution(mesh):
    in_specs = (
        P(("rep", "fsdp"), None),
        P(("rep", "fsdp")),
        P(("rep", "fsdp"), None),
        P(("rep", "fsdp")),
        P(("rep", "fsdp"), None),
        P(("rep", "fsdp"), None),
        P(("rep", "fsdp")),
        P(("rep", "fsdp"), None),
        P(("rep", "fsdp"), None),
        P(("rep", "fsdp"), None),
    )
    out_specs = (
        P(("rep", "fsdp"), None),
        P(("rep", "fsdp"), None),
        P(("rep", "fsdp")),
        P(("rep", "fsdp"), None),
        P(("rep", "fsdp"), None),
        P(("rep", "fsdp")),
        P(("rep", "fsdp"), None),
        P(("rep", "fsdp"), None),
        P(("rep", "fsdp"), None),
    )
    return jax.shard_map(shards, mesh=mesh, in_specs=in_specs, out_specs=out_specs, check_vma=False)
```

profile of v0, /device:TPU:11, one launch (start us, length us, event | category | flops | bytes accessed | tf_op | source)
XLA Modules:
  0.0 3386.1 jit_solution(7115424517110461536)
XLA Ops:
  9.7 40.6 %all-reduce.2 = (bf16[2048]{0:T(1024)(128)(2,1)S(1)}, bf16[2048]{0:T(1024)(128)(2,1)S(1)}) all-reduce(bf16[2048]{0:T(1024)(128)(2,1)S(1)} %dynamic-update-slice, bf16[2048]{0:T(1024)(128)(2,1)S(1)} %dynamic-update-slice.1), channel_id=1, replica_groups=mesh['rep'=8,'fsdp'=4] {'rep','fsdp'}, use_global_device_ids=true, to_apply=%add | all-reduce | flops 4096 | bytes 16384
  52.6 75.0 %all-gather.9.cloned.1.call-done = bf16[2048,4096]{1,0:T(8,128)(2,1)} async-done(((bf16[64,4096]{1,0:T(8,128)(2,1)}), bf16[2048,4096]{1,0:T(8,128)(2,1)}) %all-gather.9.cloned.1.call-update) | async-done | bytes 16777232 | tf_op jit(solution)/shard_map/all_gather | solution.py:71
  127.6 8.4 fusion.38
  141.0 5.3 all-gather
  147.2 6.4 all-gather.13.cloned.1.call-done
  153.6 2.0 fusion.6
  158.6 14.1 all-gather.11.cloned.1.call-done
  172.6 2.5 convolution_convert_fusion.5
  175.2 77.8 %all-gather.15.cloned.1.call-done = bf16[2048,2048]{1,0:T(8,128)(2,1)} async-done(((bf16[64,2048]{1,0:T(8,128)(2,1)}), bf16[2048,2048]{1,0:T(8,128)(2,1)}) %all-gather.15.cloned.1.call-update) | async-done | bytes 8388624 | tf_op jit(solution)/shard_map/all_gather | solution.py:72
  252.9 4.9 multiply_reduce_fusion.2
  258.8 188.3 %all-gather.19.cloned.1.call-done = bf16[2048,8192]{1,0:T(8,128)(2,1)} async-done(((bf16[64,8192]{1,0:T(8,128)(2,1)}), bf16[2048,8192]{1,0:T(8,128)(2,1)}) %all-gather.19.cloned.1.call-update) | async-done | bytes 33554448 | tf_op jit(solution)/shard_map/all_gather | solution.py:77
  447.2 17.2 fusion.50
  464.4 178.5 %all-gather.17.cloned.1.call-done = bf16[2048,8192]{1,0:T(8,128)(2,1)} async-done(((bf16[64,8192]{1,0:T(8,128)(2,1)}), bf16[2048,8192]{1,0:T(8,128)(2,1)}) %all-gather.17.cloned.1.call-update) | async-done | bytes 33554448 | tf_op jit(solution)/shard_map/all_gather | solution.py:76
  642.9 17.4 fusion.49
  660.3 178.4 %all-gather.21.cloned.1.call-done = bf16[2048,8192]{1,0:T(8,128)(2,1)} async-done(((bf16[64,8192]{1,0:T(8,128)(2,1)}), bf16[2048,8192]{1,0:T(8,128)(2,1)}) %all-gather.21.cloned.1.call-update) | async-done | bytes 33554448 | tf_op jit(solution)/shard_map/all_gather | solution.py:78
  838.7 19.4 multiply_convert_fusion
  858.1 16.3 fusion.51
  874.4 18.1 multiply_reduce_fusion
  895.1 7.1 convolution_convert_fusion.4
  902.1 2.0 copy.137
  904.2 4.2 fusion
  912.8 2.8 bitcast_convert_fusion
  915.6 2.3 copy.133
  917.9 7.0 convolution_convert_fusion.3
  928.7 8.7 reduce-scatter.20.cloned.1.call-done
  940.0 25.1 reduce-scatter.40.cloned.1.call-done
  966.2 10.2 convolution_convert_fusion.2
  977.5 15.5 convert_bitcast_fusion
  994.0 15.5 convolution_convert_fusion
  1009.5 15.4 convolution_convert_fusion.1
  1025.2 12.6 fusion.18
  1039.3 76.8 %reduce-scatter.26.cloned.1.call-done = bf16[256,2048]{1,0:T(8,128)(2,1)} async-done(((bf16[2048,2048]{1,0:T(8,128)(2,1)}), bf16[256,2048]{1,0:T(8,128)(2,1)}) %reduce-scatter.26.cloned.1.call-update) | async-done | bytes 1048592 | tf_op jit(solution)/shard_map/reduce_scatter | solution.py:50
  1116.1 285.7 %reduce-scatter.22.cloned.1.call-done = bf16[256,4096]{1,0:T(8,128)(2,1)} async-done(((bf16[2048,4096]{1,0:T(8,128)(2,1)}), bf16[256,4096]{1,0:T(8,128)(2,1)}) %reduce-scatter.22.cloned.1.call-update) | async-done | bytes 2097168 | tf_op jit(solution)/shard_map/reduce_scatter | solution.py:50
  1401.8 545.4 %reduce-scatter.38.cloned.1.call-done = bf16[256,8192]{0,1:T(8,128)(2,1)} async-done(((bf16[2048,8192]{0,1:T(8,128)(2,1)}), bf16[256,8192]{0,1:T(8,128)(2,1)}) %reduce-scatter.38.cloned.1.call-update) | async-done | bytes 4194320 | tf_op jit(solution)/shard_map/reduce_scatter | solution.py:50
  1947.2 6.4 copy.131
  1953.7 539.4 %reduce-scatter.34.cloned.1.call-done = bf16[256,8192]{1,0:T(8,128)(2,1)} async-done(((bf16[2048,8192]{1,0:T(8,128)(2,1)}), bf16[256,8192]{1,0:T(8,128)(2,1)}) %reduce-scatter.34.cloned.1.call-update) | async-done | bytes 4194320 | tf_op jit(solution)/shard_map/reduce_scatter | solution.py:50
  2493.2 546.0 %reduce-scatter.30.cloned.1.call-done = bf16[256,8192]{1,0:T(8,128)(2,1)} async-done(((bf16[2048,8192]{1,0:T(8,128)(2,1)}), bf16[256,8192]{1,0:T(8,128)(2,1)}) %reduce-scatter.30.cloned.1.call-update) | async-done | bytes 4194320 | tf_op jit(solution)/shard_map/reduce_scatter | solution.py:50
  3039.2 17.4 fusion.5
  3057.9 87.2 %reduce-scatter.42.cloned.1.call-done = f32[64,2]{1,0:T(8,128)} async-done(((f32[2048,2]{1,0:T(8,128)}), f32[64,2]{1,0:T(8,128)}) %reduce-scatter.42.cloned.1.call-update) | async-done | bytes 528
  3147.2 54.1 %reduce-scatter.28.cloned.1.call-done = bf16[64,2048]{1,0:T(8,128)(2,1)} async-done(((bf16[256,2048]{1,0:T(8,128)(2,1)}), bf16[64,2048]{1,0:T(8,128)(2,1)}) %reduce-scatter.28.cloned.1.call-update) | async-done | bytes 262160 | tf_op jit(solution)/shard_map/reduce_scatter | solution.py:58
  3203.0 32.0 reduce-scatter.24.cloned.1.call-done
  3235.1 2.1 convert_element_type.142
  3237.2 45.0 %reduce-scatter.44.cloned.1.call-done = bf16[64,8192]{1,0:T(8,128)(2,1)} async-done(((bf16[256,8192]{1,0:T(8,128)(2,1)}), bf16[64,8192]{1,0:T(8,128)(2,1)}) %reduce-scatter.44.cloned.1.call-update) | async-done | bytes 1048592
  3282.1 2.0 copy.132
  3286.0 43.2 %reduce-scatter.36.cloned.1.call-done = bf16[64,8192]{1,0:T(8,128)(2,1)} async-done(((bf16[256,8192]{1,0:T(8,128)(2,1)}), bf16[64,8192]{1,0:T(8,128)(2,1)}) %reduce-scatter.36.cloned.1.call-update) | async-done | bytes 1048592 | tf_op jit(solution)/shard_map/reduce_scatter | solution.py:58
  3329.2 2.7 convert_element_type.148
  3331.9 44.4 %reduce-scatter.32.cloned.1.call-done = bf16[64,8192]{1,0:T(8,128)(2,1)} async-done(((bf16[256,8192]{1,0:T(8,128)(2,1)}), bf16[64,8192]{1,0:T(8,128)(2,1)}) %reduce-scatter.32.cloned.1.call-update) | async-done | bytes 1048592 | tf_op jit(solution)/shard_map/reduce_scatter | solution.py:58
  3376.3 2.7 convert_element_type.146
  (121 shorter events, 39.9 us)
Async XLA Ops:
  7.2 120.5 %all-gather.9.cloned.1.call-start = ((), (), s32[]{:S(2)}) async-start(), calls=%async_computation.13 | async-start | bytes 17301504 | tf_op jit(solution)/shard_map/all_gather | solution.py:71
  7.9 145.7 %all-gather.13.cloned.1.call-start = ((), (), s32[]{:S(2)}) async-start(), calls=%async_computation.15 | async-start | bytes 1310720 | tf_op jit(solution)/shard_map/all_gather | solution.py:102
  136.1 4.9 copy-start.13
  137.3 35.4 %all-gather.11.cloned.1.call-start = ((), (), s32[]{:S(2)}) async-start(), calls=%async_computation.14 | async-start | bytes 1310720 | tf_op jit(solution)/shard_map/all_gather | solution.py:103
  138.2 114.7 %all-gather.15.cloned.1.call-start = ((), (), s32[]{:S(2)}) async-start(), calls=%async_computation.16 | async-start | bytes 8650752 | tf_op jit(solution)/shard_map/all_gather | solution.py:72
  138.8 308.4 %all-gather.19.cloned.1.call-start = ((), (), s32[]{:S(2)}) async-start(), calls=%async_computation.18 | async-start | bytes 34603008 | tf_op jit(solution)/shard_map/all_gather | solution.py:77
  139.4 503.5 %all-gather.17.cloned.1.call-start = ((), (), s32[]{:S(2)}) async-start(), calls=%async_computation.17 | async-start | bytes 34603008 | tf_op jit(solution)/shard_map/all_gather | solution.py:76
  140.0 698.8 %all-gather.21.cloned.1.call-start = ((), (), s32[]{:S(2)}) async-start(), calls=%async_computation.19 | async-start | bytes 34603008 | tf_op jit(solution)/shard_map/all_gather | solution.py:78
  140.7 796.7 %reduce-scatter.20.cloned.1.call-start = ((), (), s32[]{:S(2)}) async-start(), calls=%async_computation.20 | async-start | bytes 1310720 | tf_op jit(solution)/shard_map/reduce_scatter | solution.py:193
  147.2 8.4 copy-start.8
  155.5 2.0 copy-start
  874.4 18.2 copy-start.10
  894.1 1.0 copy-start.4
  904.2 4.2 copy-start.1
  908.4 2.6 copy-start.9
  909.6 1.3 copy-start.2
  912.7 52.3 %reduce-scatter.40.cloned.1.call-start = ((), (), s32[]{:S(2)}) async-start(), calls=%async_computation.30 | async-start | bytes 1310720
  917.9 198.2 %reduce-scatter.26.cloned.1.call-start = ((), (), s32[]{:S(2)}) async-start(), calls=%async_computation.23 | async-start | bytes 9437184 | tf_op jit(solution)/shard_map/reduce_scatter | solution.py:50
  924.9 1.6 copy-start.3
  925.0 476.8 %reduce-scatter.22.cloned.1.call-start = ((), (), s32[]{:S(2)}) async-start(), calls=%async_computation.21 | async-start | bytes 18874368 | tf_op jit(solution)/shard_map/reduce_scatter | solution.py:50
  928.6 37.6 %copy-start.6 = (bf16[128,2048]{1,0:T(8,128)(2,1)S(1)}, bf16[128,2048]{1,0:T(8,128)(2,1)}, u32[]{:S(2)}) copy-start(bf16[128,2048]{1,0:T(8,128)(2,1)} %param.10) | copy-start | bytes 1572868
  976.3 1.1 copy-start.11
  976.4 970.8 %reduce-scatter.38.cloned.1.call-start = ((), (), s32[]{:S(2)}) async-start(), calls=%async_computation.29 | async-start | bytes 37748736 | tf_op jit(solution)/shard_map/reduce_scatter | solution.py:50
  992.9 1.0 copy-start.7
  992.9 1500.2 %reduce-scatter.34.cloned.1.call-start = ((), (), s32[]{:S(2)}) async-start(), calls=%async_computation.27 | async-start | bytes 37748736 | tf_op jit(solution)/shard_map/reduce_scatter | solution.py:50
  1009.5 2029.6 %reduce-scatter.30.cloned.1.call-start = ((), (), s32[]{:S(2)}) async-start(), calls=%async_computation.25 | async-start | bytes 37748736 | tf_op jit(solution)/shard_map/reduce_scatter | solution.py:50
  1025.0 2120.1 %reduce-scatter.42.cloned.1.call-start = ((), (), s32[]{:S(2)}) async-start(), calls=%async_computation.31 | async-start | bytes 1081344
  1039.2 2162.0 %reduce-scatter.28.cloned.1.call-start = ((), (), s32[]{:S(2)}) async-start(), calls=%async_computation.24 | async-start | bytes 1310720 | tf_op jit(solution)/shard_map/reduce_scatter | solution.py:58
  1116.1 2119.0 %reduce-scatter.24.cloned.1.call-start = ((), (), s32[]{:S(2)}) async-start(), calls=%async_computation.22 | async-start | bytes 2621440 | tf_op jit(solution)/shard_map/reduce_scatter | solution.py:58
  1401.8 1880.4 %reduce-scatter.44.cloned.1.call-start = ((), (), s32[]{:S(2)}) async-start(), calls=%async_computation.32 | async-start | bytes 5242880
  1953.6 1375.6 %reduce-scatter.36.cloned.1.call-start = ((), (), s32[]{:S(2)}) async-start(), calls=%async_computation.28 | async-start | bytes 5242880 | tf_op jit(solution)/shard_map/reduce_scatter | solution.py:58
  2493.1 883.2 %reduce-scatter.32.cloned.1.call-start = ((), (), s32[]{:S(2)}) async-start(), calls=%async_computation.26 | async-start | bytes 5242880 | tf_op jit(solution)/shard_map/reduce_scatter | solution.py:58
  3039.1 17.4 copy-start.5
  3039.2 17.4 copy-start.12
Sparse Core Ops, SparseCore 0:
  10.9 116.7 all-gather.8
  137.4 16.1 all-gather.12
  155.7 16.8 all-gather.10
  175.3 77.5 all-gather.14
  255.6 191.4 all-gather.18
  449.9 192.9 all-gather.16
  645.7 192.9 all-gather.20
  912.8 24.5 reduce-scatter.19
  940.1 24.8 reduce-scatter.39
  968.5 147.4 reduce-scatter.25
  1120.3 281.4 reduce-scatter.21
  1405.4 541.7 reduce-scatter.37
  1951.0 542.0 reduce-scatter.33
  2496.7 542.3 reduce-scatter.29
  3041.8 103.2 reduce-scatter.41
  3147.6 53.5 reduce-scatter.27
  3203.6 31.4 reduce-scatter.23
  3237.6 44.4 reduce-scatter.43
  3284.7 44.4 reduce-scatter.35
  3331.7 44.5 reduce-scatter.31
where the time goes:
time: 3390 us
  waiting for transfers between devices  3050 us (90%)
  matrix products  217 us (6%)
  blocking collectives  45.8 us (1%)
    reduce_scatter x5, waiting for transfers between devices, owner_sum(): lax.psum_scatter(lax.dot_general(left_side, right_side, (((0,), (0,)), ((...  1990 us
    all_gather x1, waiting for transfers between devices, shards(): lax.all_gather(w_up, ('rep', 'fsdp'), axis=0, tiled=True)  188 us
    all_gather x1, waiting for transfers between devices, shards(): lax.all_gather(w_gate, ('rep', 'fsdp'), axis=0, tiled=True)  178 us
    all_gather x1, waiting for transfers between devices, shards(): lax.all_gather(w_down, ('rep', 'fsdp'), axis=0, tiled=True)  178 us
    reduce_scatter x4, waiting for transfers between devices, owner_sum(): lax.psum_scatter(section, 'fsdp', scatter_dimension=0, tiled=True)  174 us
    unnamed x23, waiting for transfers between devices  160 us
    all_gather x1, waiting for transfers between devices, shards(): lax.all_gather(w_out, ('rep', 'fsdp'), axis=0, tiled=True)  77.8 us
    all_gather x1, waiting for transfers between devices, shards(): lax.all_gather(w_qkv, ('rep', 'fsdp'), axis=0, tiled=True)  75 us
  transfers between devices with their start and end apart: 20, of which 20 were waited for; matrix products, arithmetic and copies ran while one was open for 5% of the time, Pallas kernels for 0%

commit v1 on v0

v1 whole, which is shorter than its diff:
```python
import functools

import jax
import jax.numpy as jnp
from jax import lax
from jax.experimental import pallas as pl
from jax.experimental.pallas import tpu as pltpu
from jax.sharding import PartitionSpec as P

HEADS = 16
KV_HEADS = 8
HEAD_DIM = 128
BLOCK = 256
MOST_BLOCKS = 2
GROUP = HEADS // KV_HEADS
EPS = 1e-05
THETA = 1000000.0
MESH = pl.DeviceIdType.MESH
F32 = jnp.float32
BF16 = jnp.bfloat16

PLANE = 8
DEPTH = 4
FLIPS = [(1, 0), (0, 1), (1, 1)]


def rope_tables(places, head_width):
    frequency = THETA ** (-(jnp.arange(0, head_width, 2, dtype=F32) / head_width))
    angles = places.astype(F32)[:, None] * frequency[None, :]
    cosine, sine = jnp.cos(angles), jnp.sin(angles)
    return jnp.concatenate([cosine, cosine], axis=1), jnp.concatenate([-sine, sine], axis=1)


def dot(a, b, dims=((1,), (0,))):
    return lax.dot_general(a, b, (dims, ((), ())), preferred_element_type=F32)


NT = ((1,), (1,))
TN = ((0,), (0,))


def flip(bit, by):
    return lax.rem(bit + by, 2)


class Place:
    def __init__(self):
        rep, self.f = lax.axis_index("rep"), lax.axis_index("fsdp")
        self.r = lax.rem(rep, PLANE)
        self.base = rep - self.r
        self.z, self.x = lax.div(self.r, 2), lax.rem(self.r, 2)
        self.y, self.c = lax.div(self.f, 2), lax.rem(self.f, 2)
        self.p = self.x * 4 + self.f
        self.q = self.z * 2 + self.c
        self.d = self.r * 4 + self.f

    def at(self, z, x, y, c):
        return (self.base + z * 2 + x, y * 2 + c)

    def plane(self, dx, dy, dc):
        x, y, c = flip(self.x, dx), flip(self.y, dy), flip(self.c, dc)
        return self.at(self.z, x, y, c), x * 4 + y * 2 + c

    def column(self, dz, dc):
        z, c = lax.rem(self.z + dz, DEPTH), flip(self.c, dc)
        return self.at(z, self.x, self.y, c), z, c

    def behind(self, dz):
        return lax.rem(self.z + (DEPTH - dz), DEPTH)


class Net:
    def __init__(self, send, recv, local):
        self.send, self.recv, self.local_sem = send, recv, local
        self.used = 0
        self.sent, self.kept = [], []

    def take(self, count):
        self.used += count
        return self.used - count

    def copy(self, src, dst, send, recv, device):
        return pltpu.make_async_remote_copy(
            src_ref=src,
            dst_ref=dst,
            send_sem=self.send.at[send],
            recv_sem=self.recv.at[recv],
            device_id=device,
            device_id_type=MESH,
        )

    def put(self, src, dst, device):
        k = self.take(1)
        copy = self.copy(src, dst, k, k, device)
        copy.start()
        self.sent.append((None, copy))
        return copy

    def put_if(self, when, copy):
        pl.when(when)(copy.start)
        self.sent.append((when, copy))
        return copy

    def keep(self, src, dst):
        copy = pltpu.make_async_copy(src, dst, self.local_sem.at[len(self.kept)])
        copy.start()
        self.kept.append(copy)
        return copy

    def finish(self):
        for when, copy in self.sent:
            if when is None:
                copy.wait_send()
            else:
                pl.when(when)(copy.wait_send)


class Chain:
    def __init__(self, me, net, slot, twins=None):
        self.me, self.net, self.slot, self.twins = me, net, slot, twins
        self.base = net.take(8)
        last = DEPTH - 1
        self.first, self.last = me.z == 0, me.z == last
        self.inner = jnp.logical_and(me.z > 0, me.z < last)
        self.order = [
            me.z,
            1 + lax.rem(me.z, 2),
            jnp.where(self.inner, last * (me.z - 1), 2 - lax.div(me.z, last)),
            last * (1 - lax.div(me.z, 2)),
        ]

    def link(self, z, k, target):
        me = self.me
        ref = self.slot(z, me.c)
        return self.net.copy(ref, ref, self.base + k, self.base + z, me.at(target, me.x, me.y, me.c))

    def start(self):
        me, net = self.me, self.net
        net.put_if(jnp.logical_not(self.last), self.link(me.z, 0, me.z + 1))
        net.put_if(jnp.logical_not(self.first), self.link(me.z, 1, me.z - 1))
        if self.twins is not None:
            self.twin(me.z, 0)

    def twin(self, z, k):
        ref, net = self.slot(z, self.me.c), self.net
        copy = net.copy(ref, ref, self.base + 4 + k, self.base + 4 + z, self.twins)
        copy.start()
        net.sent.append((None, copy))

    def arrival(self, i):
        me, net = self.me, self.net
        z = self.order[i]
        onward = self.link(z, 1 + i, me.z + jnp.where(z < me.z, 1, -1))
        across = None
        net.sent.append((self.inner, onward))
        if self.twins is not None:
            ref = self.slot(z, me.c)
            across = net.copy(ref, ref, self.base + 4 + i, self.base + 4 + z, self.twins)
            net.sent.append((None, across))

        def take(passes):
            onward.wait_recv()
            if passes:
                onward.start()
            if across is not None:
                across.start()

        return (
            lambda: pl.when(self.inner)(lambda: take(True)),
            lambda: pl.when(jnp.logical_not(self.inner))(lambda: take(False)),
        )

    def arrive(self, i):
        for step in self.arrival(i):
            step()

    def twin_has(self, z):
        ref = self.slot(z, 1 - self.me.c)
        self.net.copy(ref, ref, self.base + 4, self.base + 4 + z, self.twins).wait_recv()

    def twin_all(self):
        for z in range(DEPTH):
            self.twin_has(z)


def greet(devices):
    barrier = pltpu.get_barrier_semaphore()
    for device in devices:
        pl.semaphore_signal(barrier, inc=1, device_id=device, device_id_type=MESH)
    return barrier


def plane_ids(me):
    return [
        me.plane(dx, dy, dc)[0] for dx in (0, 1) for dy in (0, 1) for dc in (0, 1) if dx + dy + dc
    ]


def column_ids(me):
    return [me.column(dz, dc)[0] for dz in range(1, DEPTH) for dc in (0, 1)]


def sems(sends, locals_):
    return [
        pltpu.SemaphoreType.DMA((sends,)),
        pltpu.SemaphoreType.DMA((sends,)),
        pltpu.SemaphoreType.DMA((locals_,)),
    ]


ANY = pl.BlockSpec(memory_space=pl.ANY)


def call(kernel, ident, outs, args, sends, locals_, scratch=()):
    return pl.pallas_call(
        kernel,
        out_shape=outs,
        in_specs=[ANY] * len(args),
        out_specs=[ANY] * len(outs),
        scratch_shapes=list(scratch) + sems(sends, locals_),
        compiler_params=pltpu.CompilerParams(
            collective_id=ident, has_side_effects=True, vmem_limit_bytes=60 * 1024 * 1024
        ),
    )(*args)


def swap_owner(me):
    there = me.at(me.f, lax.div(me.r, 4), lax.div(lax.rem(me.r, 4), 2), lax.rem(me.r, 2))
    back = (me.base + me.p, me.z)
    away = jnp.logical_or(me.r != me.p, me.f != me.z)
    return there, back, away


def turn(v):
    return pltpu.roll(v, HEAD_DIM // 2, 1)


def attend(R, T, codes, P, A, seq, length):
    half = length // 2
    keys_at = pl.ds(pl.multiple_of(seq * length, length), length)
    keys = R[keys_at, GROUP * HEAD_DIM : (GROUP + 1) * HEAD_DIM]
    values = R[keys_at, (GROUP + 1) * HEAD_DIM :]
    code = codes[seq, 0:1, :]
    for h in range(GROUP):
        cols = slice(h * HEAD_DIM, (h + 1) * HEAD_DIM)
        for part in range(2):
            rows = pl.ds(pl.multiple_of(seq * length + part * half, half), half)
            scores = dot(R[rows, cols], keys, NT) * HEAD_DIM ** (-0.5)
            most, least = T[2, rows, 0:1], T[2, rows, HEAD_DIM // 2 : HEAD_DIM // 2 + 1]
            scores = jnp.where((code <= most) & (code >= least), scores, -1e30)
            exponent = jnp.exp(scores - jnp.max(scores, axis=-1, keepdims=True))
            weights = (exponent / jnp.sum(exponent, axis=-1, keepdims=True)).astype(BF16)
            P[h, rows, :] = weights
            A[rows, cols] = dot(weights, values).astype(BF16)


def front_kernel(
    x, tab, code, cot, wq, wo, wg, wu, wd,
    sums, Uo, Ro, Po, Ao, To, Wqo, Woo, cg, Wg, Wu, Wd,
    U, T, codes, Wq, Wo, R, P, A, E, left, right, send, recv, local,
):
    me = Place()
    net = Net(send, recv, local)
    tokens = x.shape[0]
    there, back, away = swap_owner(me)
    barrier = greet(plane_ids(me) + column_ids(me))

    @pl.when(away)
    def _():
        pl.semaphore_signal(barrier, inc=1, device_id=there, device_id_type=MESH)
        pl.semaphore_signal(barrier, inc=1, device_id=back, device_id_type=MESH)

    pl.semaphore_wait(barrier, jnp.where(away, 15, 13))
    twin = me.plane(0, 0, 1)[0]
    x_next, y_next = me.plane(1, 0, 0)[0], me.plane(0, 1, 0)[0]

    def to_column(w, W):
        got = []
        for dz in (2, 1, 3, 0):
            for dc in (0, 1):
                device, z, c = me.column(dz, dc)
                cols = pl.ds(pl.multiple_of((z * 2 + c) * 1024, 1024), 1024)
                if dz + dc:
                    got.append(net.put(w.at[:, cols], W.at[me.d], device))
                else:
                    own = net.keep(w.at[:, cols], W.at[me.d])
        return got, own

    def spread(W, arrived):
        got, own = arrived
        for copy in got:
            copy.wait_recv()
        own.wait()
        sent = []
        for z in range(DEPTH):
            rows = pl.ds(z * 8 + me.p - me.c, 2)
            sent.append((net.put(W.at[rows], W.at[rows], x_next), net.put(W.at[rows], W.at[rows], y_next)))
        return sent

    def relay(W, sent):
        last = []
        for z in range(DEPTH):
            by_x, by_y = sent[z]
            if z % 2:
                by_x.wait_recv()
                rows = pl.ds(z * 8 + me.plane(1, 0, 0)[1] - me.c, 2)
                last += [net.put(W.at[rows], W.at[rows], y_next), by_y]
            else:
                by_y.wait_recv()
                rows = pl.ds(z * 8 + me.plane(0, 1, 0)[1] - me.c, 2)
                last += [net.put(W.at[rows], W.at[rows], x_next), by_x]
        return last

    def slab(p):
        return pl.ds(pl.multiple_of(p * tokens, tokens), tokens)

    q_in = []
    for dx in (0, 1):
        for dy in (0, 1):
            for dc in (0, 1):
                if dx + dy + dc:
                    device, p = me.plane(dx, dy, dc)
                    q_in.append(net.put(wq.at[p], Wq.at[me.d], device))
    q_own = net.keep(wq.at[me.p], Wq.at[me.d])
    k = net.take(1)
    swap = net.copy(wo, Wo.at[me.f], k, k, there)
    stay = pltpu.make_async_copy(wo, Wo.at[me.f], local.at[local.shape[0] - 1])
    stays = jnp.logical_not(away)
    pl.when(away)(swap.start)
    pl.when(stays)(stay.start)
    x_in = []
    for dx, dy in FLIPS:
        device, p = me.plane(dx, dy, 0)
        x_in.append((net.put(x, U.at[slab(me.p)], device), p))
    x_late = [net.put(x, U.at[slab(me.p)], twin)]
    x_own = [net.keep(x, U.at[slab(me.p)])]
    seq = lax.div(me.p, 4)
    lanes = pl.ds(pl.multiple_of(lax.rem(me.p, 4) * tokens, tokens), tokens)
    for src, dst in ((tab, T.at[:, slab(me.p)]), (code, codes.at[seq, :, lanes])):
        for device in plane_ids(me):
            x_late.append(net.put(src, dst, device))
        x_own.append(net.keep(src, dst))
    gate_in = to_column(wg, Wg)
    for copy in q_in:
        copy.wait_recv()
    q_own.wait()
    q_chain = Chain(me, net, lambda z, c: Wq.at[pl.ds(z * PLANE, PLANE)])
    o_chain = Chain(me, net, lambda z, c: Wo.at[z])
    c_chain = Chain(me, net, lambda z, c: cg.at[z * 2 + c], twin)
    c_own = net.keep(cot, cg.at[me.q])
    q_chain.start()
    for copy, p in x_in:
        copy.wait_recv()
        x_late.append(net.put(U.at[slab(p)], U.at[slab(p)], twin))
    pl.when(away)(swap.wait)
    pl.when(stays)(stay.wait)
    o_chain.start()
    q_chain.arrive(1)
    gate_sent = spread(Wg, gate_in)
    up_in = to_column(wu, Wu)
    q_chain.arrive(2)
    o_chain.arrive(1)
    last = relay(Wg, gate_sent)
    o_chain.arrive(2)
    q_chain.arrive(3)
    o_chain.arrive(3)
    for copy in x_late:
        copy.wait_recv()
    for copy in x_own:
        copy.wait()

    block = 2 * tokens
    lead = GROUP * HEAD_DIM

    def project(i, carry):
        rows = pl.ds(pl.multiple_of(i * block, block), block)
        q = dot(U[rows, :], Wq[...].reshape(Wq.shape[0] * Wq.shape[1], Wq.shape[2]))
        cosine, sine = T[0, rows, :], T[1, rows, :]
        for h in range(GROUP + 1):
            v = q[:, h * HEAD_DIM : (h + 1) * HEAD_DIM]
            R[rows, h * HEAD_DIM : (h + 1) * HEAD_DIM] = (v * cosine + turn(v) * sine).astype(BF16)
        R[rows, lead + HEAD_DIM :] = q[:, lead + HEAD_DIM :].astype(BF16)
        return carry

    lax.fori_loop(0, 8 * tokens // block, project, 0)

    def one(seq, carry):
        attend(R, T, codes, P, A, seq, 4 * tokens)
        return carry

    lax.fori_loop(0, 2, one, 0)

    def out_block(i, carry):
        rows = pl.ds(pl.multiple_of(i * block, block), block)
        E[rows, :] = dot(A[rows, :], Wo[...].reshape(Wo.shape[0] * Wo.shape[1], Wo.shape[2])).astype(BF16)
        return carry

    lax.fori_loop(0, 8 * tokens // block, out_block, 0)
    peers = plane_peers(me)
    waits = reduce_start(me, net, E, peers, left, right, 0, slab)
    for src, dst in ((U, Uo), (R, Ro), (P, Po), (A, Ao), (T, To), (Wq, Wqo), (Wo, Woo)):
        net.keep(src, dst)
    stores = net.kept[-7:]
    up_sent = spread(Wu, up_in)
    down_in = to_column(wd, Wd)
    more, own = reduce_finish(net, sums, peers, left, right, 0, waits)
    c_own.wait()
    c_chain.start()
    last += relay(Wu, up_sent)
    c_chain.arrive(1)
    c_chain.arrive(2)
    down_sent = spread(Wd, down_in)
    c_chain.arrive(3)
    last += relay(Wd, down_sent)
    for copy in last + more:
        copy.wait_recv()
    c_chain.twin_all()
    for copy in own + stores:
        copy.wait()
    net.finish()


def add_into(left, right, k):
    rows = left.shape[1]

    def body(i, carry):
        at = pl.ds(pl.multiple_of(i * 16, 16), 16)
        left[k, at] = (left[k, at].astype(F32) + right[k, at].astype(F32)).astype(BF16)
        return carry

    lax.fori_loop(0, rows // 16, body, 0)


def reduce_start(me, net, part, peers, left, right, first, at=lambda p: p):
    twin = me.plane(0, 0, 1)[0]
    waits = []
    for k, (own, other, _) in enumerate(peers):
        got = net.put(part.at[at(other)], right.at[first + k], twin)
        mine = net.keep(part.at[at(own)], left.at[first + k])
        waits.append((got, mine))
    return waits


def reduce_finish(net, out, peers, left, right, first, waits):
    late, own = [], []
    for k, ((_, _, device), (got, mine)) in enumerate(zip(peers, waits)):
        got.wait_recv()
        mine.wait()
        add_into(left, right, first + k)
        if device is None:
            own.append(net.keep(left.at[first + k], out.at[k]))
        else:
            late.append(net.put(left.at[first + k], out.at[k], device))
    return late, own


def plane_peers(me):
    peers = []
    for dx, dy in FLIPS + [(0, 0)]:
        device, p = me.plane(dx, dy, 0)
        peers.append((p, me.plane(dx, dy, 1)[1], device if dx + dy else None))
    return peers


def column_peers(me):
    peers = []
    for dz in (2, 1, 3, 0):
        device, z, c = me.column(dz, 0)
        peers.append((z * 2 + c, z * 2 + flip(c, 1), device if dz else None))
    return peers


def ffn_kernel(x, cot, wg, wu, wd, e_out, o_out, gg, gu, gd, gain, N, C, Wg, Wu, Wd, H, DG, DU, O, E, R, G, S, n_send, n_recv, x_send, x_recv, e_send, e_recv, local):
    me = Place()
    tokens = x.shape[0]
    chip = 2 * tokens
    twin = me.plane(0, 0, 1)[0]
    ids = [me.column(dz, 0)[0] for dz in range(1, DEPTH)] + [twin]
    barrier = greet(ids)
    loads = [
        pltpu.make_async_copy(src, dst, local.at[i])
        for i, (src, dst) in enumerate(((wg, Wg), (wu, Wu), (wd, Wd), (cot, C)))
    ]
    for load in loads:
        load.start()
    own_rows = pl.ds(pl.multiple_of(me.q * tokens, tokens), tokens)
    mine = pltpu.make_async_copy(x, N.at[own_rows], local.at[4])
    mine.start()
    pl.semaphore_wait(barrier, 4)

    def rows_of(z, c):
        return pl.ds(pl.multiple_of((z * 2 + c) * tokens, tokens), tokens)

    def remote(src, dst, send, recv, device):
        return pltpu.make_async_remote_copy(
            src_ref=src,
            dst_ref=dst,
            send_sem=send,
            recv_sem=recv,
            device_id=device,
            device_id_type=MESH,
        )

    def column_id(z):
        return me.at(z, me.x, me.y, me.c)

    odd = lax.rem(me.z, 2)
    order = [me.z, 1 + odd, lax.rem(me.z + 2, DEPTH), 3 * (1 - odd)]
    net = Net(n_send, n_recv, local)
    chain = Chain(me, net, lambda z, c: N.at[rows_of(z, c)], twin)

    def twin_has(i):
        chain.twin_has(order[i])

    tile = 512

    def block(i):
        base = order[i] * chip
        rows = pl.ds(pl.multiple_of(base, chip), chip)

        def hidden_tile(t, carry):
            cols = pl.ds(pl.multiple_of(t * tile, tile), tile)
            gate = dot(N[rows, :], Wg[:, cols])
            raised = dot(N[rows, :], Wu[:, cols])
            d_hidden = dot(C[rows, :], Wd[:, cols])
            sig = jax.nn.sigmoid(gate)
            act = gate * sig
            H[rows, cols] = (act * raised).astype(BF16)
            DU[rows, cols] = (d_hidden * act).astype(BF16)
            DG[rows, cols] = (d_hidden * raised * sig * (1.0 + gate * (1.0 - sig))).astype(BF16)
            return carry

        lax.fori_loop(0, H.shape[1] // tile, hidden_tile, 0)

        def out_tile(t, carry):
            cols = pl.ds(pl.multiple_of(t * tile, tile), tile)
            e = dot(DG[rows, :], Wg[cols, :], NT) + dot(DU[rows, :], Wu[cols, :], NT)
            E[rows, cols] = e.astype(BF16)
            piece = jnp.sum((e * N[rows, cols].astype(F32)).reshape(chip // 8, 8, tile), axis=0)
            if i == 0:
                S[:, cols] = piece
            else:
                S[:, cols] += piece
            O[rows, cols] = dot(H[rows, :], Wd[cols, :], NT).astype(BF16)
            return carry

        lax.fori_loop(0, E.shape[1] // tile, out_tile, 0)

    swaps, sums = [], []

    def swap(i):
        o = order[i]
        copy = remote(E.at[rows_of(o, 1 - me.c)], R.at[i], x_send.at[i], x_recv.at[i], twin)
        copy.start()
        swaps.append(copy)

    def total(i):
        o = order[i]
        swaps[i].wait_recv()
        first = (o * 2 + me.c) * tokens

        def body(k, carry):
            at = pl.ds(pl.multiple_of(k * 16, 16), 16)
            to = pl.ds(pl.multiple_of(first + k * 16, 16), 16)
            E[to, :] = (E[to, :].astype(F32) + R[i, at, :].astype(F32)).astype(BF16)
            return carry

        lax.fori_loop(0, tokens // 16, body, 0)
        rows = rows_of(o, me.c)
        if i == 0:
            copy = pltpu.make_async_copy(E.at[rows], e_out.at[me.z], local.at[5])
        else:
            copy = remote(E.at[rows], e_out.at[me.z], e_send.at[i], e_recv.at[me.z], column_id(o))
        copy.start()
        sums.append(copy)

    mine.wait()
    chain.start()
    for load in loads:
        load.wait()
    twin_has(0)
    block(0)
    swap(0)
    chain.arrive(1)
    early, later = chain.arrival(2)
    early()
    twin_has(1)
    block(1)
    swap(1)
    total(0)
    later()
    chain.arrive(3)
    twin_has(2)
    block(2)
    swap(2)
    total(1)
    twin_has(3)
    block(3)
    swap(3)
    total(2)
    stores = [
        pltpu.make_async_copy(O, o_out, local.at[6]),
        pltpu.make_async_copy(S, gain, local.at[7]),
    ]
    for store in stores:
        store.start()
    total(3)

    span = 256

    def grad_tile(t, carry):
        rows = pl.ds(pl.multiple_of(t * span, span), span)
        n, c = N[:, rows], C[:, rows]
        G[0, rows, :] = dot(n, DG[...], TN).astype(BF16)
        G[1, rows, :] = dot(n, DU[...], TN).astype(BF16)
        G[2, rows, :] = dot(c, H[...], TN).astype(BF16)
        return carry

    lax.fori_loop(0, G.shape[1] // span, grad_tile, 0)
    for i, dst in enumerate((gg, gu, gd)):
        store = pltpu.make_async_copy(G.at[i], dst, local.at[8 + i])
        store.start()
        stores.append(store)
    for i in range(1, DEPTH):
        o = order[i]
        remote(E.at[own_rows], e_out.at[o], e_send.at[i], e_recv.at[o], twin).wait_recv()
    sums[0].wait()
    for copy in sums[1:] + swaps:
        copy.wait_send()
    net.finish()
    for store in stores:
        store.wait()


def add_rows(into, i, more, j):
    slots, rows = into.shape[-3], into.shape[-2]
    steps = rows // 16

    def body(k, carry):
        s, at = lax.div(k, steps), pl.ds(pl.multiple_of(lax.rem(k, steps) * 16, 16), 16)
        into[i, s, at] = (into[i, s, at].astype(F32) + more[j, s, at].astype(F32)).astype(BF16)
        return carry

    lax.fori_loop(0, slots * steps, body, 0)


def back_kernel(
    x, part_o, gg, gu, gd, gain_f, u, r, pw, att, t, wq, wo,
    out_o, out_e, og, ou, od, oq, oo, ov,
    D, U, R, P, A, T, Wq, Wo, dA, dR, E, GQ, GO, gains, left, right, own, side, came, rq, ro, rv,
    send, recv, local,
):
    me = Place()
    net = Net(send, recv, local)
    tokens = x.shape[0]
    back, there, away = swap_owner(me)
    barrier = greet(plane_ids(me) + column_ids(me))

    @pl.when(away)
    def _():
        pl.semaphore_signal(barrier, inc=1, device_id=there, device_id_type=MESH)
        pl.semaphore_signal(barrier, inc=1, device_id=back, device_id_type=MESH)

    pl.semaphore_wait(barrier, jnp.where(away, 15, 13))
    twin = me.plane(0, 0, 1)[0]
    x_next, px = me.plane(1, 0, 0)
    y_next, py = me.plane(0, 1, 0)
    pd = me.plane(1, 1, 0)[1]

    def slab(p):
        return pl.ds(pl.multiple_of(p * tokens, tokens), tokens)

    def quarter(grad, p, z):
        return grad.at[pl.ds(z * 8 + p - me.c, 2)]

    def first(g, grad):
        sent = []
        for z in range(DEPTH):
            device, near = (x_next, px) if z < 2 else (y_next, py)
            side_p = py if z < 2 else px
            at = pl.ds(z % 2 * 2, 2)
            half = z // 2
            sent.append(net.put(quarter(grad, near, z), came.at[g * 6 + half * 3, at], device))
            sent.append(net.put(quarter(grad, pd, z), came.at[g * 6 + half * 3 + 1, at], device))
            net.keep(quarter(grad, me.p, z), own.at[g * 2 + half, at])
            net.keep(quarter(grad, side_p, z), side.at[g * 2 + half, at])
        return sent, net.kept[-8:]

    def second(g, begun):
        sent, kept = begun
        for copy in sent:
            copy.wait_recv()
        for copy in kept:
            copy.wait()
        passed = []
        for half in (0, 1):
            add_rows(side, g * 2 + half, came, g * 6 + half * 3 + 1)
            device = x_next if half else y_next
            passed.append(net.put(side.at[g * 2 + half], came.at[g * 6 + half * 3 + 2], device))
        for half in (0, 1):
            add_rows(own, g * 2 + half, came, g * 6 + half * 3)
        return passed

    cols = pl.ds(pl.multiple_of(me.q * 1024, 1024), 1024)
    thirds = []

    def third(g, passed, out):
        for half in (0, 1):
            passed[half].wait_recv()
            add_rows(own, g * 2 + half, came, g * 6 + half * 3 + 2)
        for dz in (2, 1, 3, 0):
            for dc in (0, 1):
                device, z, c = me.column(dz, dc)
                src = own.at[g * 2 + lax.div(z, 2), lax.rem(z, 2) * 2 + c]
                if dz + dc:
                    late.append(net.put(src, out.at[:, cols], device))
                else:
                    thirds.append(net.keep(src, out.at[:, cols]))

    got = []
    for dx, dy in FLIPS:
        device, p = me.plane(dx, dy, 0)
        got.append((net.put(x, D.at[slab(me.p)], device), p))
    d_late = [net.put(x, D.at[slab(me.p)], twin)]
    loads = [net.keep(x, D.at[slab(me.p)])]
    for src, dst in ((wo, Wo), (att, A), (r, R), (pw, P), (t, T), (u, U), (wq, Wq), (gain_f, gains.at[1])):
        loads.append(net.keep(src, dst))
    late = []
    begun = [first(0, gd)]
    peers = column_peers(me)
    waits = reduce_start(me, net, part_o, peers, left, right, 0, slab)
    for copy, p in got:
        copy.wait_recv()
        d_late.append(net.put(D.at[slab(p)], D.at[slab(p)], twin))
    begun.append(first(1, gg))
    more, kept = reduce_finish(net, out_o, peers, left, right, 0, waits)
    for copy in d_late:
        copy.wait_recv()
    for copy in loads:
        copy.wait()

    block = 2 * tokens
    length = 4 * tokens
    lead = GROUP * HEAD_DIM
    scale = HEAD_DIM ** (-0.5)

    def d_attended(i, carry):
        rows = pl.ds(pl.multiple_of(i * block, block), block)
        dA[rows, :] = dot(D[rows, :], Wo[...].reshape(Wo.shape[0] * Wo.shape[1], Wo.shape[2]), NT).astype(BF16)
        return carry

    lax.fori_loop(0, 8 * tokens // block, d_attended, 0)

    def turn_back(v, rows):
        return (v * T[0, rows, :] - turn(v) * T[1, rows, :]).astype(BF16)

    def one(seq, carry):
        keys_at = pl.ds(pl.multiple_of(seq * length, length), length)
        keys = R[keys_at, lead : lead + HEAD_DIM]
        values = R[keys_at, lead + HEAD_DIM :]
        d_keys = jnp.zeros((length, HEAD_DIM), F32)
        d_values = jnp.zeros((length, HEAD_DIM), F32)
        for h in range(GROUP):
            cols = slice(h * HEAD_DIM, (h + 1) * HEAD_DIM)
            for part in range(2):
                rows = pl.ds(pl.multiple_of(seq * length + part * (length // 2), length // 2), length // 2)
                low = P[h, rows, :]
                weights = low.astype(F32)
                d_out = dA[rows, cols]
                d_weights = dot(d_out, values, NT)
                d_scores = (
                    weights * (d_weights - jnp.sum(weights * d_weights, axis=-1, keepdims=True))
                ).astype(BF16)
                dR[rows, cols] = turn_back(dot(d_scores, keys) * scale, rows)
                d_keys += dot(d_scores, R[rows, cols], TN)
                d_values += dot(low, d_out, TN)
        dR[keys_at, lead : lead + HEAD_DIM] = turn_back(d_keys * scale, keys_at)
        dR[keys_at, lead + HEAD_DIM :] = d_values.astype(BF16)
        return carry

    lax.fori_loop(0, 2, one, 0)
    tile = 512

    def e_tile(k, carry):
        i, j = lax.div(k, E.shape[1] // tile), lax.rem(k, E.shape[1] // tile)
        rows = pl.ds(pl.multiple_of(i * block, block), block)
        cols = pl.ds(pl.multiple_of(j * tile, tile), tile)
        slots = pl.ds(j * (tile // Wq.shape[1]), tile // Wq.shape[1])
        e = dot(dR[rows, :], Wq[slots].reshape(tile, Wq.shape[2]), NT)
        E[rows, cols] = e.astype(BF16)
        piece = jnp.sum((e * U[rows, cols].astype(F32)).reshape(block // 8, 8, tile), axis=0)
        gains[0, :, cols] = jnp.where(i == 0, 0.0, gains[0, :, cols]) + piece
        return carry

    lax.fori_loop(0, 8 * tokens // block * (E.shape[1] // tile), e_tile, 0)
    peers_e = plane_peers(me)
    waits_e = reduce_start(me, net, E, peers_e, left, right, 4, slab)
    passed = [second(0, begun[0])]
    begun.append(first(2, gu))
    span = 256

    def q_tile(k, carry):
        cols = pl.ds(pl.multiple_of(k * span, span), span)
        slots = pl.ds(k * (span // GQ.shape[1]), span // GQ.shape[1])
        g = dot(U[:, cols], dR[...], TN).astype(BF16)
        GQ[slots] = g.reshape(span // GQ.shape[1], GQ.shape[1], GQ.shape[2])
        return carry

    lax.fori_loop(0, U.shape[1] // span, q_tile, 0)

    def o_tile(k, carry):
        cols = pl.ds(pl.multiple_of(k * tile, tile), tile)
        g = dot(A[...], D[:, cols], TN).astype(BF16)
        GO[:, :, cols] = g.reshape(GO.shape[0], GO.shape[1], tile)
        return carry

    lax.fori_loop(0, D.shape[1] // tile, o_tile, 0)
    a_late, a_own = [], []
    for dz in (2, 1, 3, 0):
        device, z, _ = me.column(dz, 0)
        rows = pl.ds(z * PLANE, PLANE)
        lanes = pl.ds(pl.multiple_of(z * 512, 512), 512)
        for src, dst in (
            (GQ.at[rows], rq.at[dz]),
            (GO.at[z], ro.at[dz]),
            (gains.at[:, :, lanes], rv.at[dz]),
        ):
            if dz:
                a_late.append(net.put(src, dst, device))
            else:
                a_own.append(net.keep(src, dst))
    e_late, e_own = reduce_finish(net, out_e, peers_e, left, right, 4, waits_e)
    passed.append(second(1, begun[1]))
    third(0, passed[0], od)
    for copy in a_late:
        copy.wait_recv()
    for copy in a_own:
        copy.wait()

    def sum_q(k, carry):
        s, at = lax.div(k, 4), pl.ds(pl.multiple_of(lax.rem(k, 4) * 16, 16), 16)
        rq[0, s, at] = sum(rq[i, s, at].astype(F32) for i in range(DEPTH)).astype(BF16)
        return carry

    lax.fori_loop(0, PLANE * 4, sum_q, 0)

    def sum_o(k, carry):
        at = pl.ds(pl.multiple_of(k * 16, 16), 16)
        ro[0, at] = sum(ro[i, at].astype(F32) for i in range(DEPTH)).astype(BF16)
        return carry

    lax.fori_loop(0, ro.shape[1] // 16, sum_o, 0)
    rv[0] = rv[0] + rv[1] + rv[2] + rv[3]
    k = net.take(1)
    swap = net.copy(ro.at[0], oo, k, k, there)
    stay = pltpu.make_async_copy(ro.at[0], oo, local.at[local.shape[0] - 1])
    stays = jnp.logical_not(away)
    pl.when(away)(swap.start)
    pl.when(stays)(stay.start)
    for dx in (0, 1):
        for dy in (0, 1):
            for dc in (0, 1):
                device, p = me.plane(dx, dy, dc)
                lanes = pl.ds(pl.multiple_of(lax.div(p, 2) * 128, 128), 128)
                for src, dst in ((rq.at[0, p], oq.at[me.p]), (rv.at[0, :, :, lanes], ov.at[me.p])):
                    if dx + dy + dc:
                        late.append(net.put(src, dst, device))
                    else:
                        kept.append(net.keep(src, dst))
    passed.append(second(2, begun[2]))
    third(1, passed[1], og)
    third(2, passed[2], ou)
    for copy in late + more + e_late:
        copy.wait_recv()
    for copy in kept + e_own + thirds:
        copy.wait()
    net.finish()
    pl.when(away)(swap.wait)
    pl.when(stays)(stay.wait)


def shape(*dims, dtype=BF16):
    return jax.ShapeDtypeStruct(dims, dtype)


def shards(copies, block_input, positions, cotangent, norm_attn, w_qkv, w_out, norm_ffn, w_gate, w_up, w_down):
    tokens, width = block_input.shape
    ff = w_gate.shape[1]
    q_cols, kv_cols = HEADS * HEAD_DIM, KV_HEADS * HEAD_DIM
    spread = ("rep", "fsdp")
    place = lax.rem(lax.axis_index("rep"), PLANE) * 4 + lax.axis_index("fsdp")

    def take(w):
        if copies == 1:
            return w
        rows = w.shape[0] * copies
        whole = lax.all_gather(w, spread, axis=0, tiled=True)
        return lax.dynamic_slice_in_dim(whole, place * rows, rows, axis=0)

    def give(grad):
        if copies == 1:
            return grad
        rows = grad.shape[0]
        whole = jnp.zeros((rows * 32,) + grad.shape[1:], grad.dtype)
        whole = lax.dynamic_update_slice_in_dim(whole, grad, place * rows, axis=0)
        return lax.psum_scatter(whole, spread, scatter_dimension=0, tiled=True)

    gain_a = take(norm_attn).astype(F32)
    gain_f = take(norm_ffn).astype(F32)
    own_qkv = (take(w_qkv).astype(F32) * gain_a[:, None]).astype(BF16)
    rows = own_qkv.shape[0]
    own_qkv = jnp.concatenate(
        [
            own_qkv[:, :q_cols].reshape(rows, KV_HEADS, GROUP * HEAD_DIM),
            own_qkv[:, q_cols : q_cols + kv_cols].reshape(rows, KV_HEADS, HEAD_DIM),
            own_qkv[:, q_cols + kv_cols :].reshape(rows, KV_HEADS, HEAD_DIM),
        ],
        axis=2,
    ).transpose(1, 0, 2)
    own_gate = (take(w_gate).astype(F32) * gain_f[:, None]).astype(BF16)
    own_up = (take(w_up).astype(F32) * gain_f[:, None]).astype(BF16)
    own_down = take(w_down)
    own_out = take(w_out)
    head_cols = (GROUP + 2) * HEAD_DIM
    ff_cols = ff // 8
    full = 8 * tokens
    residual = block_input.astype(F32)
    inv_a = lax.rsqrt(jnp.mean(residual * residual, axis=-1, keepdims=True) + EPS)
    xhat_a = residual * inv_a
    cosine, sine = rope_tables(positions, HEAD_DIM)
    starts = lax.axis_index("fsdp") * tokens + jnp.arange(tokens, dtype=jnp.int32) - positions
    least = (starts * MOST_BLOCKS).astype(F32)
    code = least + (positions // BLOCK).astype(F32)
    half = HEAD_DIM // 2
    sees = jnp.concatenate(
        [jnp.broadcast_to(v[:, None], (tokens, half)) for v in (code, least)], axis=1
    )
    tables = jnp.stack([cosine, sine, sees])
    sums, U, R, Pw, A, T, Wq, Wo, cg, Wg, Wu, Wd = call(
        front_kernel,
        0,
        [
            shape(4, tokens, width),
            shape(full, width),
            shape(full, head_cols),
            shape(GROUP, full, full // 2),
            shape(full, GROUP * HEAD_DIM),
            shape(3, full, HEAD_DIM, dtype=F32),
            shape(32, rows, head_cols),
            shape(4, rows, width),
            shape(8, tokens, width),
            shape(32, rows, ff_cols),
            shape(32, rows, ff_cols),
            shape(32, rows, ff_cols),
        ],
        (
            xhat_a.astype(BF16),
            tables,
            jnp.broadcast_to(code[None, :], (8, tokens)),
            cotangent,
            own_qkv,
            own_out,
            own_gate,
            own_up,
            own_down,
        ),
        150,
        30,
        [
            pltpu.VMEM((full, width), BF16),
            pltpu.VMEM((3, full, HEAD_DIM), F32),
            pltpu.VMEM((2, 8, full // 2), F32),
            pltpu.VMEM((32, rows, head_cols), BF16),
            pltpu.VMEM((4, rows, width), BF16),
            pltpu.VMEM((full, head_cols), BF16),
            pltpu.VMEM((GROUP, full, full // 2), BF16),
            pltpu.VMEM((full, GROUP * HEAD_DIM), BF16),
            pltpu.VMEM((full, width), BF16),
            pltpu.VMEM((4, tokens, width), BF16),
            pltpu.VMEM((4, tokens, width), BF16),
        ],
    )
    cg = cg.reshape(full, width)
    Wg, Wu, Wd = [w.reshape(width, ff_cols) for w in (Wg, Wu, Wd)]

    middle = residual + jnp.sum(sums.astype(F32), axis=0)
    inv_f = lax.rsqrt(jnp.mean(middle * middle, axis=-1, keepdims=True) + EPS)
    unit_f = middle * inv_f
    e_sums, out_part, g_gate, g_up, g_down, gain_f_part = pl.pallas_call(
        ffn_kernel,
        out_shape=[
            shape(4, tokens, width),
            shape(full, width),
            shape(width, ff_cols),
            shape(width, ff_cols),
            shape(width, ff_cols),
            shape(8, width, dtype=F32),
        ],
        in_specs=[ANY] * 5,
        out_specs=[ANY] * 6,
        scratch_shapes=[pltpu.VMEM((full, width), BF16)] * 2
        + [pltpu.VMEM((width, ff_cols), BF16)] * 3
        + [pltpu.VMEM((full, ff_cols), BF16)] * 3
        + [pltpu.VMEM((full, width), BF16)] * 2
        + [
            pltpu.VMEM((4, tokens, width), BF16),
            pltpu.VMEM((3, width, ff_cols), BF16),
            pltpu.VMEM((8, width), F32),
        ]
        + [pltpu.SemaphoreType.DMA((8,))] * 6
        + [pltpu.SemaphoreType.DMA((12,))],
        compiler_params=pltpu.CompilerParams(
            collective_id=2, has_side_effects=True, vmem_limit_bytes=60 * 1024 * 1024
        ),
    )(unit_f.astype(BF16), cg, Wg, Wu, Wd)
    g_gate, g_up, g_down = [g.reshape(32, rows, ff_cols) for g in (g_gate, g_up, g_down)]
    e_own = jnp.sum(e_sums.astype(F32), axis=0)
    d_middle = cotangent.astype(F32) + inv_f * (
        e_own - unit_f * jnp.mean(e_own * unit_f, axis=-1, keepdims=True)
    )

    quad = pltpu.VMEM((8, tokens, width), BF16)
    out_sums, ea_sums, og, ou, od, oq, oo, ov = call(
        back_kernel,
        3,
        [shape(4, tokens, width)] * 2
        + [shape(rows, ff)] * 3
        + [
            shape(8, rows, head_cols),
            shape(rows, width),
            shape(8, 2, 8, 128, dtype=F32),
        ],
        (d_middle.astype(BF16), out_part, g_gate, g_up, g_down, gain_f_part, U, R, Pw, A, T, Wq, Wo),
        140,
        80,
        [
            pltpu.VMEM((full, width), BF16),
            pltpu.VMEM((full, width), BF16),
            pltpu.VMEM((full, head_cols), BF16),
            pltpu.VMEM((GROUP, full, full // 2), BF16),
            pltpu.VMEM((full, GROUP * HEAD_DIM), BF16),
            pltpu.VMEM((3, full, HEAD_DIM), F32),
            pltpu.VMEM((32, rows, head_cols), BF16),
            pltpu.VMEM((4, rows, width), BF16),
            pltpu.VMEM((full, GROUP * HEAD_DIM), BF16),
            pltpu.VMEM((full, head_cols), BF16),
            pltpu.VMEM((full, width), BF16),
            pltpu.VMEM((32, rows, head_cols), BF16),
            pltpu.VMEM((4, rows, width), BF16),
            pltpu.VMEM((2, 8, width), F32),
            quad,
            quad,
            pltpu.VMEM((6, 4, rows, ff_cols), BF16),
            pltpu.VMEM((6, 4, rows, ff_cols), BF16),
            pltpu.VMEM((18, 4, rows, ff_cols), BF16),
            pltpu.VMEM((4, 8, rows, head_cols), BF16),
            pltpu.VMEM((4, rows, width), BF16),
            pltpu.VMEM((4, 2, 8, 512), F32),
        ],
    )
    layer_output = (middle + jnp.sum(out_sums.astype(F32), axis=0)).astype(BF16)
    e_own_a = jnp.sum(ea_sums.astype(F32), axis=0)
    input_gradient = d_middle + inv_a * (
        e_own_a - xhat_a * jnp.mean(e_own_a * xhat_a, axis=-1, keepdims=True)
    )
    gain_sums = jnp.sum(ov, axis=(0, 2))
    gain_sums = lax.dynamic_slice_in_dim(gain_sums, place % 2 * rows, rows, axis=1)
    oq = oq.astype(F32) * gain_a[None, :, None]
    q_part = oq[:, :, : GROUP * HEAD_DIM].transpose(1, 0, 2).reshape(rows, q_cols)
    k_part = oq[:, :, GROUP * HEAD_DIM : (GROUP + 1) * HEAD_DIM].transpose(1, 0, 2)
    v_part = oq[:, :, (GROUP + 1) * HEAD_DIM :].transpose(1, 0, 2)
    grad_qkv = jnp.concatenate(
        [q_part, k_part.reshape(rows, kv_cols), v_part.reshape(rows, kv_cols)], axis=1
    )
    return (
        layer_output,
        input_gradient,
        give(gain_sums[0] / gain_a),
        give(grad_qkv),
        give(oo.astype(F32)),
        give(gain_sums[1] / gain_f),
        give(og.astype(F32) * gain_f[:, None]),
        give(ou.astype(F32) * gain_f[:, None]),
        give(od.astype(F32)),
    )


def solution(mesh):
    copies = mesh.shape["rep"] * mesh.shape["fsdp"] // 32
    rows, flat = P(("rep", "fsdp"), None), P(("rep", "fsdp"))
    return jax.shard_map(
        functools.partial(shards, copies),
        mesh=mesh,
        in_specs=(rows, flat, rows, flat, rows, rows, flat, rows, rows, rows),
        out_specs=(rows, rows, flat, rows, rows, flat, rows, rows, rows),
        check_vma=False,
    )
```

time: 3390 us -> 562 us (0.17)
  waiting for transfers between devices: 3050 us -> 0 us
  Pallas kernels: 0 us -> 521 us
  matrix products: 217 us -> 0 us
  blocking collectives: 45.8 us -> 0 us
    reduce_scatter x10 -> x0, waiting for transfers between devices: 2180 us -> none  [the longest x5 1990 us: owner_sum(): lax.psum_scatter(lax.dot_general(left_side, right_side, (((0,), (0,)), ((...]
    all_gather x7 -> x0, waiting for transfers between devices: 718 us -> none  [the longest x1 188 us: shards(): lax.all_gather(w_up, ('rep', 'fsdp'), axis=0, tiled=True)]
    pallas_call x0 -> x3, Pallas kernels: none -> 521 us  [the longest x2 423 us: call(): pl.pallas_call(kernel, out_shape=outs, in_specs=[ANY] * len(args), out_sp...]
    dot_general x21 -> x0, matrix products: 217 us -> none  [the longest x5 71.4 us: times_transpose(): lax.dot_general(left_side, right_side, (((1,), (1,)), ((), ())), preferre...]
    unnamed x23 -> x0, waiting for transfers between devices: 160 us -> none
    unnamed x1 -> x0, blocking collectives: 40.6 us -> none
  transfers between devices with their start and end apart: 20 -> 0, of which waited for: 20 -> 0; matrix products, arithmetic and copies ran while one was open for 5% -> 0% of each run, Pallas kernels for 0% -> 0%
where the time goes in v1:
time: 562 us; the launch traced here: 555 us
  Pallas kernels  521 us (93%)
  other arithmetic  29 us (5%)
    pallas_call x2, Pallas kernels, call(): pl.pallas_call(kernel, out_shape=outs, in_specs=[ANY] * len(args), out_sp...  423 us
    pallas_call x1, Pallas kernels, shards(): pl.pallas_call(ffn_kernel, out_shape=[shape(4, tokens, width), shape(full...  98 us

profile of v1, /device:TPU:11, one launch (start us, length us, event | category | flops | bytes accessed | tf_op | source)
XLA Modules:
  0.0 555.0 jit_solution(3195311762426344055)
XLA Ops:
  0.7 0.7 convert_add_fusion.1
  1.4 0.7 convert_element_type.84
  2.1 0.7 convert_element_type.87
  2.7 1.2 fusion.7
  4.0 0.7 fusion.10
  4.7 0.6 broadcast_in_dim.8.code
  5.3 0.1 broadcast_in_dim.6
  5.4 0.1 broadcast_in_dim.7
  5.5 0.1 maximum_bitcast_fusion.3
  5.6 0.3 multiply_cosine_fusion
  5.9 0.1 maximum_bitcast_fusion.1
  6.0 0.7 pad_maximum_fusion.1.tab
  6.7 0.0 copy-done.9
  6.7 0.2 multiply_convert_fusion.2
  6.8 0.0 copy-start.4
  6.8 0.0 copy-start.5
  6.9 0.1 copy_bitcast_fusion.3
  7.0 0.8 maximum_bitcast_fusion.wq
  7.9 0.9 fusion.2.x
  8.8 1.8 multiply_convert_fusion
  10.6 199.3 %shard_map.169 = (bf16[4,128,2048]{2,1,0:T(8,128)(2,1)}, bf16[1024,2048]{1,0:T(8,128)(2,1)}, bf16[1024,512]{1,0:T(8,128)(2,1)}, bf16[2,1024,512]{2,1,0:T(8,128)(...) custom-call(bf16[128,2048]{1,0:T(8,128)(2,1)} %fusion.2.x, ...), custom_call_target="tpu_custom_call" | custom-call | tf_op jit(solution)/shard_map/pallas_call | solution.py:215
  209.9 2.1 convert_reduce_fusion.3
  211.9 0.2 multiply_reduce_fusion.1
  212.2 0.9 multiply_convert_fusion.3.x
  213.1 98.0 %shard_map.170 = (bf16[4,128,2048]{2,1,0:T(8,128)(2,1)}, bf16[1024,2048]{1,0:T(8,128)(2,1)}, bf16[2048,1024]{1,0:T(8,128)(2,1)}, bf16[2048,1024]{1,0:T(8,128)(2,...) custom-call(bf16[128,2048]{1,0:T(8,128)(2,1)} %multiply_convert_fusion.3.x, bf16[1024,2048]{1,0:T(8,128)(2,1)} %bitcast.50, ...), custom_call_target="tpu_custom_call" | custom-call | tf_op jit(solution)/shard_map/pallas_call | solution.py:989
  311.1 2.1 convert_reduce_fusion.2
  313.2 0.0 copy-start.1
  313.2 0.3 multiply_reduce_fusion
  313.5 0.7 copy-done.1
  314.2 1.2 fusion.9.x
  315.4 223.9 %shard_map.171 = (bf16[4,128,2048]{2,1,0:T(8,128)(2,1)}, bf16[4,128,2048]{2,1,0:T(8,128)(2,1)}, bf16[64,8192]{1,0:T(8,128)(2,1)}, bf16[64,8192]{1,0:T(8,128)(2,1...) custom-call(bf16[128,2048]{1,0:T(8,128)(2,1)} %fusion.9.x, ...), custom_call_target="tpu_custom_call" | custom-call | tf_op jit(solution)/shard_map/pallas_call | solution.py:215
  539.3 0.0 copy-start.12
  539.3 0.0 copy-start.13
  539.3 3.1 convert_reduce_fusion.1
  542.5 0.1 constant_dynamic-slice_fusion
  542.5 0.5 bitcast_divide_fusion
  543.1 0.8 convert_element_type.100
  543.9 1.2 convert_multiply_fusion.4
  545.3 1.0 pad_maximum_fusion
  546.4 0.8 copy-done.3
  547.2 0.4 convert_reduce_fusion
  547.6 0.3 fusion.3
  547.9 0.5 copy-done.2
  548.4 1.8 fusion.6
  550.2 1.5 convert_element_type.103
  551.7 0.1 copy-done.6
  551.8 0.7 copy-done.7
  552.5 2.5 convert_multiply_fusion
  (31 shorter events, 0.3 us)
Async XLA Ops:
  0.6 6.0 %copy-start.9 = (bf16[64,4096]{1,0:T(8,128)(2,1)S(1)}, bf16[64,4096]{1,0:T(8,128)(2,1)}, u32[]{:S(2)}) copy-start(bf16[64,4096]{1,0:T(8,128)(2,1)} %param.14) | copy-start | bytes 1572868
  6.7 1.2 copy-start
  6.8 2.0 copy-start.4
  6.8 2.0 copy-start.5
  313.2 1.0 copy-start.1
  539.3 3.1 copy-start.11
  539.3 3.2 copy-start.12
  539.3 3.2 copy-start.13
  539.3 3.7 copy-start.10
  545.2 2.0 copy-start.3
  547.2 1.2 copy-start.2
  548.4 1.8 copy-start.8
  550.2 1.6 copy-start.6
  550.2 2.3 copy-start.7

commit v2 on v1

v2 whole, which is shorter than its diff:
```python
import functools
import math

import jax
import jax.numpy as jnp
from jax import lax
from jax.experimental import pallas as pl
from jax.experimental.pallas import tpu as pltpu
from jax.sharding import PartitionSpec as P

HEADS = 16
KV_HEADS = 8
HEAD_DIM = 128
BLOCK = 256
MOST_BLOCKS = 2
GROUP = HEADS // KV_HEADS
EPS = 1e-05
THETA = 1000000.0
MESH = pl.DeviceIdType.MESH
F32 = jnp.float32
BF16 = jnp.bfloat16

PLANE = 8
DEPTH = 4
FLIPS = [(1, 0), (0, 1), (1, 1)]


def dot(a, b, dims=((1,), (0,))):
    return lax.dot_general(a, b, (dims, ((), ())), preferred_element_type=F32)


NT = ((1,), (1,))
TN = ((0,), (0,))


def flip(bit, by):
    return lax.rem(bit + by, 2)


class Place:
    def __init__(self):
        rep, self.f = lax.axis_index("rep"), lax.axis_index("fsdp")
        self.r = lax.rem(rep, PLANE)
        self.base = rep - self.r
        self.z, self.x = lax.div(self.r, 2), lax.rem(self.r, 2)
        self.y, self.c = lax.div(self.f, 2), lax.rem(self.f, 2)
        self.p = self.x * 4 + self.f
        self.q = self.z * 2 + self.c
        self.d = self.r * 4 + self.f

    def at(self, z, x, y, c):
        return (self.base + z * 2 + x, y * 2 + c)

    def plane(self, dx, dy, dc):
        x, y, c = flip(self.x, dx), flip(self.y, dy), flip(self.c, dc)
        return self.at(self.z, x, y, c), x * 4 + y * 2 + c

    def column(self, dz, dc):
        z, c = lax.rem(self.z + dz, DEPTH), flip(self.c, dc)
        return self.at(z, self.x, self.y, c), z, c

    def behind(self, dz):
        return lax.rem(self.z + (DEPTH - dz), DEPTH)


class Net:
    def __init__(self, send, recv, local):
        self.send, self.recv, self.local_sem = send, recv, local
        self.used = 0
        self.sent, self.kept = [], []

    def take(self, count):
        self.used += count
        return self.used - count

    def copy(self, src, dst, send, recv, device):
        return pltpu.make_async_remote_copy(
            src_ref=src,
            dst_ref=dst,
            send_sem=self.send.at[send],
            recv_sem=self.recv.at[recv],
            device_id=device,
            device_id_type=MESH,
        )

    def put(self, src, dst, device):
        k = self.take(1)
        copy = self.copy(src, dst, k, k, device)
        copy.start()
        self.sent.append((None, copy))
        return copy

    def put_if(self, when, copy):
        pl.when(when)(copy.start)
        self.sent.append((when, copy))
        return copy

    def keep(self, src, dst):
        copy = pltpu.make_async_copy(src, dst, self.local_sem.at[len(self.kept)])
        copy.start()
        self.kept.append(copy)
        return copy

    def finish(self):
        for when, copy in self.sent:
            if when is None:
                copy.wait_send()
            else:
                pl.when(when)(copy.wait_send)


class Chain:
    def __init__(self, me, net, slot, twins=None):
        self.me, self.net, self.slot, self.twins = me, net, slot, twins
        self.base = net.take(12)
        last = DEPTH - 1
        self.first, self.last = me.z == 0, me.z == last
        self.inner = jnp.logical_and(me.z > 0, me.z < last)
        self.order = [
            me.z,
            1 + lax.rem(me.z, 2),
            jnp.where(self.inner, last * (me.z - 1), 2 - lax.div(me.z, last)),
            last * (1 - lax.div(me.z, 2)),
        ]
        self.steps = [None] + [self.arrival(i) for i in range(1, DEPTH)]

    def pass_on(self, i):
        self.steps[i][0]()

    def take_in(self, i):
        self.steps[i][1]()

    def link(self, z, k, target):
        me = self.me
        ref = self.slot(z, me.c)
        return self.net.copy(ref, ref, self.base + k, self.base + z, me.at(target, me.x, me.y, me.c))

    def start(self):
        me, net = self.me, self.net
        net.put_if(jnp.logical_not(self.last), self.link(me.z, 0, me.z + 1))
        net.put_if(jnp.logical_not(self.first), self.link(me.z, 1, me.z - 1))
        if self.twins is not None:
            self.twin(me.z, 0)

    def twin(self, z, k):
        ref, net = self.slot(z, self.me.c), self.net
        copy = net.copy(ref, ref, self.base + 8 + k, self.base + 4 + z, self.twins)
        copy.start()
        net.sent.append((None, copy))

    def arrival(self, i):
        me, net = self.me, self.net
        z = self.order[i]
        onward = self.link(z, 1 + i, me.z + jnp.where(z < me.z, 1, -1))
        across = None
        net.sent.append((self.inner, onward))
        if self.twins is not None:
            ref = self.slot(z, me.c)
            across = net.copy(ref, ref, self.base + 8 + i, self.base + 4 + z, self.twins)
            net.sent.append((None, across))

        def take(passes):
            onward.wait_recv()
            if passes:
                onward.start()
            if across is not None:
                across.start()

        return (
            lambda: pl.when(self.inner)(lambda: take(True)),
            lambda: pl.when(jnp.logical_not(self.inner))(lambda: take(False)),
        )

    def twin_has(self, z):
        ref = self.slot(z, 1 - self.me.c)
        self.net.copy(ref, ref, self.base + 4, self.base + 4 + z, self.twins).wait_recv()

    def twin_all(self):
        for z in range(DEPTH):
            self.twin_has(z)


def greet(devices):
    barrier = pltpu.get_barrier_semaphore()
    for device in devices:
        pl.semaphore_signal(barrier, inc=1, device_id=device, device_id_type=MESH)
    return barrier


def plane_ids(me):
    return [
        me.plane(dx, dy, dc)[0] for dx in (0, 1) for dy in (0, 1) for dc in (0, 1) if dx + dy + dc
    ]


def column_ids(me):
    return [me.column(dz, dc)[0] for dz in range(1, DEPTH) for dc in (0, 1)]


def sems(sends, locals_):
    return [
        pltpu.SemaphoreType.DMA((sends,)),
        pltpu.SemaphoreType.DMA((sends,)),
        pltpu.SemaphoreType.DMA((locals_,)),
    ]


ANY = pl.BlockSpec(memory_space=pl.ANY)


def call(kernel, ident, outs, args, sends, locals_, scratch=()):
    return pl.pallas_call(
        kernel,
        out_shape=outs,
        in_specs=[ANY] * len(args),
        out_specs=[ANY] * len(outs),
        scratch_shapes=list(scratch) + sems(sends, locals_),
        compiler_params=pltpu.CompilerParams(
            collective_id=ident, has_side_effects=True, vmem_limit_bytes=60 * 1024 * 1024
        ),
    )(*args)


def swap_owner(me):
    there = me.at(me.f, lax.div(me.r, 4), lax.div(lax.rem(me.r, 4), 2), lax.rem(me.r, 2))
    back = (me.base + me.p, me.z)
    away = jnp.logical_or(me.r != me.p, me.f != me.z)
    return there, back, away


def turn(v):
    return pltpu.roll(v, HEAD_DIM // 2, 1)


def rotations(table):
    swapped = turn(table)
    low = lax.broadcasted_iota(jnp.int32, table.shape, 1) < HEAD_DIM // 2
    return jnp.where(low, table, swapped), jnp.where(low, -swapped, table)


def attend(R, codes, P, A, seq, length):
    half = length // 2
    keys_at = pl.ds(seq * length, length)
    keys = R[keys_at, GROUP * HEAD_DIM : (GROUP + 1) * HEAD_DIM]
    values = R[keys_at, (GROUP + 1) * HEAD_DIM :]
    code = codes[seq, 0:1, :]
    for part in range(2):
        rows = pl.ds(seq * length + part * half, half)
        most = jnp.transpose(codes[seq, :, part * half : (part + 1) * half])[:, 0:1]
        least = jnp.floor(most * (1.0 / MOST_BLOCKS)) * MOST_BLOCKS
        allowed = (code <= most) & (code >= least)
        for h in range(GROUP):
            cols = slice(h * HEAD_DIM, (h + 1) * HEAD_DIM)
            scores = dot(R[rows, cols], keys, NT) * HEAD_DIM ** (-0.5)
            scores = jnp.where(allowed, scores, -1e30)
            exponent = jnp.exp(scores - jnp.max(scores, axis=-1, keepdims=True))
            weights = (exponent / jnp.sum(exponent, axis=-1, keepdims=True)).astype(BF16)
            P[h, rows, :] = weights
            A[rows, cols] = dot(weights, values).astype(BF16)


def front_kernel(
    x, pos, gain, cot, wq, wo, wg, wu, wd,
    sums, Uo, Ro, Po, Ao, To, Wqo, Woo, cg, Wg, Wu, Wd,
    X, places, gains, code, q_raw, q_own, g_own, u_own, U, T, codes, Wq, Wo, R, P, A, E, swapped, came, send, recv, local,
):
    me = Place()
    net = Net(send, recv, local)
    tokens = x.shape[0]
    there, back, away = swap_owner(me)
    barrier = greet(plane_ids(me) + column_ids(me))

    raw = [net.keep(src, dst) for src, dst in ((pos, places), (gain, gains), (x, X), (wq, q_raw), (wg, g_own), (wu, u_own))]

    @pl.when(away)
    def _():
        pl.semaphore_signal(barrier, inc=1, device_id=there, device_id_type=MESH)
        pl.semaphore_signal(barrier, inc=1, device_id=back, device_id_type=MESH)

    pl.semaphore_wait(barrier, jnp.where(away, 15, 13))
    twin = me.plane(0, 0, 1)[0]
    x_next, y_next = me.plane(1, 0, 0)[0], me.plane(0, 1, 0)[0]

    def slab(p):
        return pl.ds(pl.multiple_of(p * tokens, tokens), tokens)

    own_rows = slab(me.p)
    raw[1].wait()

    def normalize():
        raw[2].wait()

        def body(i, carry):
            at = pl.ds(pl.multiple_of(i * 16, 16), 16)
            v = X[at, :].astype(F32)
            v = v * lax.rsqrt(jnp.mean(v * v, axis=-1, keepdims=True) + EPS)
            U[pl.ds(pl.multiple_of(me.p * tokens + i * 16, 16), 16), :] = v.astype(BF16)
            return carry

        lax.fori_loop(0, tokens // 16, body, 0)

    def rotation_table():
        raw[0].wait()
        half = HEAD_DIM // 2
        place = places[...]
        column = jnp.transpose(place.astype(F32))[:, 0:1]
        index = lax.broadcasted_iota(jnp.int32, (1, half), 1).astype(F32)
        angles = column * jnp.exp(index * (-math.log(THETA) / half))
        T[own_rows, :] = jnp.concatenate([jnp.cos(angles), jnp.sin(angles)], axis=1)
        lane = lax.broadcasted_iota(jnp.int32, place.shape, 1)
        start = me.f * tokens + lane - place
        code[...] = (start * MOST_BLOCKS + lax.div(place, jnp.full_like(place, BLOCK))).astype(F32)

    def scale_q():
        raw[3].wait()
        by = gains[0, :, 0:1]
        lead = GROUP * HEAD_DIM
        for p in range(KV_HEADS):
            parts = (p * lead, lead), (HEADS * HEAD_DIM + p * HEAD_DIM, HEAD_DIM), ((HEADS + KV_HEADS + p) * HEAD_DIM, HEAD_DIM)
            to = 0
            for first, size in parts:
                q_own[p, :, to : to + size] = (q_raw[:, first : first + size].astype(F32) * by).astype(BF16)
                to += size

    def scale_f(k):
        raw[4 + k].wait()
        w = (g_own, u_own)[k]
        by = gains[1, :, 0:1]

        def body(i, carry):
            cols = pl.ds(pl.multiple_of(i * 1024, 1024), 1024)
            w[:, cols] = (w[:, cols].astype(F32) * by).astype(BF16)
            return carry

        lax.fori_loop(0, w.shape[1] // 1024, body, 0)

    weights = {"g": (g_own, Wg), "u": (u_own, Wu), "d": (wd, Wd)}
    taken, sent, last = {}, {}, []

    def column(n):
        if n != "d":
            scale_f("gu".index(n))
        w, W = weights[n]
        got = []
        for dz in (2, 1, 3, 0):
            for dc in (0, 1):
                device, z, c = me.column(dz, dc)
                cols = pl.ds(pl.multiple_of((z * 2 + c) * 1024, 1024), 1024)
                if dz + dc:
                    got.append(net.put(w.at[:, cols], W.at[me.d], device))
                else:
                    own = net.keep(w.at[:, cols], W.at[me.d])
        taken[n] = got, own

    def spread(n):
        W = weights[n][1]
        got, own = taken[n]
        for copy in got:
            copy.wait_recv()
        own.wait()
        for z in range(DEPTH):
            rows = pl.ds(z * 8 + me.p - me.c, 2)
            sent[n, z] = [net.put(W.at[rows], W.at[rows], device) for device in (x_next, y_next)]

    def relay(n, z):
        W = weights[n][1]
        by_x, by_y = sent[n, z]
        if z % 2:
            by_x.wait_recv()
            rows = pl.ds(z * 8 + me.plane(1, 0, 0)[1] - me.c, 2)
            last.extend((net.put(W.at[rows], W.at[rows], y_next), by_y))
        else:
            by_y.wait_recv()
            rows = pl.ds(z * 8 + me.plane(0, 1, 0)[1] - me.c, 2)
            last.extend((net.put(W.at[rows], W.at[rows], x_next), by_x))

    q_in = []

    def q_go():
        scale_q()
        for dx in (0, 1):
            for dy in (0, 1):
                for dc in (0, 1):
                    device, p = me.plane(dx, dy, dc)
                    if dx + dy + dc:
                        q_in.append(net.put(q_own.at[p], Wq.at[me.d], device))
                    else:
                        own = net.keep(q_own.at[p], Wq.at[me.d])
        q_in.append(own)

    q_chain = Chain(me, net, lambda z, c: Wq.at[pl.ds(z * PLANE, PLANE)])
    o_chain = Chain(me, net, lambda z, c: Wo.at[z])
    c_chain = Chain(me, net, lambda z, c: cg.at[z * 2 + c], twin)
    c_own = net.keep(cot, cg.at[me.q])

    def q_start():
        for copy in q_in[:-1]:
            copy.wait_recv()
        q_in[-1].wait()
        q_chain.start()

    k = net.take(1)
    swap = net.copy(wo, Wo.at[me.f], k, k, there)
    stay = pltpu.make_async_copy(wo, Wo.at[me.f], local.at[local.shape[0] - 1])
    stays = jnp.logical_not(away)

    def swap_go():
        pl.when(away)(swap.start)
        pl.when(stays)(stay.start)

    def o_start():
        pl.when(away)(swap.wait)
        pl.when(stays)(stay.wait)
        o_chain.start()

    def c_start():
        c_own.wait()
        c_chain.start()

    t_gather = PlaneGather(me, net, lambda p: T.at[slab(p)])
    x_gather = PlaneGather(me, net, lambda p: U.at[slab(p)])
    code_in = []

    def x_go():
        normalize()
        x_gather.start()

    def t_go():
        rotation_table()
        t_gather.start()

    def code_go():
        lanes = pl.ds(pl.multiple_of(lax.rem(me.p, 4) * tokens, tokens), tokens)
        at = codes.at[lax.div(me.p, 4), :, lanes]
        code_in.extend(net.put(code, at, device) for device in plane_ids(me))
        code_in.append(net.keep(code, at))

    block = 2 * tokens
    lead = GROUP * HEAD_DIM

    def project():
        def body(i, carry):
            rows = pl.ds(pl.multiple_of(i * block, block), block)
            q = dot(U[rows, :], Wq[...].reshape(Wq.shape[0] * Wq.shape[1], Wq.shape[2]))
            cosine, sine = rotations(T[rows, :])
            for h in range(GROUP + 1):
                v = q[:, h * HEAD_DIM : (h + 1) * HEAD_DIM]
                R[rows, h * HEAD_DIM : (h + 1) * HEAD_DIM] = (v * cosine + turn(v) * sine).astype(BF16)
            R[rows, lead + HEAD_DIM :] = q[:, lead + HEAD_DIM :].astype(BF16)
            return carry

        lax.fori_loop(0, 8 * tokens // block, body, 0)

    def attention(seq):
        if seq == 0:
            for copy in code_in[:-1]:
                copy.wait_recv()
            code_in[-1].wait()
        attend(R, codes, P, A, seq, 4 * tokens)

    total = PlaneSum(me, net, lambda p: E.at[slab(p)], swapped, came)
    stores = []

    def out_product():
        def body(i, carry):
            rows = pl.ds(pl.multiple_of(i * block, block), block)
            E[rows, :] = dot(A[rows, :], Wo[...].reshape(Wo.shape[0] * Wo.shape[1], Wo.shape[2])).astype(BF16)
            return carry

        lax.fori_loop(0, 8 * tokens // block, body, 0)
        total.start()
        for src, dst in ((U, Uo), (R, Ro), (P, Po), (A, Ao), (T, To), (Wq, Wqo), (Wo, Woo)):
            stores.append(net.keep(src, dst))

    column("d")
    column("u")
    t_go()
    code_go()
    column("g")
    q_go()
    x_go()
    x_gather.relay()
    x_gather.finish()
    spread("d")
    q_start()
    spread("u")
    swap_go()
    spread("g")
    relay("u", 0)
    q_chain.take_in(1)
    q_chain.pass_on(1)
    q_chain.pass_on(2)
    t_gather.relay()
    relay("u", 1)
    o_start()
    relay("u", 2)
    q_chain.pass_on(3)
    o_chain.pass_on(1)
    o_chain.pass_on(2)
    relay("g", 0)
    relay("g", 1)
    o_chain.pass_on(3)
    c_start()
    relay("g", 2)
    t_gather.finish()
    relay("d", 0)
    q_chain.take_in(2)
    relay("d", 1)
    o_chain.take_in(1)
    relay("d", 2)
    relay("g", 3)
    relay("u", 3)
    q_chain.take_in(3)
    project()
    attention(0)
    c_chain.pass_on(1)
    attention(1)
    c_chain.pass_on(2)
    o_chain.take_in(2)
    relay("d", 3)
    o_chain.take_in(3)
    out_product()
    total.cores()
    c_chain.take_in(1)
    c_chain.pass_on(3)
    total.chips()
    c_chain.take_in(2)
    c_chain.take_in(3)
    stores.append(total.finish(sums))
    for copy in last:
        copy.wait_recv()
    c_chain.twin_all()
    for copy in stores:
        copy.wait()
    net.finish()


def add_to(into, more):
    step = 16
    rows = into.shape[-2]
    steps = rows // step

    def body(k, carry):
        if len(into.shape) == 2:
            at = (pl.ds(pl.multiple_of(k * step, step), step),)
        else:
            at = (lax.div(k, steps), pl.ds(pl.multiple_of(lax.rem(k, steps) * step, step), step))
        into[at] = (into[at].astype(F32) + more[at].astype(F32)).astype(BF16)
        return carry

    lax.fori_loop(0, steps * (1 if len(into.shape) == 2 else into.shape[0]), body, 0)


class PlaneGather:
    def __init__(self, me, net, slab):
        self.me, self.net, self.slab = me, net, slab
        self.twin = me.plane(0, 0, 1)[0]
        self.x_next, self.px = me.plane(1, 0, 0)
        self.y_next, self.py = me.plane(0, 1, 0)
        self.pd = me.plane(1, 1, 0)[1]

    def start(self):
        net, own = self.net, self.slab(self.me.p)
        self.by_x = net.put(own, own, self.x_next)
        self.by_y = net.put(own, own, self.y_next)
        self.late = [net.put(own, own, self.twin)]

    def half(self, p, k):
        ref = self.slab(p)
        rows = ref.shape[0] // 2
        return ref.at[pl.ds(k * rows, rows)]

    def across(self, p):
        ref = self.slab(p)
        self.late.append(self.net.put(ref, ref, self.twin))

    def relay(self):
        net = self.net
        self.by_x.wait_recv()
        ref = self.half(self.px, 0)
        self.first = net.put(ref, ref, self.y_next)
        self.by_y.wait_recv()
        ref = self.half(self.py, 1)
        self.second = net.put(ref, ref, self.x_next)
        self.across(self.px)
        self.across(self.py)

    def finish(self):
        self.first.wait_recv()
        self.second.wait_recv()
        self.across(self.pd)
        for copy in self.late:
            copy.wait_recv()


class PlaneSum:
    def __init__(self, me, net, slab, swapped, came):
        self.me, self.net, self.slab, self.swapped, self.came = me, net, slab, swapped, came
        self.x_next, self.y_next = me.plane(1, 0, 0)[0], me.plane(0, 1, 0)[0]
        self.places = [me.plane(dx, dy, 0)[1] for dx, dy in FLIPS + [(0, 0)]]

    def start(self):
        me = self.me
        self.swaps = []
        for k, (dx, dy) in enumerate(FLIPS + [(0, 0)]):
            other = me.plane(dx, dy, 1)[1]
            self.swaps.append(
                self.net.put(self.slab(other), self.swapped.at[k], me.plane(0, 0, 1)[0])
            )

    def half(self, k, h):
        ref = self.slab(self.places[k])
        rows = ref.shape[0] // 2
        return ref.at[pl.ds(h * rows, rows)]

    def cores(self):
        for k in range(4):
            self.swaps[k].wait_recv()
            add_to(self.slab(self.places[k]), self.swapped.at[k])
            if k == 2:
                net, came = self.net, self.came
                self.first = [
                    net.put(self.half(2, 0), came.at[1], self.x_next),
                    net.put(self.half(2, 1), came.at[3], self.y_next),
                    net.put(self.half(0, 0), came.at[0], self.x_next),
                    net.put(self.half(1, 1), came.at[2], self.y_next),
                ]

    def chips(self):
        net, came = self.net, self.came
        for copy in self.first:
            copy.wait_recv()
        add_to(self.half(1, 0), came.at[1])
        second = [net.put(self.half(1, 0), came.at[4], self.y_next)]
        add_to(self.half(0, 1), came.at[3])
        second.append(net.put(self.half(0, 1), came.at[5], self.x_next))
        add_to(self.half(3, 0), came.at[0])
        add_to(self.half(3, 1), came.at[2])
        self.second = second

    def finish(self, out):
        for h in (0, 1):
            self.second[h].wait_recv()
            add_to(self.half(3, h), self.came.at[4 + h])
        return self.net.keep(self.slab(self.places[3]), out)


class ChainSum:
    def __init__(self, me, net, slots, up, down, add=add_to):
        self.me, self.net, self.slots, self.up, self.down, self.add = me, net, slots, up, down, add
        self.base = net.take(8)

    def copy(self, z, upward, target):
        me = self.me
        landing = self.up.at[z - 1] if upward else self.down.at[z]
        k = self.base + z + (0 if upward else 4)
        return self.net.copy(self.slots.at[z], landing, k, k, me.at(target, me.x, me.y, me.c))

    def step(self, at, z, upward):
        copy = self.copy(z, upward, at + 1 if upward else at - 1)
        here = self.me.z == at

        def go():
            if at != (0 if upward else DEPTH - 1):
                copy.wait_recv()
                self.add(self.slots.at[z], self.up.at[z - 1] if upward else self.down.at[z])
            copy.start()

        pl.when(here)(go)
        self.net.sent.append((here, copy))

    def begin(self, hops):
        self.step(0, hops, True)
        self.step(DEPTH - 1, DEPTH - 1 - hops, False)

    def near(self, hops):
        self.step(1, 1 + hops, True)
        self.step(2, 2 - hops, False)

    def far(self):
        self.step(2, 3, True)
        self.step(1, 0, False)

    def finish(self):
        me = self.me

        @pl.when(me.z > 0)
        def _():
            self.copy(me.z, True, me.z).wait_recv()
            self.add(self.slots.at[me.z], self.up.at[me.z - 1])

        @pl.when(me.z < DEPTH - 1)
        def _():
            self.copy(me.z, False, me.z).wait_recv()
            self.add(self.slots.at[me.z], self.down.at[me.z])


class ColumnSum:
    def __init__(self, me, net, slots, came):
        self.me, self.net, self.slots, self.came = me, net, slots, came

    def start(self):
        me = self.me
        self.sent = []
        for k, dz in enumerate((2, 1, 3)):
            device, z, _ = me.column(dz, 0)
            self.sent.append(self.net.put(self.slots.at[z], self.came.at[k], device))

    def finish(self):
        for k, copy in enumerate(self.sent):
            copy.wait_recv()
            add_to(self.slots.at[self.me.z], self.came.at[k])


def ffn_kernel(
    x, branch, cot, wg, wu, wd, e_out, o_out, gg, gu, gd, gain, X, N, C, Wg, Wu, Wd, H, DG, DU, O, E, R, G, S, n_send, n_recv, x_send, x_recv, e_send, e_recv, local,
):
    me = Place()
    tokens = x.shape[0]
    chip = 2 * tokens
    twin = me.plane(0, 0, 1)[0]
    ids = [me.column(dz, 0)[0] for dz in range(1, DEPTH)] + [twin]
    barrier = greet(ids)
    loads = [
        pltpu.make_async_copy(src, dst, local.at[i])
        for i, (src, dst) in enumerate(((wg, Wg), (wu, Wu), (wd, Wd), (cot, C)))
    ]
    own_rows = pl.ds(pl.multiple_of(me.q * tokens, tokens), tokens)
    mine = [pltpu.make_async_copy(src, X.at[i], local.at[(4, 11)[i]]) for i, src in enumerate((x, branch))]
    for load in mine:
        load.start()

    def rows_of(z, c):
        return pl.ds(pl.multiple_of((z * 2 + c) * tokens, tokens), tokens)

    def remote(src, dst, send, recv, device):
        return pltpu.make_async_remote_copy(
            src_ref=src,
            dst_ref=dst,
            send_sem=send,
            recv_sem=recv,
            device_id=device,
            device_id_type=MESH,
        )

    def column_id(z):
        return me.at(z, me.x, me.y, me.c)

    odd = lax.rem(me.z, 2)
    order = [me.z, 1 + odd, lax.rem(me.z + 2, DEPTH), 3 * (1 - odd)]
    net = Net(n_send, n_recv, local)
    chain = Chain(me, net, lambda z, c: N.at[rows_of(z, c)], twin)

    def twin_has(i):
        chain.twin_has(order[i])

    tile = 512

    def rows_at(i):
        return pl.ds(pl.multiple_of(order[i] * chip, chip), chip)

    def hidden(i):
        twin_has(i)
        rows = rows_at(i)

        def body(t, carry):
            cols = pl.ds(pl.multiple_of(t * tile, tile), tile)
            gate = dot(N[rows, :], Wg[:, cols])
            raised = dot(N[rows, :], Wu[:, cols])
            d_hidden = dot(C[rows, :], Wd[:, cols])
            sig = jax.nn.sigmoid(gate)
            act = gate * sig
            H[rows, cols] = (act * raised).astype(BF16)
            DU[rows, cols] = (d_hidden * act).astype(BF16)
            DG[rows, cols] = (d_hidden * raised * sig * (1.0 + gate * (1.0 - sig))).astype(BF16)
            return carry

        lax.fori_loop(0, H.shape[1] // tile, body, 0)

    def products(i):
        rows = rows_at(i)

        def body(t, carry):
            cols = pl.ds(pl.multiple_of(t * tile, tile), tile)
            e = dot(DG[rows, :], Wg[cols, :], NT) + dot(DU[rows, :], Wu[cols, :], NT)
            E[rows, cols] = e.astype(BF16)
            piece = jnp.sum((e * N[rows, cols].astype(F32)).reshape(chip // 8, 8, tile), axis=0)
            if i == 0:
                S[:, cols] = piece
            else:
                S[:, cols] += piece
            O[rows, cols] = dot(H[rows, :], Wd[cols, :], NT).astype(BF16)
            return carry

        lax.fori_loop(0, E.shape[1] // tile, body, 0)
        swap(i)

    swaps, sums = [], []

    def swap(i):
        o = order[i]
        copy = remote(E.at[rows_of(o, 1 - me.c)], R.at[i], x_send.at[i], x_recv.at[i], twin)
        copy.start()
        swaps.append(copy)

    def total(i):
        o = order[i]
        swaps[i].wait_recv()
        first = (o * 2 + me.c) * tokens

        def body(k, carry):
            at = pl.ds(pl.multiple_of(k * 16, 16), 16)
            to = pl.ds(pl.multiple_of(first + k * 16, 16), 16)
            E[to, :] = (E[to, :].astype(F32) + R[i, at, :].astype(F32)).astype(BF16)
            return carry

        lax.fori_loop(0, tokens // 16, body, 0)
        rows = rows_of(o, me.c)
        if i == 0:
            copy = pltpu.make_async_copy(E.at[rows], e_out.at[me.z], local.at[5])
        else:
            copy = remote(E.at[rows], e_out.at[me.z], e_send.at[i], e_recv.at[me.z], column_id(o))
        copy.start()
        sums.append(copy)

    for load in mine:
        load.wait()

    def normalize(i, carry):
        at = pl.ds(pl.multiple_of(i * 16, 16), 16)
        v = X[0, at, :].astype(F32) + X[1, at, :].astype(F32)
        v = v * lax.rsqrt(jnp.mean(v * v, axis=-1, keepdims=True) + EPS)
        N[pl.ds(pl.multiple_of(me.q * tokens + i * 16, 16), 16), :] = v.astype(BF16)
        return carry

    lax.fori_loop(0, tokens // 16, normalize, 0)
    for load in loads:
        load.start()
    pl.semaphore_wait(barrier, 4)
    chain.start()
    for load in loads:
        load.wait()
    chain.take_in(1)
    hidden(0)
    products(0)
    chain.pass_on(1)
    chain.pass_on(2)
    hidden(1)
    chain.take_in(2)
    products(1)
    total(0)
    chain.pass_on(3)
    total(1)
    hidden(2)
    chain.take_in(3)
    products(2)
    total(2)
    hidden(3)
    products(3)
    total(3)
    stores = [
        pltpu.make_async_copy(O, o_out, local.at[6]),
        pltpu.make_async_copy(S, gain, local.at[7]),
    ]
    for store in stores:
        store.start()

    span = 256

    def grad_tile(t, carry):
        rows = pl.ds(pl.multiple_of(t * span, span), span)
        n, c = N[:, rows], C[:, rows]
        G[0, rows, :] = dot(n, DG[...], TN).astype(BF16)
        G[1, rows, :] = dot(n, DU[...], TN).astype(BF16)
        G[2, rows, :] = dot(c, H[...], TN).astype(BF16)
        return carry

    lax.fori_loop(0, G.shape[1] // span, grad_tile, 0)
    for i, dst in enumerate((gg, gu, gd)):
        store = pltpu.make_async_copy(G.at[i], dst, local.at[8 + i])
        store.start()
        stores.append(store)
    for i in range(1, DEPTH):
        o = order[i]
        remote(E.at[own_rows], e_out.at[o], e_send.at[i], e_recv.at[o], twin).wait_recv()
    sums[0].wait()
    for copy in sums[1:] + swaps:
        copy.wait_send()
    net.finish()
    for store in stores:
        store.wait()


def back_kernel(
    x, branch, cot, e_parts, part_o, gg, gu, gd, gain_f, u, r, pw, att, t, wq, wo,
    d_mid, out_o, out_e, og, ou, od, oq, oo, ov,
    DM, D, U, R, P, A, T, Wq, Wo, dA, dR, E, GQ, GO, gains, out, out_swap, out_came, e_swap, e_came,
    own, side, came, q_up, q_down, o_up, o_down, v_up, v_down, send, recv, local,
):
    me = Place()
    net = Net(send, recv, local)
    tokens = x.shape[0]
    raw = [net.keep(src, E.at[pl.ds(k * tokens, tokens)]) for k, src in enumerate((x, branch, cot))]
    raw += [net.keep(e_parts.at[k], E.at[pl.ds((3 + k) * tokens, tokens)]) for k in range(DEPTH)]
    back, there, away = swap_owner(me)
    barrier = greet(plane_ids(me) + column_ids(me))

    @pl.when(away)
    def _():
        pl.semaphore_signal(barrier, inc=1, device_id=there, device_id_type=MESH)
        pl.semaphore_signal(barrier, inc=1, device_id=back, device_id_type=MESH)

    pl.semaphore_wait(barrier, jnp.where(away, 15, 13))
    twin = me.plane(0, 0, 1)[0]
    x_next, px = me.plane(1, 0, 0)
    y_next, py = me.plane(0, 1, 0)
    pd = me.plane(1, 1, 0)[1]

    def slab(p):
        return pl.ds(pl.multiple_of(p * tokens, tokens), tokens)

    def quarter(grad, p, z):
        return grad.at[pl.ds(z * 8 + p - me.c, 2)]

    grads = {"d": (0, gd, od), "g": (1, gg, og), "u": (2, gu, ou)}
    begun, passed, late, kept = {}, {}, [], []
    hand_send = hand_recv = net.take(24)

    def first(n):
        g, grad, _ = grads[n]
        for z in range(DEPTH):
            half = z // 2
            device, near, far = (y_next, py, px) if half else (x_next, px, py)
            at = pl.ds(z % 2 * 2, 2)
            begun[n, z] = [
                net.put(quarter(grad, near, z), came.at[g * 6 + half * 3, at], device),
                net.put(quarter(grad, pd, z), came.at[g * 6 + half * 3 + 1, at], device),
            ], [
                net.keep(quarter(grad, me.p, z), own.at[g * 2 + half, at]),
                net.keep(quarter(grad, far, z), side.at[g * 2 + half, at]),
            ]

    def second(n, half):
        g = grads[n][0]
        for z in (half * 2, half * 2 + 1):
            got, mine = begun[n, z]
            for copy in got:
                copy.wait_recv()
            for copy in mine:
                copy.wait()
        add_to(side.at[g * 2 + half], came.at[g * 6 + half * 3 + 1])
        device = x_next if half else y_next
        passed[n, half] = net.put(side.at[g * 2 + half], came.at[g * 6 + half * 3 + 2], device)
        add_to(own.at[g * 2 + half], came.at[g * 6 + half * 3])

    def third(n, half):
        g, _, result = grads[n]
        cols = pl.ds(pl.multiple_of(me.q * 1024, 1024), 1024)
        passed[n, half].wait_recv()
        add_to(own.at[g * 2 + half], came.at[g * 6 + half * 3 + 2])
        for z in (half * 2, half * 2 + 1):
            for c in (0, 1):
                src, dst = own.at[g * 2 + half, z % 2 * 2 + c], result.at[:, cols]
                mine = jnp.logical_and(me.z == z, me.c == c)
                k = hand_send + g * 8 + z * 2 + c
                copy = net.copy(src, dst, k, hand_recv + g * 8 + me.q, me.at(z, me.x, me.y, c))
                net.put_if(jnp.logical_not(mine), copy)
                here = pltpu.make_async_copy(src, dst, local.at[local.shape[0] - 2 - g])
                pl.when(mine)(here.start)
                late.append((mine, here))

    for copy in raw:
        copy.wait()

    def normed_back(i, carry):
        def part(k):
            return E[pl.ds(pl.multiple_of(k * tokens + i * 16, 16), 16), :].astype(F32)

        v = part(0) + part(1)
        inverse = lax.rsqrt(jnp.mean(v * v, axis=-1, keepdims=True) + EPS)
        unit = v * inverse
        e = part(3) + part(4) + part(5) + part(6)
        d = part(2) + inverse * (e - unit * jnp.mean(e * unit, axis=-1, keepdims=True))
        DM[pl.ds(pl.multiple_of(i * 16, 16), 16), :] = d
        D[pl.ds(pl.multiple_of(me.p * tokens + i * 16, 16), 16), :] = d.astype(BF16)
        return carry

    lax.fori_loop(0, tokens // 16, normed_back, 0)
    kept.append(net.keep(DM, d_mid))
    d_gather = PlaneGather(me, net, lambda p: D.at[slab(p)])
    loads = {}
    for name, src, dst in (
        ("att", att, A), ("wo", wo, Wo), ("r", r, R), ("pw", pw, P), ("t", t, T), ("u", u, U), ("wq", wq, Wq),
    ):
        loads[name] = [net.keep(src, dst)]
    loads["gain"] = [
        net.keep(gain_f.at[:, pl.ds(z * 512, 512)], gains.at[z, 1]) for z in range(DEPTH)
    ]

    def need(*names):
        for name in names:
            for copy in loads.pop(name, ()):
                copy.wait()

    out_in = []

    def out_swaps():
        for z in range(DEPTH):
            other, mine = slab(z * 2 + 1 - me.c), slab(z * 2 + me.c)
            out_in.append((net.put(part_o.at[other], out_swap.at[z], twin), net.keep(part_o.at[mine], out.at[z])))

    def out_add():
        for z in range(DEPTH):
            got, mine = out_in[z]
            got.wait_recv()
            mine.wait()
            add_to(out.at[z], out_swap.at[z])

    out_sum = ColumnSum(me, net, out, out_came)

    def out_finish():
        out_sum.finish()
        kept.append(net.keep(out.at[me.z], out_o))

    block = 2 * tokens
    length = 4 * tokens
    lead = GROUP * HEAD_DIM
    scale = HEAD_DIM ** (-0.5)

    def d_attended():
        need("wo")

        def body(i, carry):
            rows = pl.ds(pl.multiple_of(i * block, block), block)
            dA[rows, :] = dot(D[rows, :], Wo[...].reshape(Wo.shape[0] * Wo.shape[1], Wo.shape[2]), NT).astype(BF16)
            return carry

        lax.fori_loop(0, 8 * tokens // block, body, 0)

    def turn_back(v, rows):
        cosine, sine = rotations(T[rows, :])
        return (v * cosine - turn(v) * sine).astype(BF16)

    def attend_back(seq):
        need("r", "pw", "t")
        keys_at = pl.ds(seq * length, length)
        keys = R[keys_at, lead : lead + HEAD_DIM]
        values = R[keys_at, lead + HEAD_DIM :]
        d_keys = jnp.zeros((length, HEAD_DIM), F32)
        d_values = jnp.zeros((length, HEAD_DIM), F32)
        for h in range(GROUP):
            cols = slice(h * HEAD_DIM, (h + 1) * HEAD_DIM)
            for part in range(2):
                rows = pl.ds(seq * length + part * (length // 2), length // 2)
                low = P[h, rows, :]
                weights = low.astype(F32)
                d_out = dA[rows, cols]
                d_weights = dot(d_out, values, NT)
                d_scores = (
                    weights * (d_weights - jnp.sum(weights * d_weights, axis=-1, keepdims=True))
                ).astype(BF16)
                dR[rows, cols] = turn_back(dot(d_scores, keys) * scale, rows)
                d_keys += dot(d_scores, R[rows, cols], TN)
                d_values += dot(low, d_out, TN)
        dR[keys_at, lead : lead + HEAD_DIM] = turn_back(d_keys * scale, keys_at)
        dR[keys_at, lead + HEAD_DIM :] = d_values.astype(BF16)

    tile = 512

    def e_product():
        need("u", "wq", "gain")

        def body(k, carry):
            i, j = lax.div(k, E.shape[1] // tile), lax.rem(k, E.shape[1] // tile)
            rows = pl.ds(pl.multiple_of(i * block, block), block)
            cols = pl.ds(pl.multiple_of(j * tile, tile), tile)
            slots = pl.ds(j * (tile // Wq.shape[1]), tile // Wq.shape[1])
            e = dot(dR[rows, :], Wq[slots].reshape(tile, Wq.shape[2]), NT)
            E[rows, cols] = e.astype(BF16)
            piece = jnp.sum((e * U[rows, cols].astype(F32)).reshape(block // 8, 8, tile), axis=0)
            gains[j, 0] = jnp.where(i == 0, 0.0, gains[j, 0]) + piece
            return carry

        lax.fori_loop(0, 8 * tokens // block * (E.shape[1] // tile), body, 0)

    e_sum = PlaneSum(me, net, lambda p: E.at[slab(p)], e_swap, e_came)
    span = 256

    def q_product():
        need("u")

        def body(k, carry):
            cols = pl.ds(pl.multiple_of(k * span, span), span)
            per = span // GQ.shape[2]
            g = dot(U[:, cols], dR[...], TN).astype(BF16)
            at = pl.ds(lax.rem(k, PLANE // per) * per, per)
            GQ[lax.div(k, PLANE // per), at] = g.reshape(per, GQ.shape[2], GQ.shape[3])
            return carry

        lax.fori_loop(0, U.shape[1] // span, body, 0)

    def o_product():
        need("att")

        def body(k, carry):
            cols = pl.ds(pl.multiple_of(k * tile, tile), tile)
            g = dot(A[...], D[:, cols], TN).astype(BF16)
            GO[:, 0, :, cols] = g.reshape(GO.shape[0], GO.shape[2], tile)
            return carry

        lax.fori_loop(0, D.shape[1] // tile, body, 0)

    def add_all(into, more):
        into[...] = into[...] + more[...]

    q_sum = ChainSum(me, net, GQ, q_up, q_down)
    o_sum = ChainSum(me, net, GO, o_up, o_down)
    v_sum = ChainSum(me, net, gains, v_up, v_down, add_all)

    def q_begin(hops):
        q_sum.begin(hops)
        v_sum.begin(hops)

    def q_near(hops):
        q_sum.near(hops)
        v_sum.near(hops)

    def q_far():
        q_sum.far()
        v_sum.far()

    def q_finish():
        q_sum.finish()
        v_sum.finish()

    k = net.take(1)
    swap = net.copy(GO.at[me.z, 0], oo, k, k, there)
    stay = pltpu.make_async_copy(GO.at[me.z, 0], oo, local.at[local.shape[0] - 1])
    stays = jnp.logical_not(away)
    owned = []

    def to_owners():
        pl.when(away)(swap.start)
        pl.when(stays)(stay.start)
        for dx in (0, 1):
            for dy in (0, 1):
                for dc in (0, 1):
                    device, p = me.plane(dx, dy, dc)
                    lanes = pl.ds(pl.multiple_of(lax.div(p, 2) * 128, 128), 128)
                    for src, dst in ((GQ.at[me.z, p], oq.at[me.p]), (gains.at[me.z, :, :, lanes], ov.at[me.p])):
                        if dx + dy + dc:
                            owned.append(net.put(src, dst, device))
                        else:
                            kept.append(net.keep(src, dst))

    def e_finish():
        kept.append(e_sum.finish(out_e))

    out_swaps()
    d_gather.start()
    out_add()
    out_sum.start()
    first("g")
    d_gather.relay()
    second("g", 0)
    d_gather.finish()
    second("g", 1)
    o_product()
    o_sum.begin(3)
    first("d")
    o_sum.near(2)
    third("g", 0)
    d_attended()
    o_sum.begin(2)
    attend_back(0)
    third("g", 1)
    o_sum.far()
    attend_back(1)
    o_sum.near(1)
    q_product()
    first("u")
    e_product()
    q_begin(3)
    second("d", 1)
    e_sum.start()
    q_near(2)
    second("d", 0)
    q_begin(2)
    out_finish()
    e_sum.cores()
    q_near(1)
    q_begin(1)
    q_far()
    third("d", 1)
    third("d", 0)
    o_sum.begin(1)
    second("u", 0)
    second("u", 1)
    q_finish()
    third("u", 1)
    third("u", 0)
    o_sum.finish()
    e_sum.chips()
    e_finish()
    to_owners()
    for n in "dgu":
        g, _, result = grads[n]
        for dz in range(DEPTH):
            for dc in (0, 1):
                if dz + dc:
                    _, z, c = me.column(dz, dc)
                    cols = pl.ds(pl.multiple_of((z * 2 + c) * 1024, 1024), 1024)
                    k = hand_recv + g * 8 + z * 2 + c
                    net.copy(own.at[g * 2, 0], result.at[:, cols], k, k, twin).wait_recv()
    for copy in owned:
        copy.wait_recv()
    for copy in kept:
        copy.wait()
    for mine, here in late:
        pl.when(mine)(here.wait)
    net.finish()
    pl.when(away)(swap.wait)
    pl.when(stays)(stay.wait)


def final_kernel(
    og, ou, od, oq, oo, o_sum, e_sum, d_mid, x, branch, gain,
    layer, input_grad, g_gate, g_up, g_down, g_qkv, g_out,
    v_og, v_ou, v_od, v_oq, v_oo, v_o, v_e, v_d, v_x, v_b, v_gain, f_gate, f_up, f_down, f_qkv, f_out, f_layer, f_input, sem,
):
    pairs = (
        (gain, v_gain), (og, v_og), (ou, v_ou), (od, v_od), (oq, v_oq), (oo, v_oo),
        (x, v_x), (branch, v_b), (o_sum, v_o), (e_sum, v_e), (d_mid, v_d),
    )
    loads = [pltpu.make_async_copy(src, dst, sem.at[i]) for i, (src, dst) in enumerate(pairs)]
    for load in loads:
        load.start()
    loads[0].wait()
    stores = []

    def store(src, dst):
        copy = pltpu.make_async_copy(src, dst, sem.at[len(pairs) + len(stores)])
        copy.start()
        stores.append(copy)

    def columns(src, dst, by):
        def body(i, carry):
            cols = pl.ds(pl.multiple_of(i * 1024, 1024), 1024)
            v = src[:, cols].astype(F32)
            dst[:, cols] = v if by is None else v * by
            return carry

        lax.fori_loop(0, src.shape[1] // 1024, body, 0)

    for i, (src, dst, out, by) in enumerate(
        ((v_og, f_gate, g_gate, gain), (v_ou, f_up, g_up, gain), (v_od, f_down, g_down, None))
    ):
        loads[1 + i].wait()
        columns(src, dst, None if by is None else v_gain[1, :, 0:1])
        store(dst, out)
    loads[4].wait()
    by = v_gain[0, :, 0:1]
    lead = GROUP * HEAD_DIM
    for p in range(KV_HEADS):
        parts = (p * lead, lead), (HEADS * HEAD_DIM + p * HEAD_DIM, HEAD_DIM), ((HEADS + KV_HEADS + p) * HEAD_DIM, HEAD_DIM)
        at = 0
        for first, size in parts:
            f_qkv[:, first : first + size] = v_oq[p, :, at : at + size].astype(F32) * by
            at += size
    store(f_qkv, g_qkv)
    loads[5].wait()
    columns(v_oo, f_out, None)
    store(f_out, g_out)
    for load in loads[6:]:
        load.wait()

    def tokens_back(i, carry):
        at = pl.ds(pl.multiple_of(i * 16, 16), 16)
        v = v_x[at, :].astype(F32)
        f_layer[at, :] = (v + v_b[at, :].astype(F32) + v_o[at, :].astype(F32)).astype(BF16)
        inverse = lax.rsqrt(jnp.mean(v * v, axis=-1, keepdims=True) + EPS)
        unit = v * inverse
        e = v_e[at, :].astype(F32)
        f_input[at, :] = v_d[at, :] + inverse * (e - unit * jnp.mean(e * unit, axis=-1, keepdims=True))
        return carry

    lax.fori_loop(0, f_layer.shape[0] // 16, tokens_back, 0)
    store(f_layer, layer)
    store(f_input, input_grad)
    for copy in stores:
        copy.wait()


def shape(*dims, dtype=BF16):
    return jax.ShapeDtypeStruct(dims, dtype)


def shards(copies, block_input, positions, cotangent, norm_attn, w_qkv, w_out, norm_ffn, w_gate, w_up, w_down):
    tokens, width = block_input.shape
    ff = w_gate.shape[1]
    q_cols, kv_cols = HEADS * HEAD_DIM, KV_HEADS * HEAD_DIM
    spread = ("rep", "fsdp")
    place = lax.rem(lax.axis_index("rep"), PLANE) * 4 + lax.axis_index("fsdp")

    def take(w):
        if copies == 1:
            return w
        rows = w.shape[0] * copies
        whole = lax.all_gather(w, spread, axis=0, tiled=True)
        return lax.dynamic_slice_in_dim(whole, place * rows, rows, axis=0)

    def give(grad):
        if copies == 1:
            return grad
        rows = grad.shape[0]
        whole = jnp.zeros((rows * 32,) + grad.shape[1:], grad.dtype)
        whole = lax.dynamic_update_slice_in_dim(whole, grad, place * rows, axis=0)
        return lax.psum_scatter(whole, spread, scatter_dimension=0, tiled=True)

    gain_a = take(norm_attn).astype(F32)
    gain_f = take(norm_ffn).astype(F32)
    rows = gain_a.shape[0]
    gains = jnp.broadcast_to(jnp.stack([gain_a, gain_f])[:, :, None], (2, rows, 128))
    own_qkv, own_gate, own_up = take(w_qkv), take(w_gate), take(w_up)
    own_down = take(w_down)
    own_out = take(w_out)
    head_cols = (GROUP + 2) * HEAD_DIM
    ff_cols = ff // 8
    full = 8 * tokens
    places = jnp.broadcast_to(positions[None, :], (8, tokens))
    sums, U, R, Pw, A, T, Wq, Wo, cg, Wg, Wu, Wd = call(
        front_kernel,
        0,
        [
            shape(tokens, width),
            shape(full, width),
            shape(full, head_cols),
            shape(GROUP, full, full // 2),
            shape(full, GROUP * HEAD_DIM),
            shape(full, HEAD_DIM, dtype=F32),
            shape(32, rows, head_cols),
            shape(4, rows, width),
            shape(8, tokens, width),
            shape(32, rows, ff_cols),
            shape(32, rows, ff_cols),
            shape(32, rows, ff_cols),
        ],
        (
            block_input,
            places,
            gains,
            cotangent,
            own_qkv,
            own_out,
            own_gate,
            own_up,
            own_down,
        ),
        150,
        36,
        [
            pltpu.VMEM((tokens, width), BF16),
            pltpu.VMEM((8, tokens), jnp.int32),
            pltpu.VMEM((2, rows, 128), F32),
            pltpu.VMEM((8, tokens), F32),
            pltpu.VMEM((rows, q_cols + 2 * kv_cols), BF16),
            pltpu.VMEM((8, rows, head_cols), BF16),
            pltpu.VMEM((rows, ff), BF16),
            pltpu.VMEM((rows, ff), BF16),
            pltpu.VMEM((full, width), BF16),
            pltpu.VMEM((full, HEAD_DIM), F32),
            pltpu.VMEM((2, 8, full // 2), F32),
            pltpu.VMEM((32, rows, head_cols), BF16),
            pltpu.VMEM((4, rows, width), BF16),
            pltpu.VMEM((full, head_cols), BF16),
            pltpu.VMEM((GROUP, full, full // 2), BF16),
            pltpu.VMEM((full, GROUP * HEAD_DIM), BF16),
            pltpu.VMEM((full, width), BF16),
            pltpu.VMEM((4, tokens, width), BF16),
            pltpu.VMEM((6, tokens // 2, width), BF16),
        ],
    )
    cg = cg.reshape(full, width)
    Wg, Wu, Wd = [w.reshape(width, ff_cols) for w in (Wg, Wu, Wd)]

    e_sums, out_part, g_gate, g_up, g_down, gain_f_part = pl.pallas_call(
        ffn_kernel,
        out_shape=[
            shape(4, tokens, width),
            shape(full, width),
            shape(width, ff_cols),
            shape(width, ff_cols),
            shape(width, ff_cols),
            shape(8, width, dtype=F32),
        ],
        in_specs=[ANY] * 6,
        out_specs=[ANY] * 6,
        scratch_shapes=[pltpu.VMEM((2, tokens, width), BF16)]
        + [pltpu.VMEM((full, width), BF16)] * 2
        + [pltpu.VMEM((width, ff_cols), BF16)] * 3
        + [pltpu.VMEM((full, ff_cols), BF16)] * 3
        + [pltpu.VMEM((full, width), BF16)] * 2
        + [
            pltpu.VMEM((4, tokens, width), BF16),
            pltpu.VMEM((3, width, ff_cols), BF16),
            pltpu.VMEM((8, width), F32),
        ]
        + [pltpu.SemaphoreType.DMA((12,))] * 6
        + [pltpu.SemaphoreType.DMA((12,))],
        compiler_params=pltpu.CompilerParams(
            collective_id=2, has_side_effects=True, vmem_limit_bytes=60 * 1024 * 1024
        ),
    )(block_input, sums, cg, Wg, Wu, Wd)
    g_gate, g_up, g_down = [g.reshape(32, rows, ff_cols) for g in (g_gate, g_up, g_down)]
    d_mid, out_sums, ea_sums, og, ou, od, oq, oo, ov = call(
        back_kernel,
        3,
        [shape(tokens, width, dtype=F32)]
        + [shape(tokens, width)] * 2
        + [shape(rows, ff)] * 3
        + [
            shape(8, rows, head_cols),
            shape(rows, width),
            shape(8, 2, 8, 128, dtype=F32),
        ],
        (block_input, sums, cotangent, e_sums, out_part, g_gate, g_up, g_down, gain_f_part, U, R, Pw, A, T, Wq, Wo),
        140,
        90,
        [
            pltpu.VMEM((tokens, width), F32),
            pltpu.VMEM((full, width), BF16),
            pltpu.VMEM((full, width), BF16),
            pltpu.VMEM((full, head_cols), BF16),
            pltpu.VMEM((GROUP, full, full // 2), BF16),
            pltpu.VMEM((full, GROUP * HEAD_DIM), BF16),
            pltpu.VMEM((full, HEAD_DIM), F32),
            pltpu.VMEM((32, rows, head_cols), BF16),
            pltpu.VMEM((4, rows, width), BF16),
            pltpu.VMEM((full, GROUP * HEAD_DIM), BF16),
            pltpu.VMEM((full, head_cols), BF16),
            pltpu.VMEM((full, width), BF16),
            pltpu.VMEM((4, PLANE, rows, head_cols), BF16),
            pltpu.VMEM((4, 1, rows, width), BF16),
            pltpu.VMEM((4, 2, 8, width // 4), F32),
            pltpu.VMEM((4, tokens, width), BF16),
            pltpu.VMEM((4, tokens, width), BF16),
            pltpu.VMEM((3, tokens, width), BF16),
            pltpu.VMEM((4, tokens, width), BF16),
            pltpu.VMEM((6, tokens // 2, width), BF16),
            pltpu.VMEM((6, 4, rows, ff_cols), BF16),
            pltpu.VMEM((6, 4, rows, ff_cols), BF16),
            pltpu.VMEM((18, 4, rows, ff_cols), BF16),
        ]
        + [pltpu.VMEM((3, PLANE, rows, head_cols), BF16)] * 2
        + [pltpu.VMEM((3, 1, rows, width), BF16)] * 2
        + [pltpu.VMEM((3, 2, 8, width // 4), F32)] * 2,
    )
    layer_output, input_gradient, g_gate, g_up, g_down, g_qkv, g_out = pl.pallas_call(
        final_kernel,
        out_shape=[
            shape(tokens, width),
            shape(tokens, width, dtype=F32),
            shape(rows, ff, dtype=F32),
            shape(rows, ff, dtype=F32),
            shape(rows, ff, dtype=F32),
            shape(rows, q_cols + 2 * kv_cols, dtype=F32),
            shape(rows, width, dtype=F32),
        ],
        in_specs=[ANY] * 11,
        out_specs=[ANY] * 7,
        scratch_shapes=[pltpu.VMEM((rows, ff), BF16)] * 3
        + [pltpu.VMEM((8, rows, head_cols), BF16), pltpu.VMEM((rows, width), BF16)]
        + [pltpu.VMEM((tokens, width), BF16)] * 2
        + [pltpu.VMEM((tokens, width), F32)]
        + [pltpu.VMEM((tokens, width), BF16)] * 2
        + [pltpu.VMEM((2, rows, 128), F32)]
        + [pltpu.VMEM((rows, ff), F32)] * 3
        + [
            pltpu.VMEM((rows, q_cols + 2 * kv_cols), F32),
            pltpu.VMEM((rows, width), F32),
            pltpu.VMEM((tokens, width), BF16),
            pltpu.VMEM((tokens, width), F32),
            pltpu.SemaphoreType.DMA((18,)),
        ],
        compiler_params=pltpu.CompilerParams(vmem_limit_bytes=60 * 1024 * 1024),
    )(og, ou, od, oq, oo, out_sums, ea_sums, d_mid, block_input, sums, gains)
    gain_sums = jnp.sum(ov, axis=(0, 2))
    gain_sums = lax.dynamic_slice_in_dim(gain_sums, place % 2 * rows, rows, axis=1)
    return (
        layer_output,
        input_gradient,
        give(gain_sums[0] / gain_a),
        give(g_qkv),
        give(g_out),
        give(gain_sums[1] / gain_f),
        give(g_gate),
        give(g_up),
        give(g_down),
    )


def solution(mesh):
    copies = mesh.shape["rep"] * mesh.shape["fsdp"] // 32
    rows, flat = P(("rep", "fsdp"), None), P(("rep", "fsdp"))
    return jax.shard_map(
        functools.partial(shards, copies),
        mesh=mesh,
        in_specs=(rows, flat, rows, flat, rows, rows, flat, rows, rows, rows),
        out_specs=(rows, rows, flat, rows, rows, flat, rows, rows, rows),
        check_vma=False,
    )
```

time: 562 us -> 446 us (0.79)
  Pallas kernels: 521 us -> 437 us
  other arithmetic: 29 us -> 1.24 us
    pallas_call x2, Pallas kernels: 423 us -> 353 us  [call(): pl.pallas_call(kernel, out_shape=outs, in_specs=[ANY] * len(args), out_sp...]
    pallas_call x1, Pallas kernels: 98 us -> 77.9 us  [shards(): pl.pallas_call(ffn_kernel, out_shape=[shape(4, tokens, width), shape(full...]
    reduce_sum x8 -> x0, other arithmetic: 9.64 us -> none  [the longest x1 3.08 us: shards(): layer_output = (middle + jnp.sum(out_sums.astype(F32), axis=0)).astype(BF16)]
    convert_element_type x10 -> x0, other arithmetic: 9.37 us -> none  [the longest x1 1.79 us: shards(): own_up = (take(w_up).astype(F32) * gain_f[:, None]).astype(BF16)]
    pallas_call x0 -> x1, Pallas kernels: none -> 6.46 us  [shards(): pl.pallas_call(final_kernel, out_shape=[shape(tokens, width), shape(token...]
where the time goes in v2:
time: 446 us; the launch traced here: 441 us
  Pallas kernels  437 us (98%)
    pallas_call x2, Pallas kernels, call(): pl.pallas_call(kernel, out_shape=outs, in_specs=[ANY] * len(args), out_sp...  353 us
    pallas_call x1, Pallas kernels, shards(): pl.pallas_call(ffn_kernel, out_shape=[shape(4, tokens, width), shape(full...  77.9 us

profile of v2, /device:TPU:11, one launch (start us, length us, event | category | flops | bytes accessed | tf_op | source)
XLA Modules:
  0.0 441.5 jit_solution(4739624685830441187)
XLA Ops:
  0.6 0.7 convert_bitcast_fusion
  1.3 0.7 broadcast_in_dim.5.gain
  2.0 1.2 broadcast_in_dim.4.pos
  3.3 170.6 %shard_map.169 = (bf16[128,2048]{1,0:T(8,128)(2,1)}, bf16[1024,2048]{1,0:T(8,128)(2,1)}, bf16[1024,512]{1,0:T(8,128)(2,1)}, bf16[2,1024,512]{2,1,0:T(8,128)(2,1)...) custom-call(bf16[128,2048]{1,0:T(8,128)(2,1)} %x.7, ...), custom_call_target="tpu_custom_call" | custom-call | tf_op jit(solution)/shard_map/pallas_call | solution.py:212
  173.8 77.9 %shard_map.170 = (bf16[4,128,2048]{2,1,0:T(8,128)(2,1)}, bf16[1024,2048]{1,0:T(8,128)(2,1)}, bf16[2048,1024]{1,0:T(8,128)(2,1)}, bf16[2048,1024]{1,0:T(8,128)(2,...) custom-call(bf16[128,2048]{1,0:T(8,128)(2,1)} %x.7, bf16[128,2048]{1,0:T(8,128)(2,1)} %get-tuple-element.43.branch, ...), custom_call_target="tpu_custom_call" | custom-call | tf_op jit(solution)/shard_map/pallas_call | solution.py:1386
  251.7 182.6 %shard_map.171 = (f32[128,2048]{1,0:T(8,128)}, bf16[128,2048]{1,0:T(8,128)(2,1)}, bf16[128,2048]{1,0:T(8,128)(2,1)}, bf16[64,8192]{1,0:T(8,128)(2,1)}, bf16[64,8...) custom-call(bf16[128,2048]{1,0:T(8,128)(2,1)} %x.7, ...), custom_call_target="tpu_custom_call" | custom-call | tf_op jit(solution)/shard_map/pallas_call | solution.py:212
  434.3 0.0 copy-start
  434.3 0.0 copy-start.1
  434.3 0.0 copy-start.2
  434.4 6.5 %shard_map.172 = (bf16[128,2048]{1,0:T(8,128)(2,1)}, f32[128,2048]{1,0:T(8,128)}, f32[64,8192]{1,0:T(8,128)}, f32[64,8192]{1,0:T(8,128)}, f32[64,8192]{1,0:T(8,1...) custom-call(bf16[64,8192]{1,0:T(8,128)(2,1)} %get-tuple-element.61.og, bf16[64,8192]{1,0:T(8,128)(2,1)} %get-tuple-element.62.ou, ...), custom_call_target="tpu_custom_call" | custom-call | tf_op jit(solution)/shard_map/pallas_call | solution.py:1458
  440.8 0.0 copy-done
  440.9 0.1 constant_dynamic-slice_fusion
  441.0 0.0 copy-done.1
  441.0 0.0 copy-done.2
  441.0 0.5 bitcast_divide_fusion
  (2 shorter events, 0.0 us)
Async XLA Ops:
  434.3 6.5 %copy-start = (f32[8,2,8,128]{3,2,1,0:T(8,128)S(1)}, f32[8,2,8,128]{3,2,1,0:T(8,128)}, u32[]{:S(2)}) copy-start(f32[8,2,8,128]{3,2,1,0:T(8,128)} %get-tuple-element.71) | copy-start | bytes 196612
  434.3 6.6 %copy-start.1 = (bf16[64]{0:T(256)(128)(2,1)S(1)}, bf16[64]{0:T(256)(128)(2,1)}, u32[]{:S(2)}) copy-start(bf16[64]{0:T(256)(128)(2,1)} %param.16) | copy-start | bytes 388
  434.3 6.6 %copy-start.2 = (bf16[64]{0:T(256)(128)(2,1)S(1)}, bf16[64]{0:T(256)(128)(2,1)}, u32[]{:S(2)}) copy-start(bf16[64]{0:T(256)(128)(2,1)} %param.13) | copy-start | bytes 388

commit v3 on v2

--- a/solution.py
+++ b/solution.py
@@ -221,11 +221,25 @@
     )(*args)
 
 
+def head_of(p):
+    return 2 * (p % 4) + p // 4
+
+
+def head_columns(head):
+    lead = GROUP * HEAD_DIM
+    return (
+        (head * lead, lead),
+        (HEADS * HEAD_DIM + head * HEAD_DIM, HEAD_DIM),
+        ((HEADS + KV_HEADS + head) * HEAD_DIM, HEAD_DIM),
+    )
+
+
+def column_of(row):
+    return jnp.transpose(jnp.broadcast_to(row.astype(F32), (8, row.shape[1])))[:, 0:1]
+
+
 def swap_owner(me):
-    there = me.at(me.f, lax.div(me.r, 4), lax.div(lax.rem(me.r, 4), 2), lax.rem(me.r, 2))
-    back = (me.base + me.p, me.z)
-    away = jnp.logical_or(me.r != me.p, me.f != me.z)
-    return there, back, away
+    return me.at(me.f, me.x, lax.div(me.z, 2), lax.rem(me.z, 2)), me.f != me.z
 
 
 def turn(v):
@@ -267,7 +281,7 @@
     me = Place()
     net = Net(send, recv, local)
     tokens = x.shape[0]
-    there, back, away = swap_owner(me)
+    there, away = swap_owner(me)
     barrier = greet(plane_ids(me) + column_ids(me))
 
     raw = [net.keep(src, dst) for src, dst in ((pos, places), (gain, gains), (x, X), (wq, q_raw), (wg, g_own), (wu, u_own))]
@@ -275,9 +289,8 @@
     @pl.when(away)
     def _():
         pl.semaphore_signal(barrier, inc=1, device_id=there, device_id_type=MESH)
-        pl.semaphore_signal(barrier, inc=1, device_id=back, device_id_type=MESH)
-
-    pl.semaphore_wait(barrier, jnp.where(away, 15, 13))
+
+    pl.semaphore_wait(barrier, jnp.where(away, 14, 13))
     twin = me.plane(0, 0, 1)[0]
     x_next, y_next = me.plane(1, 0, 0)[0], me.plane(0, 1, 0)[0]
 
@@ -302,7 +315,7 @@
     def rotation_table():
         raw[0].wait()
         half = HEAD_DIM // 2
-        place = places[...]
+        place = jnp.broadcast_to(places[...], code.shape)
         column = jnp.transpose(place.astype(F32))[:, 0:1]
         index = lax.broadcasted_iota(jnp.int32, (1, half), 1).astype(F32)
         angles = column * jnp.exp(index * (-math.log(THETA) / half))
@@ -313,19 +326,17 @@
 
     def scale_q():
         raw[3].wait()
-        by = gains[0, :, 0:1]
-        lead = GROUP * HEAD_DIM
+        by = column_of(gains[0:1, :])[: q_raw.shape[0]]
         for p in range(KV_HEADS):
-            parts = (p * lead, lead), (HEADS * HEAD_DIM + p * HEAD_DIM, HEAD_DIM), ((HEADS + KV_HEADS + p) * HEAD_DIM, HEAD_DIM)
             to = 0
-            for first, size in parts:
+            for first, size in head_columns(head_of(p)):
                 q_own[p, :, to : to + size] = (q_raw[:, first : first + size].astype(F32) * by).astype(BF16)
                 to += size
 
     def scale_f(k):
         raw[4 + k].wait()
         w = (g_own, u_own)[k]
-        by = gains[1, :, 0:1]
+        by = column_of(gains[1:2, :])[: w.shape[0]]
 
         def body(i, carry):
             cols = pl.ds(pl.multiple_of(i * 1024, 1024), 1024)
@@ -337,41 +348,35 @@
     weights = {"g": (g_own, Wg), "u": (u_own, Wu), "d": (wd, Wd)}
     taken, sent, last = {}, {}, []
 
-    def column(n):
-        if n != "d":
-            scale_f("gu".index(n))
+    def column(n, dz):
         w, W = weights[n]
-        got = []
-        for dz in (2, 1, 3, 0):
-            for dc in (0, 1):
-                device, z, c = me.column(dz, dc)
-                cols = pl.ds(pl.multiple_of((z * 2 + c) * 1024, 1024), 1024)
-                if dz + dc:
-                    got.append(net.put(w.at[:, cols], W.at[me.d], device))
-                else:
-                    own = net.keep(w.at[:, cols], W.at[me.d])
-        taken[n] = got, own
-
-    def spread(n):
+        taken[n, dz] = []
+        for dc in (0, 1):
+            device, z, c = me.column(dz, dc)
+            cols = pl.ds(pl.multiple_of((z * 2 + c) * 1024, 1024), 1024)
+            if dz + dc:
+                taken[n, dz].append(net.put(w.at[:, cols], W.at[me.d], device).wait_recv)
+            else:
+                taken[n, dz].append(net.keep(w.at[:, cols], W.at[me.d]).wait)
+
+    def spread(n, dz):
         W = weights[n][1]
-        got, own = taken[n]
-        for copy in got:
-            copy.wait_recv()
-        own.wait()
-        for z in range(DEPTH):
-            rows = pl.ds(z * 8 + me.p - me.c, 2)
-            sent[n, z] = [net.put(W.at[rows], W.at[rows], device) for device in (x_next, y_next)]
-
-    def relay(n, z):
+        for wait in taken[n, dz]:
+            wait()
+        rows = pl.ds(me.behind(dz) * 8 + me.p - me.c, 2)
+        sent[n, dz] = [net.put(W.at[rows], W.at[rows], device) for device in (x_next, y_next)]
+
+    def relay(n, dz):
         W = weights[n][1]
-        by_x, by_y = sent[n, z]
-        if z % 2:
+        by_x, by_y = sent[n, dz]
+        first = me.behind(dz) * 8 - me.c
+        if dz % 2:
             by_x.wait_recv()
-            rows = pl.ds(z * 8 + me.plane(1, 0, 0)[1] - me.c, 2)
+            rows = pl.ds(first + me.plane(1, 0, 0)[1], 2)
             last.extend((net.put(W.at[rows], W.at[rows], y_next), by_y))
         else:
             by_y.wait_recv()
-            rows = pl.ds(z * 8 + me.plane(0, 1, 0)[1] - me.c, 2)
+            rows = pl.ds(first + me.plane(0, 1, 0)[1], 2)
             last.extend((net.put(W.at[rows], W.at[rows], x_next), by_x))
 
     q_in = []
@@ -421,14 +426,6 @@
     x_gather = PlaneGather(me, net, lambda p: U.at[slab(p)])
     code_in = []
 
-    def x_go():
-        normalize()
-        x_gather.start()
-
-    def t_go():
-        rotation_table()
-        t_gather.start()
-
     def code_go():
         lanes = pl.ds(pl.multiple_of(lax.rem(me.p, 4) * tokens, tokens), tokens)
         at = codes.at[lax.div(me.p, 4), :, lanes]
@@ -468,63 +465,87 @@
             return carry
 
         lax.fori_loop(0, 8 * tokens // block, body, 0)
-        total.start()
         for src, dst in ((U, Uo), (R, Ro), (P, Po), (A, Ao), (T, To), (Wq, Wqo), (Wo, Woo)):
             stores.append(net.keep(src, dst))
 
-    column("d")
-    column("u")
-    t_go()
-    code_go()
-    column("g")
+    column("d", 1)
     q_go()
-    x_go()
-    x_gather.relay()
-    x_gather.finish()
-    spread("d")
+    scale_f(1)
+    column("d", 3)
+    spread("d", 1)
+    scale_f(0)
+    column("u", 1)
+    normalize()
+    rotation_table()
+    x_gather.start()
+    t_gather.start()
     q_start()
-    spread("u")
+    column("d", 0)
+    column("g", 3)
+    column("g", 0)
+    spread("g", 0)
     swap_go()
-    spread("g")
-    relay("u", 0)
+    spread("d", 3)
+    column("u", 0)
+    t_gather.relay_y()
     q_chain.take_in(1)
+    x_gather.relay_x()
+    spread("u", 1)
+    x_gather.relay_y()
     q_chain.pass_on(1)
     q_chain.pass_on(2)
-    t_gather.relay()
+    spread("g", 3)
+    column("g", 2)
+    t_gather.relay_x()
+    spread("d", 0)
+    t_gather.finish()
+    spread("u", 0)
+    q_chain.pass_on(3)
+    column("u", 2)
+    code_go()
+    relay("d", 0)
+    spread("g", 2)
+    relay("d", 3)
+    relay("u", 0)
+    relay("g", 0)
+    q_chain.take_in(2)
+    q_chain.take_in(3)
+    o_start()
+    x_gather.finish()
     relay("u", 1)
-    o_start()
-    relay("u", 2)
-    q_chain.pass_on(3)
+    spread("u", 2)
+    column("g", 1)
+    relay("g", 3)
+    project()
     o_chain.pass_on(1)
     o_chain.pass_on(2)
-    relay("g", 0)
+    spread("g", 1)
+    column("u", 3)
+    attention(0)
+    o_chain.pass_on(3)
+    relay("g", 2)
+    c_start()
+    relay("d", 1)
+    spread("u", 3)
     relay("g", 1)
-    o_chain.pass_on(3)
-    c_start()
-    relay("g", 2)
-    t_gather.finish()
-    relay("d", 0)
-    q_chain.take_in(2)
-    relay("d", 1)
+    attention(1)
     o_chain.take_in(1)
-    relay("d", 2)
-    relay("g", 3)
-    relay("u", 3)
-    q_chain.take_in(3)
-    project()
-    attention(0)
-    c_chain.pass_on(1)
-    attention(1)
-    c_chain.pass_on(2)
     o_chain.take_in(2)
-    relay("d", 3)
+    relay("u", 2)
     o_chain.take_in(3)
     out_product()
+    total.start()
+    c_chain.pass_on(1)
+    c_chain.pass_on(2)
+    column("d", 2)
     total.cores()
+    total.chips()
+    spread("d", 2)
+    c_chain.pass_on(3)
+    relay("u", 3)
     c_chain.take_in(1)
-    c_chain.pass_on(3)
-    total.chips()
     c_chain.take_in(2)
+    relay("d", 2)
     c_chain.take_in(3)
     stores.append(total.finish(sums))
     for copy in last:
@@ -574,15 +595,16 @@
         ref = self.slab(p)
         self.late.append(self.net.put(ref, ref, self.twin))
 
-    def relay(self):
-        net = self.net
+    def relay_x(self):
         self.by_x.wait_recv()
         ref = self.half(self.px, 0)
-        self.first = net.put(ref, ref, self.y_next)
+        self.first = self.net.put(ref, ref, self.y_next)
+        self.across(self.px)
+
+    def relay_y(self):
         self.by_y.wait_recv()
         ref = self.half(self.py, 1)
-        self.second = net.put(ref, ref, self.x_next)
-        self.across(self.px)
+        self.second = self.net.put(ref, ref, self.x_next)
         self.across(self.py)
 
     def finish(self):
@@ -695,23 +717,6 @@
             self.add(self.slots.at[me.z], self.down.at[me.z])
 
 
-class ColumnSum:
-    def __init__(self, me, net, slots, came):
-        self.me, self.net, self.slots, self.came = me, net, slots, came
-
-    def start(self):
-        me = self.me
-        self.sent = []
-        for k, dz in enumerate((2, 1, 3)):
-            device, z, _ = me.column(dz, 0)
-            self.sent.append(self.net.put(self.slots.at[z], self.came.at[k], device))
-
-    def finish(self):
-        for k, copy in enumerate(self.sent):
-            copy.wait_recv()
-            add_to(self.slots.at[self.me.z], self.came.at[k])
-
-
 def ffn_kernel(
     x, branch, cot, wg, wu, wd, e_out, o_out, gg, gu, gd, gain, X, N, C, Wg, Wu, Wd, H, DG, DU, O, E, R, G, S, n_send, n_recv, x_send, x_recv, e_send, e_recv, local,
 ):
@@ -721,13 +726,13 @@
     twin = me.plane(0, 0, 1)[0]
     ids = [me.column(dz, 0)[0] for dz in range(1, DEPTH)] + [twin]
     barrier = greet(ids)
+    own_rows = pl.ds(pl.multiple_of(me.q * tokens, tokens), tokens)
+    mine = [pltpu.make_async_copy(src, X.at[i], local.at[(4, 11)[i]]) for i, src in enumerate((x, branch))]
     loads = [
         pltpu.make_async_copy(src, dst, local.at[i])
         for i, (src, dst) in enumerate(((wg, Wg), (wu, Wu), (wd, Wd), (cot, C)))
     ]
-    own_rows = pl.ds(pl.multiple_of(me.q * tokens, tokens), tokens)
-    mine = [pltpu.make_async_copy(src, X.at[i], local.at[(4, 11)[i]]) for i, src in enumerate((x, branch))]
-    for load in mine:
+    for load in mine + loads:
         load.start()
 
     def rows_of(z, c):
@@ -764,7 +769,7 @@
         rows = rows_at(i)
 
         def body(t, carry):
-            cols = pl.ds(pl.multiple_of(t * tile, tile), tile)
+            cols = pl.ds(t * tile, tile)
             gate = dot(N[rows, :], Wg[:, cols])
             raised = dot(N[rows, :], Wu[:, cols])
             d_hidden = dot(C[rows, :], Wd[:, cols])
@@ -775,13 +780,14 @@
             DG[rows, cols] = (d_hidden * raised * sig * (1.0 + gate * (1.0 - sig))).astype(BF16)
             return carry
 
-        lax.fori_loop(0, H.shape[1] // tile, body, 0)
+        for t in range(H.shape[1] // tile):
+            body(t, 0)
 
     def products(i):
         rows = rows_at(i)
 
         def body(t, carry):
-            cols = pl.ds(pl.multiple_of(t * tile, tile), tile)
+            cols = pl.ds(t * tile, tile)
             e = dot(DG[rows, :], Wg[cols, :], NT) + dot(DU[rows, :], Wu[cols, :], NT)
             E[rows, cols] = e.astype(BF16)
             piece = jnp.sum((e * N[rows, cols].astype(F32)).reshape(chip // 8, 8, tile), axis=0)
@@ -792,16 +798,17 @@
             O[rows, cols] = dot(H[rows, :], Wd[cols, :], NT).astype(BF16)
             return carry
 
-        lax.fori_loop(0, E.shape[1] // tile, body, 0)
+        for t in range(E.shape[1] // tile):
+            body(t, 0)
         swap(i)
 
-    swaps, sums = [], []
+    swaps, sums = {}, {}
 
     def swap(i):
         o = order[i]
         copy = remote(E.at[rows_of(o, 1 - me.c)], R.at[i], x_send.at[i], x_recv.at[i], twin)
         copy.start()
-        swaps.append(copy)
+        swaps[i] = copy
 
     def total(i):
         o = order[i]
@@ -821,7 +828,7 @@
         else:
             copy = remote(E.at[rows], e_out.at[me.z], e_send.at[i], e_recv.at[me.z], column_id(o))
         copy.start()
-        sums.append(copy)
+        sums[i] = copy
 
     for load in mine:
         load.wait()
@@ -834,58 +841,60 @@
         return carry
 
     lax.fori_loop(0, tokens // 16, normalize, 0)
-    for load in loads:
-        load.start()
     pl.semaphore_wait(barrier, 4)
+    span = 256
+    stores = []
+
+    def grad_tile(t):
+        rows = pl.ds(t * span, span)
+        n, c = N[:, rows], C[:, rows]
+        for k, (left, right, out) in enumerate(((c, H, gd), (n, DG, gg), (n, DU, gu))):
+            G[k, rows, :] = dot(left, right[...], TN).astype(BF16)
+            store = pltpu.make_async_copy(G.at[k, rows], out.at[rows], local.at[12 + len(stores)])
+            store.start()
+            stores.append(store)
+
     chain.start()
     for load in loads:
         load.wait()
-    chain.take_in(1)
     hidden(0)
     products(0)
     chain.pass_on(1)
     chain.pass_on(2)
+    chain.take_in(1)
     hidden(1)
+    products(1)
     chain.take_in(2)
-    products(1)
-    total(0)
     chain.pass_on(3)
     total(1)
+    chain.take_in(3)
     hidden(2)
-    chain.take_in(3)
     products(2)
     total(2)
     hidden(3)
     products(3)
     total(3)
-    stores = [
-        pltpu.make_async_copy(O, o_out, local.at[6]),
-        pltpu.make_async_copy(S, gain, local.at[7]),
-    ]
-    for store in stores:
-        store.start()
-
-    span = 256
-
-    def grad_tile(t, carry):
-        rows = pl.ds(pl.multiple_of(t * span, span), span)
-        n, c = N[:, rows], C[:, rows]
-        G[0, rows, :] = dot(n, DG[...], TN).astype(BF16)
-        G[1, rows, :] = dot(n, DU[...], TN).astype(BF16)
-        G[2, rows, :] = dot(c, H[...], TN).astype(BF16)
-        return carry
-
-    lax.fori_loop(0, G.shape[1] // span, grad_tile, 0)
-    for i, dst in enumerate((gg, gu, gd)):
-        store = pltpu.make_async_copy(G.at[i], dst, local.at[8 + i])
+    total(0)
+    grad_tile(0)
+    grad_tile(1)
+    grad_tile(2)
+    grad_tile(3)
+    grad_tile(4)
+    grad_tile(5)
+    grad_tile(6)
+    grad_tile(7)
+    for src, dst, k in ((O, o_out, 6), (S, gain, 7)):
+        store = pltpu.make_async_copy(src, dst, local.at[k])
         store.start()
         stores.append(store)
     for i in range(1, DEPTH):
         o = order[i]
         remote(E.at[own_rows], e_out.at[o], e_send.at[i], e_recv.at[o], twin).wait_recv()
     sums[0].wait()
-    for copy in sums[1:] + swaps:
-        copy.wait_send()
+    for i in range(DEPTH):
+        swaps[i].wait_send()
+        if i:
+            sums[i].wait_send()
     net.finish()
     for store in stores:
         store.wait()
@@ -894,7 +903,7 @@
 def back_kernel(
     x, branch, cot, e_parts, part_o, gg, gu, gd, gain_f, u, r, pw, att, t, wq, wo,
     d_mid, out_o, out_e, og, ou, od, oq, oo, ov,
-    DM, D, U, R, P, A, T, Wq, Wo, dA, dR, E, GQ, GO, gains, out, out_swap, out_came, e_swap, e_came,
+    DM, D, U, R, P, A, T, Wq, Wo, dA, dR, E, GQ, GO, gains, out, out_swap, out_up, out_down, e_swap, e_came,
     own, side, came, q_up, q_down, o_up, o_down, v_up, v_down, send, recv, local,
 ):
     me = Place()
@@ -902,15 +911,14 @@
     tokens = x.shape[0]
     raw = [net.keep(src, E.at[pl.ds(k * tokens, tokens)]) for k, src in enumerate((x, branch, cot))]
     raw += [net.keep(e_parts.at[k], E.at[pl.ds((3 + k) * tokens, tokens)]) for k in range(DEPTH)]
-    back, there, away = swap_owner(me)
+    there, away = swap_owner(me)
     barrier = greet(plane_ids(me) + column_ids(me))
 
     @pl.when(away)
     def _():
         pl.semaphore_signal(barrier, inc=1, device_id=there, device_id_type=MESH)
-        pl.semaphore_signal(barrier, inc=1, device_id=back, device_id_type=MESH)
-
-    pl.semaphore_wait(barrier, jnp.where(away, 15, 13))
+
+    pl.semaphore_wait(barrier, jnp.where(away, 14, 13))
     twin = me.plane(0, 0, 1)[0]
     x_next, px = me.plane(1, 0, 0)
     y_next, py = me.plane(0, 1, 0)
@@ -926,67 +934,63 @@
     begun, passed, late, kept = {}, {}, [], []
     hand_send = hand_recv = net.take(24)
 
-    def first(n):
+    def first(n, z):
         g, grad, _ = grads[n]
-        for z in range(DEPTH):
-            half = z // 2
-            device, near, far = (y_next, py, px) if half else (x_next, px, py)
-            at = pl.ds(z % 2 * 2, 2)
-            begun[n, z] = [
-                net.put(quarter(grad, near, z), came.at[g * 6 + half * 3, at], device),
-                net.put(quarter(grad, pd, z), came.at[g * 6 + half * 3 + 1, at], device),
-            ], [
-                net.keep(quarter(grad, me.p, z), own.at[g * 2 + half, at]),
-                net.keep(quarter(grad, far, z), side.at[g * 2 + half, at]),
-            ]
-
-    def second(n, half):
-        g = grads[n][0]
-        for z in (half * 2, half * 2 + 1):
-            got, mine = begun[n, z]
-            for copy in got:
-                copy.wait_recv()
-            for copy in mine:
-                copy.wait()
-        add_to(side.at[g * 2 + half], came.at[g * 6 + half * 3 + 1])
-        device = x_next if half else y_next
-        passed[n, half] = net.put(side.at[g * 2 + half], came.at[g * 6 + half * 3 + 2], device)
-        add_to(own.at[g * 2 + half], came.at[g * 6 + half * 3])
-
-    def third(n, half):
+        half = z // 2
+        device, near, far = (y_next, py, px) if half else (x_next, px, py)
+        at = pl.ds(z % 2 * 2, 2)
+        begun[n, z] = [
+            net.put(quarter(grad, near, z), came.at[g * 6 + half * 3, at], device).wait_recv,
+            net.put(quarter(grad, pd, z), came.at[g * 6 + half * 3 + 1, at], device).wait_recv,
+            net.keep(quarter(grad, me.p, z), own.at[g * 2 + half, at]).wait,
+            net.keep(quarter(grad, far, z), side.at[g * 2 + half, at]).wait,
+        ]
+
+    def second(n, z):
+        g, half, at = grads[n][0], z // 2, pl.ds(z % 2 * 2, 2)
+        for wait in begun[n, z]:
+            wait()
+        mine = side.at[g * 2 + half, at]
+        add_to(mine, came.at[g * 6 + half * 3 + 1, at])
+        passed[n, z] = net.put(mine, came.at[g * 6 + half * 3 + 2, at], x_next if half else y_next)
+        add_to(own.at[g * 2 + half, at], came.at[g * 6 + half * 3, at])
+
+    def third(n, z):
         g, _, result = grads[n]
+        half, at = z // 2, pl.ds(z % 2 * 2, 2)
         cols = pl.ds(pl.multiple_of(me.q * 1024, 1024), 1024)
-        passed[n, half].wait_recv()
-        add_to(own.at[g * 2 + half], came.at[g * 6 + half * 3 + 2])
-        for z in (half * 2, half * 2 + 1):
-            for c in (0, 1):
-                src, dst = own.at[g * 2 + half, z % 2 * 2 + c], result.at[:, cols]
-                mine = jnp.logical_and(me.z == z, me.c == c)
-                k = hand_send + g * 8 + z * 2 + c
-                copy = net.copy(src, dst, k, hand_recv + g * 8 + me.q, me.at(z, me.x, me.y, c))
-                net.put_if(jnp.logical_not(mine), copy)
-                here = pltpu.make_async_copy(src, dst, local.at[local.shape[0] - 2 - g])
-                pl.when(mine)(here.start)
-                late.append((mine, here))
-
-    for copy in raw:
-        copy.wait()
-
-    def normed_back(i, carry):
-        def part(k):
-            return E[pl.ds(pl.multiple_of(k * tokens + i * 16, 16), 16), :].astype(F32)
-
-        v = part(0) + part(1)
-        inverse = lax.rsqrt(jnp.mean(v * v, axis=-1, keepdims=True) + EPS)
-        unit = v * inverse
-        e = part(3) + part(4) + part(5) + part(6)
-        d = part(2) + inverse * (e - unit * jnp.mean(e * unit, axis=-1, keepdims=True))
-        DM[pl.ds(pl.multiple_of(i * 16, 16), 16), :] = d
-        D[pl.ds(pl.multiple_of(me.p * tokens + i * 16, 16), 16), :] = d.astype(BF16)
-        return carry
-
-    lax.fori_loop(0, tokens // 16, normed_back, 0)
-    kept.append(net.keep(DM, d_mid))
+        passed[n, z].wait_recv()
+        add_to(own.at[g * 2 + half, at], came.at[g * 6 + half * 3 + 2, at])
+        for c in (0, 1):
+            src, dst = own.at[g * 2 + half, z % 2 * 2 + c], result.at[:, cols]
+            mine = jnp.logical_and(me.z == z, me.c == c)
+            k = hand_send + g * 8 + z * 2 + c
+            copy = net.copy(src, dst, k, hand_recv + g * 8 + me.q, me.at(z, me.x, me.y, c))
+            net.put_if(jnp.logical_not(mine), copy)
+            here = pltpu.make_async_copy(src, dst, local.at[local.shape[0] - 2 - g])
+            pl.when(mine)(here.start)
+            late.append((mine, here))
+
+    def norm():
+        for copy in raw:
+            copy.wait()
+
+        def body(i, carry):
+            def part(k):
+                return E[pl.ds(pl.multiple_of(k * tokens + i * 16, 16), 16), :].astype(F32)
+
+            v = part(0) + part(1)
+            inverse = lax.rsqrt(jnp.mean(v * v, axis=-1, keepdims=True) + EPS)
+            unit = v * inverse
+            e = part(3) + part(4) + part(5) + part(6)
+            d = part(2) + inverse * (e - unit * jnp.mean(e * unit, axis=-1, keepdims=True))
+            DM[pl.ds(pl.multiple_of(i * 16, 16), 16), :] = d
+            D[pl.ds(pl.multiple_of(me.p * tokens + i * 16, 16), 16), :] = d.astype(BF16)
+            return carry
+
+        lax.fori_loop(0, tokens // 16, body, 0)
+        kept.append(net.keep(DM, d_mid))
+
     d_gather = PlaneGather(me, net, lambda p: D.at[slab(p)])
     loads = {}
     for name, src, dst in (
@@ -1016,7 +1020,7 @@
             mine.wait()
             add_to(out.at[z], out_swap.at[z])
 
-    out_sum = ColumnSum(me, net, out, out_came)
+    out_sum = ChainSum(me, net, out, out_up, out_down)
 
     def out_finish():
         out_sum.finish()
@@ -1139,9 +1143,11 @@
     stays = jnp.logical_not(away)
     owned = []
 
-    def to_owners():
+    def o_owners():
         pl.when(away)(swap.start)
         pl.when(stays)(stay.start)
+
+    def q_owners():
         for dx in (0, 1):
             for dy in (0, 1):
                 for dc in (0, 1):
@@ -1157,52 +1163,81 @@
         kept.append(e_sum.finish(out_e))
 
     out_swaps()
+    norm()
     d_gather.start()
     out_add()
-    out_sum.start()
-    first("g")
-    d_gather.relay()
-    second("g", 0)
+    out_sum.begin(3)
+    d_gather.relay_y()
+    d_gather.relay_x()
+    first("d", 0)
+    out_sum.near(2)
+    first("d", 3)
+    out_sum.begin(2)
     d_gather.finish()
-    second("g", 1)
     o_product()
+    out_sum.near(1)
+    d_attended()
     o_sum.begin(3)
-    first("d")
-    o_sum.near(2)
-    third("g", 0)
-    d_attended()
     o_sum.begin(2)
     attend_back(0)
+    second("d", 0)
+    first("u", 2)
+    second("d", 3)
+    o_sum.near(2)
+    attend_back(1)
+    o_sum.begin(1)
+    first("g", 1)
+    third("d", 0)
+    q_product()
+    third("d", 3)
+    e_product()
+    first("g", 0)
+    first("d", 1)
+    o_sum.near(1)
+    first("g", 3)
+    out_sum.far()
+    o_sum.far()
+    q_begin(3)
+    q_near(2)
+    second("u", 2)
+    q_begin(2)
+    first("g", 2)
+    first("u", 3)
+    out_sum.begin(1)
+    q_near(1)
+    q_far()
+    second("g", 1)
+    second("g", 3)
+    second("g", 0)
+    first("u", 0)
+    third("u", 2)
+    third("g", 3)
+    second("d", 1)
+    second("g", 2)
     third("g", 1)
-    o_sum.far()
-    attend_back(1)
-    o_sum.near(1)
-    q_product()
-    first("u")
-    e_product()
-    q_begin(3)
-    second("d", 1)
+    first("d", 2)
+    second("u", 3)
+    o_sum.finish()
+    out_finish()
+    o_owners()
+    third("g", 2)
     e_sum.start()
-    q_near(2)
-    second("d", 0)
-    q_begin(2)
-    out_finish()
+    first("u", 1)
+    third("g", 0)
+    second("u", 0)
+    third("d", 1)
+    third("u", 3)
     e_sum.cores()
-    q_near(1)
     q_begin(1)
-    q_far()
-    third("d", 1)
-    third("d", 0)
-    o_sum.begin(1)
-    second("u", 0)
+    second("d", 2)
+    third("u", 0)
     second("u", 1)
+    third("d", 2)
+    e_sum.chips()
+    third("u", 1)
     q_finish()
-    third("u", 1)
-    third("u", 0)
-    o_sum.finish()
-    e_sum.chips()
+    q_owners()
     e_finish()
-    to_owners()
     for n in "dgu":
         g, _, result = grads[n]
         for dz in range(DEPTH):
@@ -1256,15 +1291,13 @@
         ((v_og, f_gate, g_gate, gain), (v_ou, f_up, g_up, gain), (v_od, f_down, g_down, None))
     ):
         loads[1 + i].wait()
-        columns(src, dst, None if by is None else v_gain[1, :, 0:1])
+        columns(src, dst, None if by is None else column_of(v_gain[1:2, :])[: f_gate.shape[0]])
         store(dst, out)
     loads[4].wait()
-    by = v_gain[0, :, 0:1]
-    lead = GROUP * HEAD_DIM
+    by = column_of(v_gain[0:1, :])[: f_qkv.shape[0]]
     for p in range(KV_HEADS):
-        parts = (p * lead, lead), (HEADS * HEAD_DIM + p * HEAD_DIM, HEAD_DIM), ((HEADS + KV_HEADS + p) * HEAD_DIM, HEAD_DIM)
         at = 0
-        for first, size in parts:
+        for first, size in head_columns(head_of(p)):
             f_qkv[:, first : first + size] = v_oq[p, :, at : at + size].astype(F32) * by
             at += size
     store(f_qkv, g_qkv)
@@ -1320,14 +1353,14 @@
     gain_a = take(norm_attn).astype(F32)
     gain_f = take(norm_ffn).astype(F32)
     rows = gain_a.shape[0]
-    gains = jnp.broadcast_to(jnp.stack([gain_a, gain_f])[:, :, None], (2, rows, 128))
+    gains = jnp.pad(jnp.stack([gain_a, gain_f]), ((0, 0), (0, 128 - rows)))
     own_qkv, own_gate, own_up = take(w_qkv), take(w_gate), take(w_up)
     own_down = take(w_down)
     own_out = take(w_out)
     head_cols = (GROUP + 2) * HEAD_DIM
     ff_cols = ff // 8
     full = 8 * tokens
-    places = jnp.broadcast_to(positions[None, :], (8, tokens))
+    places = positions[None, :]
     sums, U, R, Pw, A, T, Wq, Wo, cg, Wg, Wu, Wd = call(
         front_kernel,
         0,
@@ -1360,8 +1393,8 @@
         36,
         [
             pltpu.VMEM((tokens, width), BF16),
-            pltpu.VMEM((8, tokens), jnp.int32),
-            pltpu.VMEM((2, rows, 128), F32),
+            pltpu.VMEM((1, tokens), jnp.int32),
+            pltpu.VMEM((2, 128), F32),
             pltpu.VMEM((8, tokens), F32),
             pltpu.VMEM((rows, q_cols + 2 * kv_cols), BF16),
             pltpu.VMEM((8, rows, head_cols), BF16),
@@ -1406,7 +1439,7 @@
             pltpu.VMEM((8, width), F32),
         ]
         + [pltpu.SemaphoreType.DMA((12,))] * 6
-        + [pltpu.SemaphoreType.DMA((12,))],
+        + [pltpu.SemaphoreType.DMA((12 + 3 * width // 256,))],
         compiler_params=pltpu.CompilerParams(
             collective_id=2, has_side_effects=True, vmem_limit_bytes=60 * 1024 * 1024
         ),
@@ -1445,6 +1478,7 @@
             pltpu.VMEM((4, tokens, width), BF16),
             pltpu.VMEM((4, tokens, width), BF16),
             pltpu.VMEM((3, tokens, width), BF16),
+            pltpu.VMEM((3, tokens, width), BF16),
             pltpu.VMEM((4, tokens, width), BF16),
             pltpu.VMEM((6, tokens // 2, width), BF16),
             pltpu.VMEM((6, 4, rows, ff_cols), BF16),
@@ -1473,7 +1507,7 @@
         + [pltpu.VMEM((tokens, width), BF16)] * 2
         + [pltpu.VMEM((tokens, width), F32)]
         + [pltpu.VMEM((tokens, width), BF16)] * 2
-        + [pltpu.VMEM((2, rows, 128), F32)]
+        + [pltpu.VMEM((2, 128), F32)]
         + [pltpu.VMEM((rows, ff), F32)] * 3
         + [
             pltpu.VMEM((rows, q_cols + 2 * kv_cols), F32),

time: 446 us -> 426 us (0.955)
  Pallas kernels: 437 us -> 417 us
    pallas_call x1, Pallas kernels: 77.9 us -> 67.6 us  [shards(): pl.pallas_call(ffn_kernel, out_shape=[shape(4, tokens, width), shape(full...]
    pallas_call x2, Pallas kernels: 353 us -> 344 us  [call(): pl.pallas_call(kernel, out_shape=outs, in_specs=[ANY] * len(args), out_sp...]
where the time goes in v3:
time: 426 us; the launch traced here: 420 us
  Pallas kernels  417 us (98%)
    pallas_call x2, Pallas kernels, call(): pl.pallas_call(kernel, out_shape=outs, in_specs=[ANY] * len(args), out_sp...  344 us
    pallas_call x1, Pallas kernels, shards(): pl.pallas_call(ffn_kernel, out_shape=[shape(4, tokens, width), shape(full...  67.6 us

profile of v3, /device:TPU:11, one launch (start us, length us, event | category | flops | bytes accessed | tf_op | source)
XLA Modules:
  0.0 420.4 jit_solution(8575954387708900708)
XLA Ops:
  0.6 0.7 convert_bitcast_fusion
  1.3 0.6 select_maximum_fusion.gain
  1.9 166.4 %shard_map.169 = (bf16[128,2048]{1,0:T(8,128)(2,1)}, bf16[1024,2048]{1,0:T(8,128)(2,1)}, bf16[1024,512]{1,0:T(8,128)(2,1)}, bf16[2,1024,512]{2,1,0:T(8,128)(2,1)...) custom-call(bf16[128,2048]{1,0:T(8,128)(2,1)} %x.9, ...), custom_call_target="tpu_custom_call" | custom-call | tf_op jit(solution)/shard_map/pallas_call | solution.py:212
  168.3 67.6 %shard_map.170 = (bf16[4,128,2048]{2,1,0:T(8,128)(2,1)}, bf16[1024,2048]{1,0:T(8,128)(2,1)}, bf16[2048,1024]{1,0:T(8,128)(2,1)}, bf16[2048,1024]{1,0:T(8,128)(2,...) custom-call(bf16[128,2048]{1,0:T(8,128)(2,1)} %x.9, bf16[128,2048]{1,0:T(8,128)(2,1)} %get-tuple-element.43.branch, ...), custom_call_target="tpu_custom_call" | custom-call | tf_op jit(solution)/shard_map/pallas_call | solution.py:1419
  235.9 177.1 %shard_map.171 = (f32[128,2048]{1,0:T(8,128)}, bf16[128,2048]{1,0:T(8,128)(2,1)}, bf16[128,2048]{1,0:T(8,128)(2,1)}, bf16[64,8192]{1,0:T(8,128)(2,1)}, bf16[64,8...) custom-call(bf16[128,2048]{1,0:T(8,128)(2,1)} %x.9, ...), custom_call_target="tpu_custom_call" | custom-call | tf_op jit(solution)/shard_map/pallas_call | solution.py:212
  413.0 0.0 copy-start
  413.0 0.0 copy-start.1
  413.0 0.0 copy-start.2
  413.1 6.2 %shard_map.172 = (bf16[128,2048]{1,0:T(8,128)(2,1)}, f32[128,2048]{1,0:T(8,128)}, f32[64,8192]{1,0:T(8,128)}, f32[64,8192]{1,0:T(8,128)}, f32[64,8192]{1,0:T(8,1...) custom-call(bf16[64,8192]{1,0:T(8,128)(2,1)} %get-tuple-element.61.og, bf16[64,8192]{1,0:T(8,128)(2,1)} %get-tuple-element.62.ou, ...), custom_call_target="tpu_custom_call" | custom-call | tf_op jit(solution)/shard_map/pallas_call | solution.py:1492
  419.3 0.0 copy-done
  419.3 0.1 constant_dynamic-slice_fusion
  419.4 0.0 copy-done.1
  419.4 0.0 copy-done.2
  419.4 0.5 bitcast_divide_fusion
  (1 shorter events, 0.0 us)
Async XLA Ops:
  413.0 6.3 %copy-start = (f32[8,2,8,128]{3,2,1,0:T(8,128)S(1)}, f32[8,2,8,128]{3,2,1,0:T(8,128)}, u32[]{:S(2)}) copy-start(f32[8,2,8,128]{3,2,1,0:T(8,128)} %get-tuple-element.71) | copy-start | bytes 196612
  413.0 6.4 %copy-start.1 = (bf16[64]{0:T(256)(128)(2,1)S(1)}, bf16[64]{0:T(256)(128)(2,1)}, u32[]{:S(2)}) copy-start(bf16[64]{0:T(256)(128)(2,1)} %param.16) | copy-start | bytes 388
  413.0 6.4 %copy-start.2 = (bf16[64]{0:T(256)(128)(2,1)S(1)}, bf16[64]{0:T(256)(128)(2,1)}, u32[]{:S(2)}) copy-start(bf16[64]{0:T(256)(128)(2,1)} %param.13) | copy-start | bytes 388

commit v4 on v3

--- a/solution.py
+++ b/solution.py
@@ -276,7 +276,7 @@
 def front_kernel(
     x, pos, gain, cot, wq, wo, wg, wu, wd,
     sums, Uo, Ro, Po, Ao, To, Wqo, Woo, cg, Wg, Wu, Wd,
-    X, places, gains, code, q_raw, q_own, g_own, u_own, U, T, codes, Wq, Wo, R, P, A, E, swapped, came, send, recv, local,
+    X, places, gains, code, q_raw, q_own, g_own, u_own, d_own, c_own, U, T, codes, Wq, Wo, R, P, A, E, swapped, came, send, recv, local,
 ):
     me = Place()
     net = Net(send, recv, local)
@@ -284,7 +284,7 @@
     there, away = swap_owner(me)
     barrier = greet(plane_ids(me) + column_ids(me))
 
-    raw = [net.keep(src, dst) for src, dst in ((pos, places), (gain, gains), (x, X), (wq, q_raw), (wg, g_own), (wu, u_own))]
+    raw = [net.keep(src, dst) for src, dst in ((pos, places), (gain, gains), (wd, d_own), (x, X), (wq, q_raw), (wg, g_own), (wu, u_own), (cot, c_own))]
 
     @pl.when(away)
     def _():
@@ -299,9 +299,10 @@
 
     own_rows = slab(me.p)
     raw[1].wait()
+    raw[2].wait()
 
     def normalize():
-        raw[2].wait()
+        raw[3].wait()
 
         def body(i, carry):
             at = pl.ds(pl.multiple_of(i * 16, 16), 16)
@@ -325,7 +326,7 @@
         code[...] = (start * MOST_BLOCKS + lax.div(place, jnp.full_like(place, BLOCK))).astype(F32)
 
     def scale_q():
-        raw[3].wait()
+        raw[4].wait()
         by = column_of(gains[0:1, :])[: q_raw.shape[0]]
         for p in range(KV_HEADS):
             to = 0
@@ -334,7 +335,7 @@
                 to += size
 
     def scale_f(k):
-        raw[4 + k].wait()
+        raw[5 + k].wait()
         w = (g_own, u_own)[k]
         by = column_of(gains[1:2, :])[: w.shape[0]]
 
@@ -345,7 +346,7 @@
 
         lax.fori_loop(0, w.shape[1] // 1024, body, 0)
 
-    weights = {"g": (g_own, Wg), "u": (u_own, Wu), "d": (wd, Wd)}
+    weights = {"g": (g_own, Wg), "u": (u_own, Wu), "d": (d_own, Wd)}
     taken, sent, last = {}, {}, []
 
     def column(n, dz):
@@ -396,7 +397,6 @@
     q_chain = Chain(me, net, lambda z, c: Wq.at[pl.ds(z * PLANE, PLANE)])
     o_chain = Chain(me, net, lambda z, c: Wo.at[z])
     c_chain = Chain(me, net, lambda z, c: cg.at[z * 2 + c], twin)
-    c_own = net.keep(cot, cg.at[me.q])
 
     def q_start():
         for copy in q_in[:-1]:
@@ -419,7 +419,8 @@
         o_chain.start()
 
     def c_start():
-        c_own.wait()
+        raw[7].wait()
+        net.keep(c_own, cg.at[me.q]).wait()
         c_chain.start()
 
     t_gather = PlaneGather(me, net, lambda p: T.at[slab(p)])
@@ -471,67 +472,67 @@
     column("d", 1)
     q_go()
     scale_f(1)
-    column("d", 3)
+    column("u", 1)
     spread("d", 1)
+    column("u", 0)
+    q_start()
+    spread("u", 0)
+    rotation_table()
+    t_gather.start()
+    column("u", 3)
+    code_go()
+    normalize()
     scale_f(0)
-    column("u", 1)
-    normalize()
-    rotation_table()
+    column("g", 0)
     x_gather.start()
-    t_gather.start()
-    q_start()
+    swap_go()
+    column("g", 3)
+    t_gather.relay_y()
+    relay("u", 0)
+    column("u", 2)
+    spread("u", 1)
+    x_gather.relay_x()
+    q_chain.take_in(1)
+    x_gather.relay_y()
+    o_start()
     column("d", 0)
-    column("g", 3)
-    column("g", 0)
+    spread("u", 3)
+    t_gather.relay_x()
+    q_chain.pass_on(1)
     spread("g", 0)
-    swap_go()
-    spread("d", 3)
-    column("u", 0)
-    t_gather.relay_y()
-    q_chain.take_in(1)
-    x_gather.relay_x()
-    spread("u", 1)
-    x_gather.relay_y()
-    q_chain.pass_on(1)
     q_chain.pass_on(2)
+    t_gather.finish()
+    spread("u", 2)
     spread("g", 3)
+    o_chain.pass_on(1)
+    relay("u", 3)
+    q_chain.take_in(2)
     column("g", 2)
-    t_gather.relay_x()
     spread("d", 0)
-    t_gather.finish()
-    spread("u", 0)
+    relay("g", 0)
+    relay("d", 1)
+    o_chain.pass_on(2)
+    relay("g", 3)
     q_chain.pass_on(3)
-    column("u", 2)
-    code_go()
+    x_gather.finish()
+    relay("u", 1)
+    column("g", 1)
     relay("d", 0)
     spread("g", 2)
-    relay("d", 3)
-    relay("u", 0)
-    relay("g", 0)
-    q_chain.take_in(2)
     q_chain.take_in(3)
-    o_start()
-    x_gather.finish()
-    relay("u", 1)
-    spread("u", 2)
-    column("g", 1)
-    relay("g", 3)
+    o_chain.take_in(1)
+    column("d", 3)
+    o_chain.pass_on(3)
+    o_chain.take_in(2)
     project()
-    o_chain.pass_on(1)
-    o_chain.pass_on(2)
     spread("g", 1)
-    column("u", 3)
+    c_start()
+    relay("u", 2)
     attention(0)
-    o_chain.pass_on(3)
+    spread("d", 3)
+    attention(1)
+    relay("g", 1)
     relay("g", 2)
-    c_start()
-    relay("d", 1)
-    spread("u", 3)
-    relay("g", 1)
-    attention(1)
-    o_chain.take_in(1)
-    o_chain.take_in(2)
-    relay("u", 2)
     o_chain.take_in(3)
     out_product()
     total.start()
@@ -541,9 +542,9 @@
     total.cores()
     total.chips()
     spread("d", 2)
+    c_chain.take_in(1)
     c_chain.pass_on(3)
-    relay("u", 3)
-    c_chain.take_in(1)
+    relay("d", 3)
     c_chain.take_in(2)
     relay("d", 2)
     c_chain.take_in(3)
@@ -1167,77 +1168,77 @@
     d_gather.start()
     out_add()
     out_sum.begin(3)
+    d_gather.relay_x()
     d_gather.relay_y()
-    d_gather.relay_x()
-    first("d", 0)
     out_sum.near(2)
-    first("d", 3)
+    first("g", 2)
     out_sum.begin(2)
     d_gather.finish()
+    first("d", 0)
+    first("u", 0)
+    first("d", 1)
+    d_attended()
     o_product()
-    out_sum.near(1)
-    d_attended()
     o_sum.begin(3)
     o_sum.begin(2)
+    out_sum.near(1)
+    first("d", 3)
     attend_back(0)
-    second("d", 0)
-    first("u", 2)
-    second("d", 3)
+    out_sum.far()
     o_sum.near(2)
     attend_back(1)
+    o_sum.near(1)
+    first("g", 1)
     o_sum.begin(1)
-    first("g", 1)
-    third("d", 0)
+    first("u", 3)
+    e_product()
+    o_sum.far()
     q_product()
+    q_begin(3)
+    o_sum.finish()
+    o_owners()
+    second("d", 0)
+    q_begin(2)
+    second("d", 3)
+    second("u", 0)
+    second("d", 1)
+    q_near(2)
+    first("d", 2)
+    second("u", 3)
+    third("u", 0)
+    second("g", 1)
+    first("u", 2)
     third("d", 3)
-    e_product()
-    first("g", 0)
-    first("d", 1)
-    o_sum.near(1)
+    second("g", 2)
+    third("d", 1)
+    third("g", 2)
     first("g", 3)
-    out_sum.far()
-    o_sum.far()
-    q_begin(3)
-    q_near(2)
-    second("u", 2)
-    q_begin(2)
-    first("g", 2)
-    first("u", 3)
     out_sum.begin(1)
+    third("u", 3)
+    second("d", 2)
     q_near(1)
     q_far()
-    second("g", 1)
+    q_begin(1)
+    first("g", 0)
+    second("u", 2)
+    e_sum.start()
+    third("d", 0)
+    first("u", 1)
+    third("g", 1)
+    second("g", 0)
     second("g", 3)
-    second("g", 0)
-    first("u", 0)
+    third("d", 2)
+    e_sum.cores()
+    q_finish()
+    third("g", 3)
+    third("g", 0)
+    second("u", 1)
     third("u", 2)
-    third("g", 3)
-    second("d", 1)
-    second("g", 2)
-    third("g", 1)
-    first("d", 2)
-    second("u", 3)
-    o_sum.finish()
     out_finish()
-    o_owners()
-    third("g", 2)
-    e_sum.start()
-    first("u", 1)
-    third("g", 0)
-    second("u", 0)
-    third("d", 1)
-    third("u", 3)
-    e_sum.cores()
-    q_begin(1)
-    second("d", 2)
-    third("u", 0)
-    second("u", 1)
-    third("d", 2)
+    third("u", 1)
     e_sum.chips()
-    third("u", 1)
-    q_finish()
+    e_finish()
     q_owners()
-    e_finish()
     for n in "dgu":
         g, _, result = grads[n]
         for dz in range(DEPTH):
@@ -1400,6 +1401,8 @@
             pltpu.VMEM((8, rows, head_cols), BF16),
             pltpu.VMEM((rows, ff), BF16),
             pltpu.VMEM((rows, ff), BF16),
+            pltpu.VMEM((rows, ff), BF16),
+            pltpu.VMEM((tokens, width), BF16),
             pltpu.VMEM((full, width), BF16),
             pltpu.VMEM((full, HEAD_DIM), F32),
             pltpu.VMEM((2, 8, full // 2), F32),

time: 426 us -> 421 us (0.988)
  Pallas kernels: 417 us -> 412 us
    pallas_call x2, Pallas kernels: 344 us -> 334 us  [call(): pl.pallas_call(kernel, out_shape=outs, in_specs=[ANY] * len(args), out_sp...]
where the time goes in v4:
time: 421 us; the launch traced here: 415 us
  Pallas kernels  412 us (98%)
    pallas_call x2, Pallas kernels, call(): pl.pallas_call(kernel, out_shape=outs, in_specs=[ANY] * len(args), out_sp...  334 us
    pallas_call x1, Pallas kernels, shards(): pl.pallas_call(ffn_kernel, out_shape=[shape(4, tokens, width), shape(full...  71.1 us

profile of v4, /device:TPU:11, one launch (start us, length us, event | category | flops | bytes accessed | tf_op | source)
XLA Modules:
  0.0 414.6 jit_solution(13841798286272661223)
XLA Ops:
  0.6 0.7 convert_bitcast_fusion
  1.3 0.6 select_maximum_fusion.gain
  1.9 160.1 %shard_map.169 = (bf16[128,2048]{1,0:T(8,128)(2,1)}, bf16[1024,2048]{1,0:T(8,128)(2,1)}, bf16[1024,512]{1,0:T(8,128)(2,1)}, bf16[2,1024,512]{2,1,0:T(8,128)(2,1)...) custom-call(bf16[128,2048]{1,0:T(8,128)(2,1)} %x.9, ...), custom_call_target="tpu_custom_call" | custom-call | tf_op jit(solution)/shard_map/pallas_call | solution.py:212
  162.0 71.1 %shard_map.170 = (bf16[4,128,2048]{2,1,0:T(8,128)(2,1)}, bf16[1024,2048]{1,0:T(8,128)(2,1)}, bf16[2048,1024]{1,0:T(8,128)(2,1)}, bf16[2048,1024]{1,0:T(8,128)(2,...) custom-call(bf16[128,2048]{1,0:T(8,128)(2,1)} %x.9, bf16[128,2048]{1,0:T(8,128)(2,1)} %get-tuple-element.43.branch, ...), custom_call_target="tpu_custom_call" | custom-call | tf_op jit(solution)/shard_map/pallas_call | solution.py:1422
  233.2 174.1 %shard_map.171 = (f32[128,2048]{1,0:T(8,128)}, bf16[128,2048]{1,0:T(8,128)(2,1)}, bf16[128,2048]{1,0:T(8,128)(2,1)}, bf16[64,8192]{1,0:T(8,128)(2,1)}, bf16[64,8...) custom-call(bf16[128,2048]{1,0:T(8,128)(2,1)} %x.9, ...), custom_call_target="tpu_custom_call" | custom-call | tf_op jit(solution)/shard_map/pallas_call | solution.py:212
  407.3 0.0 copy-start
  407.3 0.0 copy-start.1
  407.3 0.0 copy-start.2
  407.3 6.2 %shard_map.172 = (bf16[128,2048]{1,0:T(8,128)(2,1)}, f32[128,2048]{1,0:T(8,128)}, f32[64,8192]{1,0:T(8,128)}, f32[64,8192]{1,0:T(8,128)}, f32[64,8192]{1,0:T(8,1...) custom-call(bf16[64,8192]{1,0:T(8,128)(2,1)} %get-tuple-element.61.og, bf16[64,8192]{1,0:T(8,128)(2,1)} %get-tuple-element.62.ou, ...), custom_call_target="tpu_custom_call" | custom-call | tf_op jit(solution)/shard_map/pallas_call | solution.py:1495
  413.5 0.0 copy-done
  413.6 0.1 constant_dynamic-slice_fusion
  413.7 0.0 copy-done.1
  413.7 0.0 copy-done.2
  413.7 0.5 bitcast_divide_fusion
  (1 shorter events, 0.0 us)
Async XLA Ops:
  407.3 6.3 %copy-start = (f32[8,2,8,128]{3,2,1,0:T(8,128)S(1)}, f32[8,2,8,128]{3,2,1,0:T(8,128)}, u32[]{:S(2)}) copy-start(f32[8,2,8,128]{3,2,1,0:T(8,128)} %get-tuple-element.71) | copy-start | bytes 196612
  407.3 6.4 %copy-start.1 = (bf16[64]{0:T(256)(128)(2,1)S(1)}, bf16[64]{0:T(256)(128)(2,1)}, u32[]{:S(2)}) copy-start(bf16[64]{0:T(256)(128)(2,1)} %param.16) | copy-start | bytes 388
  407.3 6.4 %copy-start.2 = (bf16[64]{0:T(256)(128)(2,1)S(1)}, bf16[64]{0:T(256)(128)(2,1)}, u32[]{:S(2)}) copy-start(bf16[64]{0:T(256)(128)(2,1)} %param.13) | copy-start | bytes 388

commit v5 on v4

--- a/solution.py
+++ b/solution.py
@@ -290,7 +290,10 @@
     def _():
         pl.semaphore_signal(barrier, inc=1, device_id=there, device_id_type=MESH)
 
-    pl.semaphore_wait(barrier, jnp.where(away, 14, 13))
+
+    def enter():
+        pl.semaphore_wait(barrier, jnp.where(away, 14, 13))
+
     twin = me.plane(0, 0, 1)[0]
     x_next, y_next = me.plane(1, 0, 0)[0], me.plane(0, 1, 0)[0]
 
@@ -383,7 +386,6 @@
     q_in = []
 
     def q_go():
-        scale_q()
         for dx in (0, 1):
             for dy in (0, 1):
                 for dc in (0, 1):
@@ -469,6 +471,8 @@
         for src, dst in ((U, Uo), (R, Ro), (P, Po), (A, Ao), (T, To), (Wq, Wqo), (Wo, Woo)):
             stores.append(net.keep(src, dst))
 
+    scale_q()
+    enter()
     column("d", 1)
     q_go()
     scale_f(1)
@@ -919,7 +923,10 @@
     def _():
         pl.semaphore_signal(barrier, inc=1, device_id=there, device_id_type=MESH)
 
-    pl.semaphore_wait(barrier, jnp.where(away, 14, 13))
+
+    def enter():
+        pl.semaphore_wait(barrier, jnp.where(away, 14, 13))
+
     twin = me.plane(0, 0, 1)[0]
     x_next, px = me.plane(1, 0, 0)
     y_next, py = me.plane(0, 1, 0)
@@ -1163,9 +1170,10 @@
     def e_finish():
         kept.append(e_sum.finish(out_e))
 
+    norm()
+    enter()
+    d_gather.start()
     out_swaps()
-    norm()
-    d_gather.start()
     out_add()
     out_sum.begin(3)
     d_gather.relay_x()

time: 421 us -> 421 us (level)
  no operation moved by 1% of the time
where the time goes in v5:
time: 421 us; the launch traced here: 415 us
  Pallas kernels  412 us (98%)
    pallas_call x2, Pallas kernels, call(): pl.pallas_call(kernel, out_shape=outs, in_specs=[ANY] * len(args), out_sp...  335 us
    pallas_call x1, Pallas kernels, shards(): pl.pallas_call(ffn_kernel, out_shape=[shape(4, tokens, width), shape(full...  71.1 us

profile of v5, /device:TPU:11, one launch (start us, length us, event | category | flops | bytes accessed | tf_op | source)
XLA Modules:
  0.0 415.4 jit_solution(11825753931567974416)
XLA Ops:
  0.6 0.7 convert_bitcast_fusion
  1.3 0.6 select_maximum_fusion.gain
  1.9 160.1 %shard_map.169 = (bf16[128,2048]{1,0:T(8,128)(2,1)}, bf16[1024,2048]{1,0:T(8,128)(2,1)}, bf16[1024,512]{1,0:T(8,128)(2,1)}, bf16[2,1024,512]{2,1,0:T(8,128)(2,1)...) custom-call(bf16[128,2048]{1,0:T(8,128)(2,1)} %x.9, ...), custom_call_target="tpu_custom_call" | custom-call | tf_op jit(solution)/shard_map/pallas_call | solution.py:212
  162.0 71.1 %shard_map.170 = (bf16[4,128,2048]{2,1,0:T(8,128)(2,1)}, bf16[1024,2048]{1,0:T(8,128)(2,1)}, bf16[2048,1024]{1,0:T(8,128)(2,1)}, bf16[2048,1024]{1,0:T(8,128)(2,...) custom-call(bf16[128,2048]{1,0:T(8,128)(2,1)} %x.9, bf16[128,2048]{1,0:T(8,128)(2,1)} %get-tuple-element.43.branch, ...), custom_call_target="tpu_custom_call" | custom-call | tf_op jit(solution)/shard_map/pallas_call | solution.py:1430
  233.2 174.8 %shard_map.171 = (f32[128,2048]{1,0:T(8,128)}, bf16[128,2048]{1,0:T(8,128)(2,1)}, bf16[128,2048]{1,0:T(8,128)(2,1)}, bf16[64,8192]{1,0:T(8,128)(2,1)}, bf16[64,8...) custom-call(bf16[128,2048]{1,0:T(8,128)(2,1)} %x.9, ...), custom_call_target="tpu_custom_call" | custom-call | tf_op jit(solution)/shard_map/pallas_call | solution.py:212
  408.0 0.0 copy-start
  408.0 0.0 copy-start.1
  408.0 0.0 copy-start.2
  408.0 6.2 %shard_map.172 = (bf16[128,2048]{1,0:T(8,128)(2,1)}, f32[128,2048]{1,0:T(8,128)}, f32[64,8192]{1,0:T(8,128)}, f32[64,8192]{1,0:T(8,128)}, f32[64,8192]{1,0:T(8,1...) custom-call(bf16[64,8192]{1,0:T(8,128)(2,1)} %get-tuple-element.61.og, bf16[64,8192]{1,0:T(8,128)(2,1)} %get-tuple-element.62.ou, ...), custom_call_target="tpu_custom_call" | custom-call | tf_op jit(solution)/shard_map/pallas_call | solution.py:1503
  414.3 0.0 copy-done
  414.3 0.1 constant_dynamic-slice_fusion
  414.4 0.0 copy-done.1
  414.4 0.0 copy-done.2
  414.4 0.5 bitcast_divide_fusion
  (1 shorter events, 0.0 us)
Async XLA Ops:
  408.0 6.3 %copy-start = (f32[8,2,8,128]{3,2,1,0:T(8,128)S(1)}, f32[8,2,8,128]{3,2,1,0:T(8,128)}, u32[]{:S(2)}) copy-start(f32[8,2,8,128]{3,2,1,0:T(8,128)} %get-tuple-element.71) | copy-start | bytes 196612
  408.0 6.4 %copy-start.1 = (bf16[64]{0:T(256)(128)(2,1)S(1)}, bf16[64]{0:T(256)(128)(2,1)}, u32[]{:S(2)}) copy-start(bf16[64]{0:T(256)(128)(2,1)} %param.16) | copy-start | bytes 388
  408.0 6.4 %copy-start.2 = (bf16[64]{0:T(256)(128)(2,1)S(1)}, bf16[64]{0:T(256)(128)(2,1)}, u32[]{:S(2)}) copy-start(bf16[64]{0:T(256)(128)(2,1)} %param.13) | copy-start | bytes 388
